TPU v7x, 32 devices: a whole 2x2x4 slice. The times are simulated.
32 devices in a mesh: gx: 4 (over z), gy: 8 (over y, x, core).
Axes of the slice: x: 2, y: 2, z: 4, core: 2. Of those that a mesh axis runs over, the one named last changes fastest.
Arguments:
- tiles: bfloat16 [6144, 128, 128], P(('gx', 'gy')), may hold values from -6 to 6
- tile_rows: int32 [6144], P(('gx', 'gy')), may hold values from 0 to 63, as said below
- tile_cols: int32 [6144], P(('gx', 'gy')), may hold values from 0 to 255
- tile_counts: int32 [32], P(('gx', 'gy')), may hold values from 48 to 192
- block_order: int32 [256], replicated, may hold values from 0 to 255, each once
- sketch: bfloat16 [32768, 128], replicated, may hold values from -6 to 6
Outputs:
- cell_factor: bfloat16 [262144, 128], P(('gx', 'gy'))
- gene_factor: float32 [32768, 128], P(('gx', 'gy'))
Inputs may be any that keep to these rules, and one draw needn't show every extreme that they name: On each device the live slots (those below its count) hold distinct coordinate pairs (tile_rows, tile_cols) in increasing lexicographic order; later slots are unused. `block_order`: device d along gx+gy owns the gene blocks in entries d * 8 to (d + 1) * 8 - 1.
All inputs are finite; a program needn't handle non-finite values.
Results may differ from a plain program's by a relative error of at most 0.0019.
Values sent between devices are 32-bit elements; how exact they have to be, the bound alone decides.
No kernel may reach another device: no remote copies, remote signals or barrier semaphores. Data moves between devices by JAX's collectives and lax.ppermute only.
A program may use at most 192 MiB of HBM per device.

v0:
```python
import math

import jax
import jax.numpy as jnp
from jax import lax
from jax.sharding import PartitionSpec as P

TILE = 128
SKETCH = 128
GENES = 32768
CB_DEV = 64


def on_device(tiles, tile_rows, tile_cols, tile_counts, block_order, sketch):
    live_count = tile_counts[0]
    blocks_total = GENES // TILE
    sketch_blocks = sketch.reshape(blocks_total, TILE, SKETCH)
    width = 16
    turns = (live_count + width - 1) // width

    def take(start):
        tile_block = lax.dynamic_slice_in_dim(tiles, start, width, 0)
        row_block = lax.dynamic_slice_in_dim(tile_rows, start, width, 0)
        col_block = lax.dynamic_slice_in_dim(tile_cols, start, width, 0)
        alive = start + jnp.arange(width, dtype=jnp.int32) < live_count
        return (tile_block, row_block, col_block, alive)

    def cell_step(turn, total):
        tile_block, row_block, col_block, alive = take(turn * width)
        product = jnp.einsum(
            "tij,tjs->tis", tile_block, sketch_blocks[col_block], preferred_element_type=jnp.float32
        )
        product = jnp.where(alive[:, None, None], product, 0.0)
        return total.at[row_block].add(product)

    cell_sum = lax.fori_loop(0, turns, cell_step, jnp.zeros((CB_DEV, TILE, SKETCH), jnp.float32))
    cell_sum = cell_sum.reshape(CB_DEV * TILE, SKETCH)
    local_gram = jnp.dot(
        cell_sum.T, cell_sum, precision=lax.Precision.HIGHEST, preferred_element_type=jnp.float32
    )
    inner_gram = lax.psum(local_gram, "gy")
    gram = lax.psum(inner_gram, "gx")
    cells_all = CB_DEV * TILE * lax.axis_size("gx") * lax.axis_size("gy")
    lower = jnp.linalg.cholesky(gram)
    cell_factor = (
        math.sqrt(cells_all)
        * lax.linalg.triangular_solve(
            lower, cell_sum, left_side=False, lower=True, transpose_a=True
        )
    ).astype(jnp.bfloat16)
    cell_blocks = cell_factor.reshape(CB_DEV, TILE, SKETCH)

    def gene_step(turn, total):
        tile_block, row_block, col_block, alive = take(turn * width)
        product = jnp.einsum(
            "tji,tjs->tis", tile_block, cell_blocks[row_block], preferred_element_type=jnp.float32
        )
        product = jnp.where(alive[:, None, None], product, 0.0)
        return total.at[col_block].add(product)

    gene_sum = lax.fori_loop(
        0, turns, gene_step, jnp.zeros((blocks_total, TILE, SKETCH), jnp.float32)
    )
    ordered = gene_sum[block_order].reshape(GENES, SKETCH)
    owned = lax.psum_scatter(ordered, ("gx", "gy"), scatter_dimension=0, tiled=True)
    gene_gram = lax.psum(
        jnp.dot(
            owned.T, owned, precision=lax.Precision.HIGHEST, preferred_element_type=jnp.float32
        ),
        ("gx", "gy"),
    )
    lower_genes = jnp.linalg.cholesky(gene_gram)
    gene_factor = math.sqrt(GENES) * lax.linalg.triangular_solve(
        lower_genes, owned, left_side=False, lower=True, transpose_a=True
    )
    return (cell_factor, gene_factor)


def solution(mesh):
    placed = (
        P(("gx", "gy"), None, None),
        P(("gx", "gy")),
        P(("gx", "gy")),
        P(("gx", "gy")),
        P(),
        P(),
    )
    return jax.shard_map(
        on_device,
        mesh=mesh,
        in_specs=placed,
        out_specs=(P(("gx", "gy"), None), P(("gx", "gy"), None)),
        check_vma=False,
    )
```

profile of v0, /device:TPU:0, one launch (start us, length us, event | category | flops | bytes accessed | tf_op | source)
XLA Modules:
  0.0 717.0 jit_solution(9725028844231067474)
XLA Ops:
  7.9 2.4 broadcast_in_dim.44
  10.3 47.1 %while.20 = (s32[]{:T(128)}, f32[64,128,128]{2,1,0:T(8,128)}, s32[]{:T(128)}, s32[192]{0:T(256)S(1)}, s32[]{:T(128)}, /*index=5*/bf16[192,128,128]{2,1,0:T(8,128...) while((s32[]{:T(128)}, f32[64,128,128]{2,1,0:T(8,128)}, ...), condition=%wide.region_2.3_spmd, body=%wide.region_0.2_spmd.sunk | while | flops 67634312 | bytes 6296211 | solution.py:36
  10.4 4.0 gather_fusion
  14.5 0.7 add_compare_fusion.4
  15.1 1.3 convolution_select_fusion.4
  16.5 3.3 scatter_fusion
  19.8 4.0 gather_fusion
  23.9 0.7 add_compare_fusion.4
  24.5 1.3 convolution_select_fusion.4
  25.9 3.3 scatter_fusion
  29.3 4.0 gather_fusion
  33.3 0.7 add_compare_fusion.4
  34.0 1.3 convolution_select_fusion.4
  35.3 3.3 scatter_fusion
  38.7 4.0 gather_fusion
  42.7 0.7 add_compare_fusion.4
  43.4 1.3 convolution_select_fusion.4
  44.7 3.3 scatter_fusion
  48.1 4.0 gather_fusion
  52.1 0.7 add_compare_fusion.4
  52.8 1.3 convolution_select_fusion.4
  54.1 3.3 scatter_fusion
  57.5 10.8 %convolution_bitcast_fusion = f32[128,128]{0,1:T(8,128)} fusion(f32[64,128,128]{2,1,0:T(8,128)} %get-tuple-element.89), kind=kOutput, calls=%fused_computation.22 | convolution fusion | flops 1610612736 | bytes 4259840 | tf_op jit(solution)/shard_map/dot_general | solution.py:38
  68.4 121.4 %all-reduce.4.cloned.1.call-done = f32[128,128]{0,1:T(8,128)} async-done(((f32[128,128]{0,1:T(8,128)}), f32[128,128]{0,1:T(8,128)}) %all-reduce.4.cloned.1.call-update) | async-done | bytes 65552 | tf_op jit(solution)/shard_map/psum | solution.py:41
  190.1 35.6 %all-reduce.6.cloned.1.call-done = f32[128,128]{0,1:T(8,128)} async-done(((f32[128,128]{0,1:T(8,128)}), f32[128,128]{0,1:T(8,128)}) %all-reduce.6.cloned.1.call-update) | async-done | bytes 65552 | tf_op jit(solution)/shard_map/psum | solution.py:42
  225.6 0.9 copy.10
  226.6 0.9 fusion.10
  227.4 11.7 %cholesky.44 = f32[128,128]{1,0:T(8,128)S(1)} custom-call(f32[128,128]{1,0:T(8,128)S(1)} %fusion.10), custom_call_target="Cholesky" | custom-call | tf_op jit(solution)/shard_map/jit(cholesky)/cholesky | solution.py:44
  239.8 0.7 fusion.5
  240.5 9.8 %custom-call.8 = f32[1,128,128]{1,2,0:T(8,128)S(1)} custom-call(f32[1,128,128]{2,1,0:T(8,128)S(1)} %fusion.5), custom_call_target="InvertDiagBlocksLowerTriangular" | custom-call | tf_op jit(solution)/shard_map/triangular_solve | solution.py:47
  250.3 6.2 fusion.4
  256.4 7.8 %broadcast_in_dim.45 = f32[256,128,128]{2,1,0:T(8,128)} broadcast(f32[]{:T(128)} %constant.86.clone.1), dimensions={} | broadcast | bytes 16777220 | tf_op jit(solution)/shard_map/broadcast_in_dim | solution.py:62
  264.3 39.0 %while.21 = (s32[]{:T(128)}, f32[256,128,128]{2,1,0:T(8,128)}, s32[]{:T(128)}, s32[192]{0:T(256)S(1)}, s32[]{:T(128)}, /*index=5*/bf16[192,128,128]{2,1,0:T(8,12...) while((s32[]{:T(128)}, f32[256,128,128]{2,1,0:T(8,128)}, ...), condition=%wide.region_9.11_spmd, body=%wide.region_7.10_spmd.sunk | while | flops 67634312 | bytes 6296211 | solution.py:61
  264.4 2.2 gather_fusion.1
  266.6 0.7 add_compare_fusion.5
  267.3 1.4 convolution_select_fusion.5
  268.7 3.4 scatter_fusion.1
  272.2 2.2 gather_fusion.1
  274.4 0.7 add_compare_fusion.5
  275.1 1.4 convolution_select_fusion.5
  276.5 3.4 scatter_fusion.1
  280.0 2.2 gather_fusion.1
  282.2 0.7 add_compare_fusion.5
  282.9 1.4 convolution_select_fusion.5
  284.3 3.4 scatter_fusion.1
  287.7 2.2 gather_fusion.1
  290.0 0.7 add_compare_fusion.5
  290.6 1.4 convolution_select_fusion.5
  292.1 3.4 scatter_fusion.1
  295.5 2.2 gather_fusion.1
  297.7 0.7 add_compare_fusion.5
  298.4 1.4 convolution_select_fusion.5
  299.8 3.4 scatter_fusion.1
  303.2 17.7 %gather_fusion.2 = f32[256,128,128]{2,1,0:T(8,128)} fusion(f32[256,128,128]{2,1,0:T(8,128)} %get-tuple-element.90, s32[1024]{0:T(1024)S(1)} %pad_clamp_fusion.2), kind=kCustom, calls=%fused_computation.2 | custom fusion | bytes 33555456 | tf_op jit(solution)/shard_map/gather | solution.py:64
  321.0 237.1 %reduce-scatter.2.cloned.1.call-done = f32[1024,128]{1,0:T(8,128)} async-done(((f32[32768,128]{1,0:T(8,128)}), f32[1024,128]{1,0:T(8,128)}) %reduce-scatter.2.cloned.1.call-update) | async-done | bytes 524304 | tf_op jit(solution)/shard_map/reduce_scatter | solution.py:65
  558.1 2.8 fusion.11
  560.9 122.4 %all-reduce.8.cloned.1.call-done = f32[128,128]{0,1:T(8,128)} async-done(((f32[128,128]{0,1:T(8,128)}), f32[128,128]{0,1:T(8,128)}) %all-reduce.8.cloned.1.call-update) | async-done | bytes 65552 | tf_op jit(solution)/shard_map/psum | solution.py:66
  683.4 0.9 copy.13
  684.3 0.9 fusion.8
  685.2 11.7 %cholesky.55 = f32[128,128]{1,0:T(8,128)S(1)} custom-call(f32[128,128]{1,0:T(8,128)S(1)} %fusion.8), custom_call_target="Cholesky" | custom-call | tf_op jit(solution)/shard_map/jit(cholesky)/cholesky | solution.py:72
  696.9 0.6 compare_reduce_fusion
  697.6 0.7 fusion.6
  698.2 9.8 %custom-call.9 = f32[1,128,128]{1,2,0:T(8,128)S(1)} custom-call(f32[1,128,128]{2,1,0:T(8,128)S(1)} %fusion.6), custom_call_target="InvertDiagBlocksLowerTriangular" | custom-call | tf_op jit(solution)/shard_map/triangular_solve | solution.py:73
  708.1 2.4 convolution_multiply_fusion.1
  (39 shorter events, 2.0 us)
Async XLA Ops:
  7.2 3.2 copy-start
  7.2 3.2 copy-start.1
  7.2 182.6 %all-reduce.4.cloned.1.call-start = ((), (), s32[]{:S(2)}) async-start(), calls=%async_computation.1 | async-start | bytes 131072 | tf_op jit(solution)/shard_map/psum | solution.py:41
  57.5 10.9 %copy-start.2 = (s32[256]{0:T(256)S(1)}, s32[256]{0:T(256)}, u32[]{:S(2)}) copy-start(s32[256]{0:T(256)} %param.15) | copy-start | bytes 3076
  68.3 157.3 %all-reduce.6.cloned.1.call-start = ((), (), s32[]{:S(2)}) async-start(), calls=%async_computation.2 | async-start | bytes 131072 | tf_op jit(solution)/shard_map/psum | solution.py:42
  189.8 368.3 %reduce-scatter.2.cloned.1.call-start = ((), (), s32[]{:S(2)}) async-start(), calls=%async_computation.3 | async-start | bytes 17301504 | tf_op jit(solution)/shard_map/reduce_scatter | solution.py:65
  320.9 362.5 %all-reduce.8.cloned.1.call-start = ((), (), s32[]{:S(2)}) async-start(), calls=%async_computation.4 | async-start | bytes 131072 | tf_op jit(solution)/shard_map/psum | solution.py:66
Sparse Core Ops, SparseCore 0:
  68.5 121.2 all-reduce.3
  192.2 33.3 all-reduce.5
  321.0 237.0 reduce-scatter.1
  564.1 119.2 all-reduce.7
where the time goes:
time: 722 us; the launch traced here: 717 us
  waiting for transfers between devices  517 us (72%)
  other arithmetic  88.3 us (12%)
  local copies, waits for them, and re-layouts  61.1 us (8%)
  matrix products  35.9 us (5%)
  between operations  14.5 us (2%)
    reduce_scatter x1, waiting for transfers between devices, on_device(): lax.psum_scatter(ordered, ('gx', 'gy'), scatter_dimension=0, tiled=True)  237 us
    psum x1, waiting for transfers between devices, on_device(): lax.psum(jnp.dot(owned.T, owned, precision=lax.Precision.HIGHEST, preferr...  122 us
    psum x1, waiting for transfers between devices, on_device(): inner_gram = lax.psum(local_gram, 'gy')  121 us
    psum x1, waiting for transfers between devices, on_device(): gram = lax.psum(inner_gram, 'gx')  35.6 us
    gather x5, local copies, waits for them, and re-layouts, cell_step(): sketch_blocks[col_block]  20.1 us
    gather x1, local copies, waits for them, and re-layouts, on_device(): ordered = gene_sum[block_order].reshape(GENES, SKETCH)  17.7 us
    scatter-add x5, other arithmetic, gene_step(): return total.at[col_block].add(product)  17 us
    scatter-add x5, other arithmetic, cell_step(): return total.at[row_block].add(product)  16.5 us
  transfers between devices with their start and end apart: 4, of which 4 were waited for; matrix products, arithmetic and copies ran while one was open for 0% of the time, Pallas kernels for 0%

commit v1 on v0

v1 whole, which is shorter than its diff:
```python
import functools
import math

import jax
import jax.numpy as jnp
from jax import lax
from jax.experimental import pallas as pl
from jax.experimental.pallas import tpu as pltpu
from jax.sharding import PartitionSpec as P

GROUP = 16
QUAD = 4


def bit_orders(nx, ny):
    low = (ny - 1).bit_length()
    bits = list(range(low + (nx - 1).bit_length()))
    swapped = list(bits)
    if low >= 3:
        swapped[1], swapped[2] = swapped[2], swapped[1]
    return bits, swapped


def place_in(order, owner):
    place = 0
    for bit in order:
        place = place * 2 + ((owner >> bit) & 1)
    return place


def sparse_kernel(
    plan, rows, cols, count, order, tiles, sketch, *refs
):
    nx, ny, parts, orders = plan
    pieces = refs[: 2 * parts]
    y_out, gram_out = refs[2 * parts : 2 * parts + 2]
    sketch_v, tiles_v, y_v, split_v, sums_v, slots, sem_s, sem_t, sem_y, sem_p = refs[2 * parts + 2 :]
    slots_all, side = tiles_v.shape[0], tiles_v.shape[1]
    blocks = sketch_v.shape[0]
    devices = nx * ny
    owned = blocks // devices
    per_part = owned // parts
    groups = slots_all // GROUP
    load_s = pltpu.make_async_copy(sketch, sketch_v, sem_s)
    load_s.start()

    def load(g):
        at = pl.ds(g * GROUP, GROUP)
        return pltpu.make_async_copy(tiles.at[at], tiles_v.at[at], sem_t.at[g])

    for g in range(groups):
        load(g).start()
    live = count[0]
    me = lax.axis_index("gx") * ny + lax.axis_index("gy")
    mine = [place_in(o, me) for o in orders]
    for owner in range(devices):
        for part in range(parts):
            kind = part % 2
            place = (place_in(orders[kind], owner) ^ mine[kind]) * per_part + part * devices * per_part
            for j in range(per_part):
                slots[order[owner * owned + part * per_part + j]] = place + j
    y_v[...] = jnp.zeros_like(y_v)

    @pl.loop(0, blocks)
    def _(b):
        sums_v[b] = jnp.zeros(sums_v.shape[1:], jnp.float32)

    load_s.wait()

    @pl.loop(0, groups)
    def _(g):
        load(g).wait()
        turns = jnp.clip((live - g * GROUP + QUAD - 1) // QUAD, 0, GROUP // QUAD)

        @pl.loop(0, turns)
        def _(q):
            start = g * GROUP + q * QUAD
            products = []
            for u in range(QUAD):
                t = start + u
                product = jnp.dot(tiles_v[t], sketch_v[cols[t]], preferred_element_type=jnp.float32)
                products.append(jnp.where(t < live, product, 0.0))
            for u in range(QUAD):
                y_v[rows[start + u]] += products[u]

    save_y = pltpu.make_async_copy(y_v, y_out, sem_y)
    save_y.start()
    gram_out[...] = jnp.zeros_like(gram_out)

    @pl.loop(0, y_v.shape[0] // QUAD)
    def _(b):
        at = pl.ds(b * QUAD, QUAD)
        y = y_v[at]
        high = y.astype(jnp.bfloat16)
        low = (y - high.astype(jnp.float32)).astype(jnp.bfloat16)
        both = jnp.concatenate([high, low], axis=-1)
        split_v[at] = both
        both = both.reshape(QUAD * side, 2 * y.shape[-1])
        g = lax.dot_general(both, both, (((0,), (0,)), ((), ())), preferred_element_type=jnp.float32)
        n = y.shape[-1]
        gram_out[...] += g[:n, :n] + ((g[:n, n:] + g[n:, :n]) + g[n:, n:])

    @pl.loop(0, (live + QUAD - 1) // QUAD)
    def _(q):
        products = []
        for u in range(QUAD):
            t = q * QUAD + u
            product = lax.dot_general(
                tiles_v[t], split_v[rows[t]], (((0,), (0,)), ((), ())), preferred_element_type=jnp.float32
            )
            n = product.shape[-1] // 2
            products.append(jnp.where(t < live, product[:, :n] + product[:, n:], 0.0))
        for u in range(QUAD):
            sums_v[slots[cols[q * QUAD + u]]] += products[u]

    size = devices * per_part // 2
    saves = [
        pltpu.make_async_copy(sums_v.at[pl.ds(k * size, size)], pieces[k], sem_p.at[k]) for k in range(2 * parts)
    ]
    for s in saves:
        s.start()
    for s in saves:
        s.wait()
    save_y.wait()


def on_device(tiles, tile_rows, tile_cols, tile_counts, block_order, sketch, nx, ny):
    slots_all, side, _ = tiles.shape
    genes, wide = sketch.shape
    blocks = genes // side
    cell_blocks = 64
    devices = nx * ny
    owned = blocks // devices
    parts = min(4, owned)
    per_part = owned // parts
    orders = bit_orders(nx, ny)
    size = devices * per_part // 2
    smem = pl.BlockSpec(memory_space=pltpu.SMEM)
    anywhere = pl.BlockSpec(memory_space=pl.ANY)
    outs = pl.pallas_call(
        functools.partial(sparse_kernel, (nx, ny, parts, orders)),
        out_shape=[jax.ShapeDtypeStruct((size, side, wide), jnp.float32)] * (2 * parts)
        + [
            jax.ShapeDtypeStruct((cell_blocks, side, wide), jnp.float32),
            jax.ShapeDtypeStruct((wide, wide), jnp.float32),
        ],
        in_specs=[smem] * 4 + [anywhere] * 2,
        out_specs=[anywhere] * (2 * parts + 1) + [pl.BlockSpec(memory_space=pltpu.VMEM)],
        scratch_shapes=[
            pltpu.VMEM((blocks, side, wide), jnp.bfloat16),
            pltpu.VMEM((slots_all, side, side), jnp.bfloat16),
            pltpu.VMEM((cell_blocks, side, wide), jnp.float32),
            pltpu.VMEM((cell_blocks, side, 2 * wide), jnp.bfloat16),
            pltpu.VMEM((blocks, side, wide), jnp.float32),
            pltpu.SMEM((blocks,), jnp.int32),
            pltpu.SemaphoreType.DMA,
            pltpu.SemaphoreType.DMA((slots_all // GROUP,)),
            pltpu.SemaphoreType.DMA,
            pltpu.SemaphoreType.DMA((2 * parts,)),
        ],
        compiler_params=pltpu.CompilerParams(vmem_limit_bytes=60 * 2**20),
        name="tile_products",
    )(tile_rows, tile_cols, tile_counts, block_order, tiles, sketch.reshape(blocks, side, wide))
    pieces, cell_sum, local_gram = outs[: 2 * parts], outs[-2], outs[-1]

    def swap(value, bit):
        partner = 1 << bit
        if partner < ny:
            return lax.ppermute(value, "gy", [(i, i ^ partner) for i in range(ny)])
        partner //= ny
        return lax.ppermute(value, "gx", [(i, i ^ partner) for i in range(nx)])

    def sum_all(value):
        for bit in orders[0]:
            value = value + swap(value, bit)
        return value

    def total(terms):
        return functools.reduce(jnp.add, terms)

    state = []
    for part in range(parts):
        state.append([pieces[2 * part], swap(pieces[2 * part + 1], orders[part % 2][0])])
    for step in range(1, len(orders[0])):
        for part in range(parts):
            terms = state[part]
            half = terms[0].shape[0] // 2
            arrived = swap(total([t[half:] for t in terms]), orders[part % 2][step])
            state[part] = [total([t[:half] for t in terms]), arrived]
    raw = jnp.concatenate([total(terms) for terms in state], axis=0).reshape(owned * side, wide)

    exact = lax.Precision.HIGHEST
    eye = jnp.eye(wide, dtype=jnp.float32)

    def inverse_of_factor(gram):
        lower = jnp.linalg.cholesky(gram)
        return lax.linalg.triangular_solve(lower, eye, left_side=True, lower=True)

    cells_all = cell_blocks * side * devices
    inverse = math.sqrt(cells_all) * inverse_of_factor(sum_all(local_gram))
    cell_factor = lax.dot_general(
        cell_sum.reshape(cell_blocks * side, wide), inverse, (((1,), (1,)), ((), ())), precision=exact
    ).astype(jnp.bfloat16)
    z = lax.dot_general(raw, inverse, (((1,), (1,)), ((), ())), precision=exact)
    gene_gram = sum_all(lax.dot_general(z, z, (((0,), (0,)), ((), ())), precision=exact))
    inverse_genes = math.sqrt(genes) * inverse_of_factor(gene_gram)
    gene_factor = lax.dot_general(z, inverse_genes, (((1,), (1,)), ((), ())), precision=exact)
    return (cell_factor, gene_factor)


def solution(mesh):
    placed = (
        P(("gx", "gy"), None, None),
        P(("gx", "gy")),
        P(("gx", "gy")),
        P(("gx", "gy")),
        P(),
        P(),
    )
    return jax.shard_map(
        functools.partial(on_device, nx=mesh.shape["gx"], ny=mesh.shape["gy"]),
        mesh=mesh,
        in_specs=placed,
        out_specs=(P(("gx", "gy"), None), P(("gx", "gy"), None)),
        check_vma=False,
    )
```

time: 722 us -> 237 us (0.33)
  waiting for transfers between devices: 517 us -> 94.5 us
  local copies, waits for them, and re-layouts: 61.1 us -> 1.12 us
  starting transfers between devices: 0.34 us -> 51.7 us
  other arithmetic: 88.3 us -> 53.6 us
  matrix products: 35.9 us -> 8.29 us
  Pallas kernels: 0 us -> 25.8 us
  between operations: 14.5 us -> 1.59 us
    psum x3 -> x0, waiting for transfers between devices: 279 us -> none  [the longest x1 122 us: on_device(): lax.psum(jnp.dot(owned.T, owned, precision=lax.Precision.HIGHEST, preferr...]
    reduce_scatter x1 -> x0, waiting for transfers between devices: 237 us -> none  [on_device(): lax.psum_scatter(ordered, ('gx', 'gy'), scatter_dimension=0, tiled=True)]
    ppermute x0 -> x30, waiting for transfers between devices: none -> 94.5 us  [the longest x18 67.4 us: swap(): return lax.ppermute(value, 'gy', [(i, i ^ partner) for i in range(ny)])]
    ppermute x0 -> x30, starting transfers between devices: none -> 51.7 us  [the longest x12 30.4 us: swap(): return lax.ppermute(value, 'gx', [(i, i ^ partner) for i in range(nx)])]
    gather x11 -> x0, local copies, waits for them, and re-layouts: 49 us -> none  [the longest x5 20.1 us: cell_step(): sketch_blocks[col_block]]
    scatter-add x10 -> x0, other arithmetic: 33.5 us -> none  [the longest x5 17 us: gene_step(): return total.at[col_block].add(product)]
    pallas_call x0 -> x1, Pallas kernels: none -> 25.8 us  [on_device(): pl.pallas_call(functools.partial(sparse_kernel, (nx, ny, parts, orders)),...]
    dot_general x12 -> x4, matrix products: 27.3 us -> 7.72 us  [the longest x1 4.58 us: on_device(): lax.dot_general(cell_sum.reshape(cell_blocks * side, wide), inverse, (((1...]
  transfers between devices with their start and end apart: 4 -> 30, of which waited for: 4 -> 22; matrix products, arithmetic and copies ran while one was open for 0% -> 15% of each run, Pallas kernels for 0% -> 0%
where the time goes in v1:
time: 237 us
  waiting for transfers between devices  94.5 us (40%)
  other arithmetic  53.6 us (23%)
  starting transfers between devices  51.7 us (22%)
  Pallas kernels  25.8 us (11%)
  matrix products  8.29 us (3%)
    ppermute x18, waiting for transfers between devices, swap(): return lax.ppermute(value, 'gy', [(i, i ^ partner) for i in range(ny)])  67.4 us
    ppermute x12, starting transfers between devices, swap(): return lax.ppermute(value, 'gx', [(i, i ^ partner) for i in range(nx)])  30.4 us
    ppermute x12, waiting for transfers between devices, swap(): return lax.ppermute(value, 'gx', [(i, i ^ partner) for i in range(nx)])  27.1 us
    pallas_call x1, Pallas kernels, on_device(): pl.pallas_call(functools.partial(sparse_kernel, (nx, ny, parts, orders)),...  25.8 us
    another operation x6, other arithmetic, inverse_of_factor(): lower = jnp.linalg.cholesky(gram)  24.8 us
    ppermute x18, starting transfers between devices, swap(): return lax.ppermute(value, 'gy', [(i, i ^ partner) for i in range(ny)])  21.3 us
    another operation x4, other arithmetic, inverse_of_factor(): return lax.linalg.triangular_solve(lower, eye, left_side=True, lower=True)  20.9 us
    add x20, other arithmetic, total(): return functools.reduce(jnp.add, terms)  7.78 us
  transfers between devices with their start and end apart: 30, of which 22 were waited for; matrix products, arithmetic and copies ran while one was open for 15% of the time, Pallas kernels for 0%

profile of v1, /device:TPU:0, one launch (start us, length us, event | category | flops | bytes accessed | tf_op | source)
XLA Modules:
  0.0 236.6 jit_solution(5096172519748730096)
XLA Ops:
  1.3 25.8 %tile_products.1 = (f32[32,128,128]{2,1,0:T(8,128)}, f32[32,128,128]{2,1,0:T(8,128)}, f32[32,128,128]{2,1,0:T(8,128)}, f32[32,128,128]{2,1,0:T(8,128)}, f32[32,1...) custom-call(s32[192]{0:T(256)} %rows.1, s32[192]{0:T(256)} %cols.1, ...), custom_call_target="tpu_custom_call" | custom-call | tf_op jit(solution)/shard_map/tile_products/pallas_call | solution.py:140
  27.2 0.5 collective-permute-start.10
  27.7 0.4 collective-permute-start.20
  28.2 0.9 copy.9
  29.2 2.3 collective-permute-done
  31.6 4.3 %collective-permute-start.1 = (f32[128,128]{0,1:T(8,128)S(1)}, f32[128,128]{0,1:T(8,128)S(1)}, u32[]{:S(2)}, u32[]{:S(2)}) collective-permute-start(f32[128,128]{0,1:T(8,128)S(1)} %add.146), channel_id=1, source_target_pairs={{0,2},{1,3},{2,0},{3,1},{4,6},{5,7},{6,4},{7,5},{8,10},{9,11},{10,... | collective-permute-start | bytes 196616 | tf_op jit(solution)/shard_map/ppermute | solution.py:169
  35.9 2.4 %collective-permute-done.1 = f32[128,128]{0,1:T(8,128)S(1)} collective-permute-done((f32[128,128]{0,1:T(8,128)S(1)}, f32[128,128]{0,1:T(8,128)S(1)}, u32[]{:S(2)}, u32[]{:S(2)}) %collective-permute-start.1) | collective-permute-done | bytes 65568 | tf_op jit(solution)/shard_map/ppermute | solution.py:169
  38.3 3.5 %collective-permute-start.2 = (f32[128,128]{0,1:T(8,128)S(1)}, f32[128,128]{0,1:T(8,128)S(1)}, u32[]{:S(2)}, u32[]{:S(2)}) collective-permute-start(f32[128,128]{0,1:T(8,128)S(1)} %add.147), channel_id=1, source_target_pairs={{0,4},{1,5},{2,6},{3,7},{4,0},{5,1},{6,2},{7,3},{8,12},{9,13},{10,... | collective-permute-start | bytes 196616 | tf_op jit(solution)/shard_map/ppermute | solution.py:169
  41.9 2.2 collective-permute-done.2
  44.1 5.2 %collective-permute-start.3 = (f32[128,128]{0,1:T(8,128)S(1)}, f32[128,128]{0,1:T(8,128)S(1)}, u32[]{:S(2)}, u32[]{:S(2)}) collective-permute-start(f32[128,128]{0,1:T(8,128)S(1)} %add.148), channel_id=1, source_target_pairs={{0,8},{8,0},{16,24},{24,16},{1,9},{9,1},{17,25},{25,17},{2,10},{10... | collective-permute-start | bytes 196616 | tf_op jit(solution)/shard_map/ppermute | solution.py:171
  49.3 2.2 collective-permute-done.3
  51.6 9.2 %collective-permute-start.4 = (f32[128,128]{0,1:T(8,128)S(1)}, f32[128,128]{0,1:T(8,128)S(1)}, u32[]{:S(2)}, u32[]{:S(2)}) collective-permute-start(f32[128,128]{0,1:T(8,128)S(1)} %add.149), channel_id=1, source_target_pairs={{0,16},{8,24},{16,0},{24,8},{1,17},{9,25},{17,1},{25,9},{2,18},{10... | collective-permute-start | bytes 196616 | tf_op jit(solution)/shard_map/ppermute | solution.py:171
  60.8 2.2 collective-permute-done.4
  63.1 11.7 %cholesky.44 = f32[128,128]{1,0:T(8,128)S(1)} custom-call(f32[128,128]{1,0:T(8,128)S(1)} %fusion.11), custom_call_target="Cholesky" | custom-call | tf_op jit(solution)/shard_map/jit(cholesky)/cholesky | solution.py:196
  74.9 0.6 compare_reduce_fusion.1
  75.5 0.7 fusion.6
  76.2 9.8 %custom-call.6 = f32[1,128,128]{1,2,0:T(8,128)S(1)} custom-call(f32[1,128,128]{2,1,0:T(8,128)S(1)} %fusion.6), custom_call_target="InvertDiagBlocksLowerTriangular" | custom-call | tf_op jit(solution)/shard_map/triangular_solve/custom-call.0 | solution.py:197
  86.0 2.6 %slice_add_fusion.7 = (f32[16,128,128]{2,1,0:T(8,128)S(1)}, f32[16,128,128]{2,1,0:T(8,128)S(1)}) fusion(f32[32,128,128]{2,1,0:T(8,128)} %collective-permute-done.5, f32[32,128,128]{2,1,0:T(8,128)} %get-tuple-element.16), kind=kLoop, calls=%fused_computation.10 | loop fusion | flops 524288 | bytes 6291456 | tf_op jit(solution)/shard_map/add | solution.py:179
  88.6 1.6 collective-permute-start.6
  90.2 2.0 slice_add_fusion.5
  92.2 1.5 collective-permute-start.11
  93.7 2.0 slice_add_fusion.3
  95.7 1.5 collective-permute-start.16
  97.2 0.3 slice_add_fusion.1
  97.7 0.3 convolution_multiply_fusion.1
  98.0 16.7 %collective-permute-done.6 = f32[16,128,128]{2,1,0:T(8,128)S(1)} collective-permute-done((f32[16,128,128]{2,1,0:T(8,128)S(1)}, f32[16,128,128]{2,1,0:T(8,128)S(1)}, u32[]{:S(2)}, u32[]{:S(2)}) %collective-permute-start.6) | collective-permute-done | bytes 1048608 | tf_op jit(solution)/shard_map/ppermute | solution.py:169
  114.9 2.4 %collective-permute-start.7 = (f32[8,128,128]{2,1,0:T(8,128)S(1)}, f32[8,128,128]{2,1,0:T(8,128)S(1)}, u32[]{:S(2)}, u32[]{:S(2)}) collective-permute-start(f32[8,128,128]{2,1,0:T(8,128)S(1)} %get-tuple-element.33), channel_id=1, source_target_pairs={{0,4},{1,5},{2,6},{3,7},{4,0},{5,1},{6,2},{7,3},{8,12},{9,13},{10,... | collective-permute-start | bytes 1572872 | tf_op jit(solution)/shard_map/ppermute | solution.py:169
  117.3 1.1 collective-permute-done.11
  118.5 0.9 collective-permute-start.12
  119.4 17.8 %collective-permute-done.16 = f32[16,128,128]{2,1,0:T(8,128)S(1)} collective-permute-done((f32[16,128,128]{2,1,0:T(8,128)S(1)}, f32[16,128,128]{2,1,0:T(8,128)S(1)}, u32[]{:S(2)}, u32[]{:S(2)}) %collective-permute-start.16) | collective-permute-done | bytes 1048608 | tf_op jit(solution)/shard_map/ppermute | solution.py:169
  137.4 2.4 %collective-permute-start.17 = (f32[8,128,128]{2,1,0:T(8,128)S(1)}, f32[8,128,128]{2,1,0:T(8,128)S(1)}, u32[]{:S(2)}, u32[]{:S(2)}) collective-permute-start(f32[8,128,128]{2,1,0:T(8,128)S(1)} %get-tuple-element.37), channel_id=1, source_target_pairs={{0,4},{1,5},{2,6},{3,7},{4,0},{5,1},{6,2},{7,3},{8,12},{9,13},{10,... | collective-permute-start | bytes 1572872 | tf_op jit(solution)/shard_map/ppermute | solution.py:169
  139.8 1.1 collective-permute-done.21
  141.0 0.9 collective-permute-start.22
  141.9 10.2 %collective-permute-done.7 = f32[8,128,128]{2,1,0:T(8,128)S(1)} collective-permute-done((f32[8,128,128]{2,1,0:T(8,128)S(1)}, f32[8,128,128]{2,1,0:T(8,128)S(1)}, u32[]{:S(2)}, u32[]{:S(2)}) %collective-permute-start.7) | collective-permute-done | bytes 524320 | tf_op jit(solution)/shard_map/ppermute | solution.py:169
  152.2 2.1 collective-permute-start.8
  154.4 4.3 %collective-permute-done.17 = f32[8,128,128]{2,1,0:T(8,128)S(1)} collective-permute-done((f32[8,128,128]{2,1,0:T(8,128)S(1)}, f32[8,128,128]{2,1,0:T(8,128)S(1)}, u32[]{:S(2)}, u32[]{:S(2)}) %collective-permute-start.17) | collective-permute-done | bytes 524320 | tf_op jit(solution)/shard_map/ppermute | solution.py:169
  158.8 1.8 collective-permute-start.18
  160.7 0.4 collective-permute-start.23
  161.0 0.7 collective-permute-done.8
  161.8 4.7 %collective-permute-start.9 = (f32[2,128,128]{2,1,0:T(8,128)S(1)}, f32[2,128,128]{2,1,0:T(8,128)S(1)}, u32[]{:S(2)}, u32[]{:S(2)}) collective-permute-start(f32[2,128,128]{2,1,0:T(8,128)S(1)} %slice_add_fusion.30), channel_id=1, source_target_pairs={{0,16},{8,24},{16,0},{24,8},{1,17},{9,25},{17,1},{25,9},{2,18},{10... | collective-permute-start | bytes 393224 | tf_op jit(solution)/shard_map/ppermute | solution.py:171
  166.5 5.1 %collective-permute-done.13 = f32[4,128,128]{2,1,0:T(8,128)S(1)} collective-permute-done((f32[4,128,128]{2,1,0:T(8,128)S(1)}, f32[4,128,128]{2,1,0:T(8,128)S(1)}, u32[]{:S(2)}, u32[]{:S(2)}) %collective-permute-start.13) | collective-permute-done | bytes 262176 | tf_op jit(solution)/shard_map/ppermute | solution.py:171
  171.6 1.1 collective-permute-start.14
  172.7 2.8 %collective-permute-done.18 = f32[4,128,128]{2,1,0:T(8,128)S(1)} collective-permute-done((f32[4,128,128]{2,1,0:T(8,128)S(1)}, f32[4,128,128]{2,1,0:T(8,128)S(1)}, u32[]{:S(2)}, u32[]{:S(2)}) %collective-permute-start.18) | collective-permute-done | bytes 262176 | tf_op jit(solution)/shard_map/ppermute | solution.py:171
  175.5 3.0 %collective-permute-start.19 = (f32[2,128,128]{2,1,0:T(8,128)S(1)}, f32[2,128,128]{2,1,0:T(8,128)S(1)}, u32[]{:S(2)}, u32[]{:S(2)}) collective-permute-start(f32[2,128,128]{2,1,0:T(8,128)S(1)} %slice_add_fusion.26), channel_id=1, source_target_pairs={{0,16},{8,24},{16,0},{24,8},{1,17},{9,25},{17,1},{25,9},{2,18},{10... | collective-permute-start | bytes 393224 | tf_op jit(solution)/shard_map/ppermute | solution.py:171
  178.5 1.9 collective-permute-done.23
  180.3 1.8 collective-permute-start.24
  182.2 3.0 %collective-permute-done.14 = f32[2,128,128]{2,1,0:T(8,128)S(1)} collective-permute-done((f32[2,128,128]{2,1,0:T(8,128)S(1)}, f32[2,128,128]{2,1,0:T(8,128)S(1)}, u32[]{:S(2)}, u32[]{:S(2)}) %collective-permute-start.14) | collective-permute-done | bytes 131104 | tf_op jit(solution)/shard_map/ppermute | solution.py:171
  185.2 3.5 %collective-permute-done.19 = f32[2,128,128]{2,1,0:T(8,128)S(1)} collective-permute-done((f32[2,128,128]{2,1,0:T(8,128)S(1)}, f32[2,128,128]{2,1,0:T(8,128)S(1)}, u32[]{:S(2)}, u32[]{:S(2)}) %collective-permute-start.19) | collective-permute-done | bytes 131104 | tf_op jit(solution)/shard_map/ppermute | solution.py:171
  188.7 1.4 collective-permute-done.24
  190.1 0.6 fusion.12
  190.7 1.2 fusion.13
  192.0 1.2 collective-permute-done.25
  193.2 0.6 collective-permute-start.26
  193.8 3.7 %collective-permute-done.26 = f32[128,128]{0,1:T(8,128)S(1)} collective-permute-done((f32[128,128]{0,1:T(8,128)S(1)}, f32[128,128]{0,1:T(8,128)S(1)}, u32[]{:S(2)}, u32[]{:S(2)}) %collective-permute-start.26) | collective-permute-done | bytes 65568 | tf_op jit(solution)/shard_map/ppermute | solution.py:169
  197.7 4.3 %collective-permute-done.27 = f32[128,128]{0,1:T(8,128)S(1)} collective-permute-done((f32[128,128]{0,1:T(8,128)S(1)}, f32[128,128]{0,1:T(8,128)S(1)}, u32[]{:S(2)}, u32[]{:S(2)}) %collective-permute-start.27) | collective-permute-done | bytes 65568 | tf_op jit(solution)/shard_map/ppermute | solution.py:169
  202.0 4.3 %collective-permute-done.28 = f32[128,128]{0,1:T(8,128)S(1)} collective-permute-done((f32[128,128]{0,1:T(8,128)S(1)}, f32[128,128]{0,1:T(8,128)S(1)}, u32[]{:S(2)}, u32[]{:S(2)}) %collective-permute-start.28) | collective-permute-done | bytes 65568 | tf_op jit(solution)/shard_map/ppermute | solution.py:171
  206.3 1.1 collective-permute-start.29
  207.3 4.6 %convolution_convert_fusion = bf16[8192,128]{1,0:T(8,128)(2,1)} fusion(f32[8192,128]{1,0:T(8,128)S(1)} %bitcast.29, f32[128,128]{1,0:T(8,128)S(1)} %convolution_multiply_fusion.1), kind=kOutput, calls=%fused_computation | convolution fusion | flops 1611661312 | bytes 6356992 | tf_op jit(solution)/shard_map/dot_general | solution.py:201
  212.1 11.7 %cholesky.55 = f32[128,128]{1,0:T(8,128)S(1)} custom-call(f32[128,128]{1,0:T(8,128)S(1)} %fusion.9), custom_call_target="Cholesky" | custom-call | tf_op jit(solution)/shard_map/jit(cholesky)/cholesky | solution.py:196
  223.8 0.6 compare_reduce_fusion
  224.4 0.7 fusion.7
  225.1 9.8 %custom-call.7 = f32[1,128,128]{1,2,0:T(8,128)S(1)} custom-call(f32[1,128,128]{2,1,0:T(8,128)S(1)} %fusion.7), custom_call_target="InvertDiagBlocksLowerTriangular" | custom-call | tf_op jit(solution)/shard_map/triangular_solve/custom-call.0 | solution.py:197
  234.9 0.3 convolution_multiply_fusion
  235.2 1.4 fusion.14
  (57 shorter events, 2.2 us)
Async XLA Ops:
  27.1 58.9 %collective-permute-start.5 = (f32[32,128,128]{2,1,0:T(8,128)}, f32[32,128,128]{2,1,0:T(8,128)}, u32[]{:S(2)}, u32[]{:S(2)}) collective-permute-start(f32[32,128,128]{2,1,0:T(8,128)} %get-tuple-element.17), channel_id=1, source_target_pairs={{0,1},{1,0},{2,3},{3,2},{4,5},{5,4},{6,7},{7,6},{8,9},{9,8},{10,11... | collective-permute-start | bytes 6291464 | tf_op jit(solution)/shard_map/ppermute | solution.py:169
  27.2 63.1 %collective-permute-start.10 = (f32[32,128,128]{2,1,0:T(8,128)}, f32[32,128,128]{2,1,0:T(8,128)}, u32[]{:S(2)}, u32[]{:S(2)}) collective-permute-start(f32[32,128,128]{2,1,0:T(8,128)} %get-tuple-element.19), channel_id=1, source_target_pairs={{0,1},{1,0},{2,3},{3,2},{4,5},{5,4},{6,7},{7,6},{8,9},{9,8},{10,11... | collective-permute-start | bytes 6291464 | tf_op jit(solution)/shard_map/ppermute | solution.py:169
  27.6 66.1 %collective-permute-start.15 = (f32[32,128,128]{2,1,0:T(8,128)}, f32[32,128,128]{2,1,0:T(8,128)}, u32[]{:S(2)}, u32[]{:S(2)}) collective-permute-start(f32[32,128,128]{2,1,0:T(8,128)} %get-tuple-element.21), channel_id=1, source_target_pairs={{0,1},{1,0},{2,3},{3,2},{4,5},{5,4},{6,7},{7,6},{8,9},{9,8},{10,11... | collective-permute-start | bytes 6291464 | tf_op jit(solution)/shard_map/ppermute | solution.py:169
  27.7 69.5 %collective-permute-start.20 = (f32[32,128,128]{2,1,0:T(8,128)}, f32[32,128,128]{2,1,0:T(8,128)S(1)}, u32[]{:S(2)}, u32[]{:S(2)}) collective-permute-start(f32[32,128,128]{2,1,0:T(8,128)} %get-tuple-element.23), channel_id=1, source_target_pairs={{0,1},{1,0},{2,3},{3,2},{4,5},{5,4},{6,7},{7,6},{8,9},{9,8},{10,11... | collective-permute-start | bytes 6291464 | tf_op jit(solution)/shard_map/ppermute | solution.py:169
  29.1 2.5 %collective-permute-start = (f32[128,128]{0,1:T(8,128)S(1)}, f32[128,128]{0,1:T(8,128)S(1)}, u32[]{:S(2)}, u32[]{:S(2)}) collective-permute-start(f32[128,128]{0,1:T(8,128)S(1)} %copy.9), channel_id=1, source_target_pairs={{0,1},{1,0},{2,3},{3,2},{4,5},{5,4},{6,7},{7,6},{8,9},{9,8},{10,11... | collective-permute-start | bytes 196616 | tf_op jit(solution)/shard_map/ppermute | solution.py:169
  31.6 6.7 %collective-permute-start.1 = (f32[128,128]{0,1:T(8,128)S(1)}, f32[128,128]{0,1:T(8,128)S(1)}, u32[]{:S(2)}, u32[]{:S(2)}) collective-permute-start(f32[128,128]{0,1:T(8,128)S(1)} %add.146), channel_id=1, source_target_pairs={{0,2},{1,3},{2,0},{3,1},{4,6},{5,7},{6,4},{7,5},{8,10},{9,11},{10,... | collective-permute-start | bytes 196616 | tf_op jit(solution)/shard_map/ppermute | solution.py:169
  38.3 5.8 %collective-permute-start.2 = (f32[128,128]{0,1:T(8,128)S(1)}, f32[128,128]{0,1:T(8,128)S(1)}, u32[]{:S(2)}, u32[]{:S(2)}) collective-permute-start(f32[128,128]{0,1:T(8,128)S(1)} %add.147), channel_id=1, source_target_pairs={{0,4},{1,5},{2,6},{3,7},{4,0},{5,1},{6,2},{7,3},{8,12},{9,13},{10,... | collective-permute-start | bytes 196616 | tf_op jit(solution)/shard_map/ppermute | solution.py:169
  44.1 7.5 %collective-permute-start.3 = (f32[128,128]{0,1:T(8,128)S(1)}, f32[128,128]{0,1:T(8,128)S(1)}, u32[]{:S(2)}, u32[]{:S(2)}) collective-permute-start(f32[128,128]{0,1:T(8,128)S(1)} %add.148), channel_id=1, source_target_pairs={{0,8},{8,0},{16,24},{24,16},{1,9},{9,1},{17,25},{25,17},{2,10},{10... | collective-permute-start | bytes 196616 | tf_op jit(solution)/shard_map/ppermute | solution.py:171
  51.6 11.4 %collective-permute-start.4 = (f32[128,128]{0,1:T(8,128)S(1)}, f32[128,128]{0,1:T(8,128)S(1)}, u32[]{:S(2)}, u32[]{:S(2)}) collective-permute-start(f32[128,128]{0,1:T(8,128)S(1)} %add.149), channel_id=1, source_target_pairs={{0,16},{8,24},{16,0},{24,8},{1,17},{9,25},{17,1},{25,9},{2,18},{10... | collective-permute-start | bytes 196616 | tf_op jit(solution)/shard_map/ppermute | solution.py:171
  86.0 4.2 %copy-start.3 = (f32[32,128,128]{2,1,0:T(8,128)S(1)}, f32[32,128,128]{2,1,0:T(8,128)}, u32[]{:S(2)}) copy-start(f32[32,128,128]{2,1,0:T(8,128)} %get-tuple-element.18) | copy-start | bytes 6291460
  88.6 26.2 %collective-permute-start.6 = (f32[16,128,128]{2,1,0:T(8,128)S(1)}, f32[16,128,128]{2,1,0:T(8,128)S(1)}, u32[]{:S(2)}, u32[]{:S(2)}) collective-permute-start(f32[16,128,128]{2,1,0:T(8,128)S(1)} %get-tuple-element.25), channel_id=1, source_target_pairs={{0,2},{1,3},{2,0},{3,1},{4,6},{5,7},{6,4},{7,5},{8,10},{9,11},{10,... | collective-permute-start | bytes 3145736 | tf_op jit(solution)/shard_map/ppermute | solution.py:169
  90.2 3.5 %copy-start.2 = (f32[32,128,128]{2,1,0:T(8,128)S(1)}, f32[32,128,128]{2,1,0:T(8,128)}, u32[]{:S(2)}) copy-start(f32[32,128,128]{2,1,0:T(8,128)} %get-tuple-element.20) | copy-start | bytes 6291460
  92.2 26.2 %collective-permute-start.11 = (f32[16,128,128]{2,1,0:T(8,128)S(1)}, f32[16,128,128]{2,1,0:T(8,128)S(1)}, u32[]{:S(2)}, u32[]{:S(2)}) collective-permute-start(f32[16,128,128]{2,1,0:T(8,128)S(1)} %get-tuple-element.27), channel_id=1, source_target_pairs={{0,4},{1,5},{2,6},{3,7},{4,0},{5,1},{6,2},{7,3},{8,12},{9,13},{10,... | collective-permute-start | bytes 3145736 | tf_op jit(solution)/shard_map/ppermute | solution.py:169
  93.7 3.5 %copy-start.1 = (f32[32,128,128]{2,1,0:T(8,128)S(1)}, f32[32,128,128]{2,1,0:T(8,128)}, u32[]{:S(2)}) copy-start(f32[32,128,128]{2,1,0:T(8,128)} %get-tuple-element.22) | copy-start | bytes 6291460
  95.7 41.5 %collective-permute-start.16 = (f32[16,128,128]{2,1,0:T(8,128)S(1)}, f32[16,128,128]{2,1,0:T(8,128)S(1)}, u32[]{:S(2)}, u32[]{:S(2)}) collective-permute-start(f32[16,128,128]{2,1,0:T(8,128)S(1)} %get-tuple-element.29), channel_id=1, source_target_pairs={{0,2},{1,3},{2,0},{3,1},{4,6},{5,7},{6,4},{7,5},{8,10},{9,11},{10,... | collective-permute-start | bytes 3145736 | tf_op jit(solution)/shard_map/ppermute | solution.py:169
  97.5 43.4 %collective-permute-start.21 = (f32[16,128,128]{2,1,0:T(8,128)S(1)}, f32[16,128,128]{2,1,0:T(8,128)S(1)}, u32[]{:S(2)}, u32[]{:S(2)}) collective-permute-start(f32[16,128,128]{2,1,0:T(8,128)S(1)} %get-tuple-element.31), channel_id=1, source_target_pairs={{0,4},{1,5},{2,6},{3,7},{4,0},{5,1},{6,2},{7,3},{8,12},{9,13},{10,... | collective-permute-start | bytes 3145736 | tf_op jit(solution)/shard_map/ppermute | solution.py:169
  114.9 37.2 %collective-permute-start.7 = (f32[8,128,128]{2,1,0:T(8,128)S(1)}, f32[8,128,128]{2,1,0:T(8,128)S(1)}, u32[]{:S(2)}, u32[]{:S(2)}) collective-permute-start(f32[8,128,128]{2,1,0:T(8,128)S(1)} %get-tuple-element.33), channel_id=1, source_target_pairs={{0,4},{1,5},{2,6},{3,7},{4,0},{5,1},{6,2},{7,3},{8,12},{9,13},{10,... | collective-permute-start | bytes 1572872 | tf_op jit(solution)/shard_map/ppermute | solution.py:169
  118.5 35.7 %collective-permute-start.12 = (f32[8,128,128]{2,1,0:T(8,128)S(1)}, f32[8,128,128]{2,1,0:T(8,128)S(1)}, u32[]{:S(2)}, u32[]{:S(2)}) collective-permute-start(f32[8,128,128]{2,1,0:T(8,128)S(1)} %get-tuple-element.35), channel_id=1, source_target_pairs={{0,2},{1,3},{2,0},{3,1},{4,6},{5,7},{6,4},{7,5},{8,10},{9,11},{10,... | collective-permute-start | bytes 1572872 | tf_op jit(solution)/shard_map/ppermute | solution.py:169
  137.4 21.3 %collective-permute-start.17 = (f32[8,128,128]{2,1,0:T(8,128)S(1)}, f32[8,128,128]{2,1,0:T(8,128)S(1)}, u32[]{:S(2)}, u32[]{:S(2)}) collective-permute-start(f32[8,128,128]{2,1,0:T(8,128)S(1)} %get-tuple-element.37), channel_id=1, source_target_pairs={{0,4},{1,5},{2,6},{3,7},{4,0},{5,1},{6,2},{7,3},{8,12},{9,13},{10,... | collective-permute-start | bytes 1572872 | tf_op jit(solution)/shard_map/ppermute | solution.py:169
  141.0 19.6 %collective-permute-start.22 = (f32[8,128,128]{2,1,0:T(8,128)S(1)}, f32[8,128,128]{2,1,0:T(8,128)S(1)}, u32[]{:S(2)}, u32[]{:S(2)}) collective-permute-start(f32[8,128,128]{2,1,0:T(8,128)S(1)} %get-tuple-element.39), channel_id=1, source_target_pairs={{0,2},{1,3},{2,0},{3,1},{4,6},{5,7},{6,4},{7,5},{8,10},{9,11},{10,... | collective-permute-start | bytes 1572872 | tf_op jit(solution)/shard_map/ppermute | solution.py:169
  152.2 9.6 %collective-permute-start.8 = (f32[4,128,128]{2,1,0:T(8,128)S(1)}, f32[4,128,128]{2,1,0:T(8,128)S(1)}, u32[]{:S(2)}, u32[]{:S(2)}) collective-permute-start(f32[4,128,128]{2,1,0:T(8,128)S(1)} %get-tuple-element.41), channel_id=1, source_target_pairs={{0,8},{8,0},{16,24},{24,16},{1,9},{9,1},{17,25},{25,17},{2,10},{10... | collective-permute-start | bytes 786440 | tf_op jit(solution)/shard_map/ppermute | solution.py:171
  154.3 17.2 %collective-permute-start.13 = (f32[4,128,128]{2,1,0:T(8,128)S(1)}, f32[4,128,128]{2,1,0:T(8,128)S(1)}, u32[]{:S(2)}, u32[]{:S(2)}) collective-permute-start(f32[4,128,128]{2,1,0:T(8,128)S(1)} %get-tuple-element.43), channel_id=1, source_target_pairs={{0,8},{8,0},{16,24},{24,16},{1,9},{9,1},{17,25},{25,17},{2,10},{10... | collective-permute-start | bytes 786440 | tf_op jit(solution)/shard_map/ppermute | solution.py:171
  158.8 16.7 %collective-permute-start.18 = (f32[4,128,128]{2,1,0:T(8,128)S(1)}, f32[4,128,128]{2,1,0:T(8,128)S(1)}, u32[]{:S(2)}, u32[]{:S(2)}) collective-permute-start(f32[4,128,128]{2,1,0:T(8,128)S(1)} %get-tuple-element.45), channel_id=1, source_target_pairs={{0,8},{8,0},{16,24},{24,16},{1,9},{9,1},{17,25},{25,17},{2,10},{10... | collective-permute-start | bytes 786440 | tf_op jit(solution)/shard_map/ppermute | solution.py:171
  160.7 19.7 %collective-permute-start.23 = (f32[4,128,128]{2,1,0:T(8,128)S(1)}, f32[4,128,128]{2,1,0:T(8,128)S(1)}, u32[]{:S(2)}, u32[]{:S(2)}) collective-permute-start(f32[4,128,128]{2,1,0:T(8,128)S(1)} %get-tuple-element.47), channel_id=1, source_target_pairs={{0,8},{8,0},{16,24},{24,16},{1,9},{9,1},{17,25},{25,17},{2,10},{10... | collective-permute-start | bytes 786440 | tf_op jit(solution)/shard_map/ppermute | solution.py:171
  161.8 20.4 %collective-permute-start.9 = (f32[2,128,128]{2,1,0:T(8,128)S(1)}, f32[2,128,128]{2,1,0:T(8,128)S(1)}, u32[]{:S(2)}, u32[]{:S(2)}) collective-permute-start(f32[2,128,128]{2,1,0:T(8,128)S(1)} %slice_add_fusion.30), channel_id=1, source_target_pairs={{0,16},{8,24},{16,0},{24,8},{1,17},{9,25},{17,1},{25,9},{2,18},{10... | collective-permute-start | bytes 393224 | tf_op jit(solution)/shard_map/ppermute | solution.py:171
  171.6 13.6 %collective-permute-start.14 = (f32[2,128,128]{2,1,0:T(8,128)S(1)}, f32[2,128,128]{2,1,0:T(8,128)S(1)}, u32[]{:S(2)}, u32[]{:S(2)}) collective-permute-start(f32[2,128,128]{2,1,0:T(8,128)S(1)} %slice_add_fusion.28), channel_id=1, source_target_pairs={{0,16},{8,24},{16,0},{24,8},{1,17},{9,25},{17,1},{25,9},{2,18},{10... | collective-permute-start | bytes 393224 | tf_op jit(solution)/shard_map/ppermute | solution.py:171
  175.5 13.2 %collective-permute-start.19 = (f32[2,128,128]{2,1,0:T(8,128)S(1)}, f32[2,128,128]{2,1,0:T(8,128)S(1)}, u32[]{:S(2)}, u32[]{:S(2)}) collective-permute-start(f32[2,128,128]{2,1,0:T(8,128)S(1)} %slice_add_fusion.26), channel_id=1, source_target_pairs={{0,16},{8,24},{16,0},{24,8},{1,17},{9,25},{17,1},{25,9},{2,18},{10... | collective-permute-start | bytes 393224 | tf_op jit(solution)/shard_map/ppermute | solution.py:171
  180.3 9.7 %collective-permute-start.24 = (f32[2,128,128]{2,1,0:T(8,128)S(1)}, f32[2,128,128]{2,1,0:T(8,128)S(1)}, u32[]{:S(2)}, u32[]{:S(2)}) collective-permute-start(f32[2,128,128]{2,1,0:T(8,128)S(1)} %slice_add_fusion.24), channel_id=1, source_target_pairs={{0,16},{8,24},{16,0},{24,8},{1,17},{9,25},{17,1},{25,9},{2,18},{10... | collective-permute-start | bytes 393224 | tf_op jit(solution)/shard_map/ppermute | solution.py:171
  190.1 17.3 %copy-start = (f32[64,128,128]{2,1,0:T(8,128)S(1)}, f32[64,128,128]{2,1,0:T(8,128)}, u32[]{:S(2)}) copy-start(f32[64,128,128]{2,1,0:T(8,128)} %get-tuple-element.14) | copy-start | bytes 12582916
  191.9 1.3 collective-permute-start.25
  193.2 4.3 %collective-permute-start.26 = (f32[128,128]{0,1:T(8,128)S(1)}, f32[128,128]{0,1:T(8,128)S(1)}, u32[]{:S(2)}, u32[]{:S(2)}) collective-permute-start(f32[128,128]{0,1:T(8,128)S(1)} %add.187), channel_id=1, source_target_pairs={{0,2},{1,3},{2,0},{3,1},{4,6},{5,7},{6,4},{7,5},{8,10},{9,11},{10,... | collective-permute-start | bytes 196616 | tf_op jit(solution)/shard_map/ppermute | solution.py:169
  197.6 4.3 %collective-permute-start.27 = (f32[128,128]{0,1:T(8,128)S(1)}, f32[128,128]{0,1:T(8,128)S(1)}, u32[]{:S(2)}, u32[]{:S(2)}) collective-permute-start(f32[128,128]{0,1:T(8,128)S(1)} %add.188), channel_id=1, source_target_pairs={{0,4},{1,5},{2,6},{3,7},{4,0},{5,1},{6,2},{7,3},{8,12},{9,13},{10,... | collective-permute-start | bytes 196616 | tf_op jit(solution)/shard_map/ppermute | solution.py:169
  201.9 4.3 %collective-permute-start.28 = (f32[128,128]{0,1:T(8,128)S(1)}, f32[128,128]{0,1:T(8,128)S(1)}, u32[]{:S(2)}, u32[]{:S(2)}) collective-permute-start(f32[128,128]{0,1:T(8,128)S(1)} %add.189), channel_id=1, source_target_pairs={{0,8},{8,0},{16,24},{24,16},{1,9},{9,1},{17,25},{25,17},{2,10},{10... | collective-permute-start | bytes 196616 | tf_op jit(solution)/shard_map/ppermute | solution.py:171
  206.3 5.7 %collective-permute-start.29 = (f32[128,128]{0,1:T(8,128)S(1)}, f32[128,128]{0,1:T(8,128)S(1)}, u32[]{:S(2)}, u32[]{:S(2)}) collective-permute-start(f32[128,128]{0,1:T(8,128)S(1)} %add.190), channel_id=1, source_target_pairs={{0,16},{8,24},{16,0},{24,8},{1,17},{9,25},{17,1},{25,9},{2,18},{10... | collective-permute-start | bytes 196616 | tf_op jit(solution)/shard_map/ppermute | solution.py:171

commit v2 on v0

v2 whole, which is shorter than its diff:
```python
import functools
import math

import jax
import jax.numpy as jnp
from jax import lax
from jax.experimental import pallas as pl
from jax.experimental.pallas import tpu as pltpu
from jax.sharding import PartitionSpec as P

GROUP = 16
PANEL = 32
EXACT = lax.Precision.HIGHEST
SMEM = pl.BlockSpec(memory_space=pltpu.SMEM)
VMEM = pl.BlockSpec(memory_space=pltpu.VMEM)
ANY = pl.BlockSpec(memory_space=pl.ANY)
ROOMY = pltpu.CompilerParams(vmem_limit_bytes=60 * 2**20)
CELL_BLOCKS = 64


def bit_orders(nx, ny, far_first=False):
    low = (ny - 1).bit_length()
    near, far = list(range(low)), list(range(low, low + (nx - 1).bit_length()))
    swapped = list(near)
    if low >= 3:
        swapped[1], swapped[2] = swapped[2], swapped[1]
    if far_first:
        return [o[:1] + far + o[1:] for o in (near, swapped)]
    return [o + far for o in (near, swapped)]


def place_in(order, owner):
    place = 0
    for bit in order:
        place = place * 2 + ((owner >> bit) & 1)
    return place


def pair_table(owned):
    if owned % 8:
        return [(0, owned // 2, False)]
    return [(0, owned // 4, False), (owned // 2, owned // 8, True), (3 * owned // 4, owned // 8, False)]


def list_tiles(nx, ny, pairs, owned, rows, cols, live, order, slots, list_row, list_tile, list_slot):
    devices = nx * ny
    me = lax.axis_index("gx") * ny + lax.axis_index("gy")

    @pl.loop(0, slots.shape[0])
    def _(b):
        slots[b] = -1

    total = 0
    for first, each, far_first in pairs:
        size = devices * each // 2
        for part, bits in enumerate(bit_orders(nx, ny, far_first)):
            mine = place_in(bits, me)
            for owner in range(devices):
                place = (place_in(bits, owner) ^ mine) * each
                place += jnp.where(place < size, 0, size) + part * size + total
                for j in range(each):
                    slots[order[owner * owned + first + part * each + j]] = place + j
        total += 4 * size

    def step(t, found):
        slot = slots[cols[t]]
        list_tile[found] = t
        list_row[found] = rows[t]
        list_slot[found] = slot
        return found + (slot >= 0).astype(jnp.int32)

    found = lax.fori_loop(0, live, step, jnp.int32(0))
    for u in range(GROUP):
        list_tile[found + u] = 0
        list_row[found + u] = 0
        list_slot[found + u] = total
    return found


def add_products(found, list_row, list_tile, list_slot, tiles_v, split_v, sums_v):
    @pl.loop(0, (found + GROUP - 1) // GROUP)
    def _(q):
        products = []
        for u in range(GROUP):
            k = q * GROUP + u
            product = lax.dot_general(
                tiles_v[list_tile[k]],
                split_v[list_row[k]],
                (((0,), (0,)), ((), ())),
                preferred_element_type=jnp.float32,
            )
            n = product.shape[-1] // 2
            products.append(product[:, :n] + product[:, n:])
        for u in range(GROUP):
            sums_v[list_slot[q * GROUP + u]] += products[u]


def zero(ref):
    @pl.loop(0, ref.shape[0])
    def _(b):
        ref[b] = jnp.zeros(ref.shape[1:], ref.dtype)


def save_pieces(pairs, sums_v, pieces, sem):
    saves = []
    base = 0
    for p in range(len(pairs)):
        size = pieces[8 * p].shape[0]
        for k in (5, 7, 4, 6, 1, 3, 0, 2):
            at = pl.ds(base + k * size, size)
            to = pieces[8 * p + k].at[pl.ds(0, size)]
            saves.append(pltpu.make_async_copy(sums_v.at[at], to, sem.at[8 * p + k]))
        base += 8 * size
    for s in saves:
        s.start()
    return saves


def first_kernel(nx, ny, pairs, owned, rows, cols, count, order, tiles, sketch, *refs):
    n_pieces = 8 * len(pairs)
    pieces, split_out = refs[:n_pieces], refs[n_pieces]
    (
        sketch_v, tiles_v, y_v, split_v, sums_v, gram_v, slots, list_row, list_tile, list_slot,
        sem_s, sem_t, sem_y, sem_p, sem_g,
    ) = refs[n_pieces + 1 :]
    cell_blocks = split_v.shape[0]
    live = count[0]
    groups = (live + GROUP - 1) // GROUP

    def load_tiles(g):
        at = pl.ds(g * GROUP, GROUP)
        return pltpu.make_async_copy(tiles.at[at], tiles_v.at[at], sem_t.at[g])

    @pl.loop(0, groups)
    def _(g):
        load_tiles(g).start()
        for u in range(GROUP):
            t = g * GROUP + u
            pltpu.make_async_copy(sketch.at[cols[t]], sketch_v.at[t], sem_s.at[g]).start()

    zero(y_v)
    zero(sums_v)
    found = list_tiles(nx, ny, pairs, owned, rows, cols, live, order, slots, list_row, list_tile, list_slot)

    @pl.loop(0, groups)
    def _(g):
        load_tiles(g).wait()
        at = pl.ds(g * GROUP, GROUP)
        pltpu.make_async_copy(sketch.at[pl.ds(0, GROUP)], sketch_v.at[at], sem_s.at[g]).wait()
        products = []
        for u in range(GROUP):
            t = g * GROUP + u
            products.append(jnp.dot(tiles_v[t], sketch_v[t], preferred_element_type=jnp.float32))
        for u in range(GROUP):
            t = g * GROUP + u
            y_v[jnp.where(t < live, rows[t], cell_blocks)] += products[u]

    gram_v[...] = jnp.zeros_like(gram_v)

    @pl.loop(0, cell_blocks // 8)
    def _(b):
        at = pl.ds(b * 8, 8)
        y = y_v[at]
        high = y.astype(jnp.bfloat16)
        low = (y - high.astype(jnp.float32)).astype(jnp.bfloat16)
        both = jnp.concatenate([high, low], axis=-1)
        split_v[at] = both
        rows = y.shape[0] * y.shape[1]
        gram_v[0] += lax.dot_general(
            high.reshape(rows, -1), both.reshape(rows, -1), (((0,), (0,)), ((), ())), preferred_element_type=jnp.float32
        )

    save_split = pltpu.make_async_copy(split_v, split_out, sem_y)
    save_split.start()
    n = y_v.shape[-1]
    cross = gram_v[0, :, n:]
    gram_v[0, :, :n] += cross + cross.T
    rider = pieces[5]
    save_gram = pltpu.make_async_copy(gram_v.at[:, :, pl.ds(0, n)], rider.at[pl.ds(rider.shape[0] - 1, 1)], sem_g)
    save_gram.start()
    add_products(found, list_row, list_tile, list_slot, tiles_v, split_v, sums_v)
    for s in save_pieces(pairs, sums_v, pieces, sem_p):
        s.wait()
    save_split.wait()
    save_gram.wait()


def second_kernel(nx, ny, pairs, owned, rows, cols, count, order, tiles, split, *refs):
    pieces = refs[: 8 * len(pairs)]
    tiles_v, split_v, sums_v, slots, list_row, list_tile, list_slot, sem_t, sem_y, sem_p = refs[8 * len(pairs) :]
    live = count[0]
    load_split = pltpu.make_async_copy(split, split_v, sem_y)
    load_tiles = pltpu.make_async_copy(tiles, tiles_v, sem_t)
    load_split.start()
    load_tiles.start()
    zero(sums_v)
    found = list_tiles(nx, ny, pairs, owned, rows, cols, live, order, slots, list_row, list_tile, list_slot)
    load_split.wait()
    load_tiles.wait()
    add_products(found, list_row, list_tile, list_slot, tiles_v, split_v, sums_v)
    for s in save_pieces(pairs, sums_v, pieces, sem_p):
        s.wait()


def combine_kernel(counts, *refs):
    out = refs[-1]
    first = row = 0
    for terms, size in counts:
        total = refs[first][...]
        for k in range(1, terms):
            total += refs[first + k][...]
        out[pl.ds(row, size)] = total
        first += terms
        row += size


def inverse_factor(gram):
    n = gram.shape[0]
    row = lax.broadcasted_iota(jnp.int32, (PANEL, n), 0)
    eye = lax.broadcasted_iota(jnp.int32, (n, n), 0) == lax.broadcasted_iota(jnp.int32, (n, n), 1)
    rest = jnp.concatenate([gram, eye.astype(jnp.float32)], axis=1)
    done = []
    for p in range(0, n, PANEL):
        a, w = rest[:PANEL, :n], rest[:PANEL, n:]
        columns = [jnp.broadcast_to(a[:, p + t : p + t + 1], (PANEL, n)) for t in range(PANEL)]
        scale = jnp.zeros((PANEL, n), jnp.float32)
        for s in range(PANEL):
            pivot = columns[s][s : s + 1]
            scale = jnp.where(row == s, lax.rsqrt(pivot), scale)
            if s + 1 < PANEL:
                factor = jnp.where(row > s, columns[s] * (1.0 / pivot), 0.0)
                for t in range(s + 1, PANEL):
                    columns[t] = columns[t] - factor * columns[t][s : s + 1]
                a = a - factor * a[s : s + 1]
                w = w - factor * w[s : s + 1]
        a, w = a * scale, w * scale
        done.append(w)
        if p + PANEL < n:
            update = lax.dot_general(
                a, jnp.concatenate([a, w], axis=1), (((0,), (0,)), ((), ())),
                precision=EXACT, preferred_element_type=jnp.float32,
            )
            rest = rest[PANEL:] - update[p + PANEL :]
    return jnp.concatenate(done, axis=0)


def times_transposed(x, w):
    return lax.dot_general(x, w, (((1,), (1,)), ((), ())), precision=EXACT, preferred_element_type=jnp.float32)


def factor_kernel(scale, gram, out):
    out[...] = inverse_factor(gram[...]) * scale


def cell_kernel(inverse, split, out):
    w = inverse[...]
    high = w.astype(jnp.bfloat16)
    low = (w - high.astype(jnp.float32)).astype(jnp.bfloat16)
    y = split[...].reshape(out.shape[0], -1)
    n = w.shape[0]

    def product(a, b):
        return lax.dot_general(a, b, (((1,), (1,)), ((), ())), preferred_element_type=jnp.float32)

    both = product(y, jnp.concatenate([high, high], axis=1))
    out[...] = (both + product(y[:, :n], low)).astype(out.dtype)


def owned_kernel(inverse, *refs):
    terms, (z_out, gram_out) = refs[:-2], refs[-2:]
    w = inverse[...]
    gram = None
    at = 0
    for term in terms:
        raw = term[...].reshape(-1, term.shape[-1])
        z = times_transposed(raw, w)
        z_out[pl.ds(at, raw.shape[0]), :] = z
        at += raw.shape[0]
        g = lax.dot_general(z, z, (((0,), (0,)), ((), ())), precision=EXACT, preferred_element_type=jnp.float32)
        gram = g if gram is None else gram + g
    gram_out[...] = gram


def gene_kernel(scale, gram, z, out):
    out[...] = times_transposed(z[...], inverse_factor(gram[...]) * scale)


def cost(microseconds):
    return pl.CostEstimate(flops=int(microseconds * 1e9), bytes_accessed=int(microseconds * 3e6), transcendentals=0)


def on_device(tiles, tile_rows, tile_cols, tile_counts, block_order, sketch, nx, ny):
    slots_all, side, _ = tiles.shape
    genes, wide = sketch.shape
    blocks = genes // side
    devices = nx * ny
    owned = blocks // devices
    table = pair_table(owned)
    orders = bit_orders(nx, ny)
    early_pairs, late_pairs = table[:2], table[2:]
    f32, bf16 = jnp.float32, jnp.bfloat16

    def piece_shapes(pairs, rider):
        sizes = [devices * each // 4 for _, each, _ in pairs for _ in range(8)]
        sizes[5] += rider
        return [jax.ShapeDtypeStruct((n, side, wide), f32) for n in sizes]

    def list_scratch():
        room = slots_all + GROUP
        return [pltpu.SMEM((blocks,), jnp.int32)] + [pltpu.SMEM((room,), jnp.int32)] * 3

    def sums_scratch(pairs):
        return pltpu.VMEM((sum(2 * each for _, each, _ in pairs) * devices + 1, side, wide), f32)

    def swap(value, bit):
        partner = 1 << bit
        if partner < ny:
            return lax.ppermute(value, "gy", [(i, i ^ partner) for i in range(ny)])
        partner //= ny
        return lax.ppermute(value, "gx", [(i, i ^ partner) for i in range(nx)])

    *early, split = pl.pallas_call(
        functools.partial(first_kernel, nx, ny, early_pairs, owned),
        out_shape=piece_shapes(early_pairs, 1)
        + [jax.ShapeDtypeStruct((CELL_BLOCKS, side, 2 * wide), bf16)],
        in_specs=[SMEM] * 4 + [ANY] * 2,
        out_specs=[ANY] * (8 * len(early_pairs) + 1),
        scratch_shapes=[
            pltpu.VMEM((slots_all, side, wide), bf16),
            pltpu.VMEM((slots_all, side, side), bf16),
            pltpu.VMEM((CELL_BLOCKS + 1, side, wide), f32),
            pltpu.VMEM((CELL_BLOCKS, side, 2 * wide), bf16),
            sums_scratch(early_pairs),
            pltpu.VMEM((1, wide, 2 * wide), f32),
            *list_scratch(),
            pltpu.SemaphoreType.DMA((slots_all // GROUP,)),
            pltpu.SemaphoreType.DMA((slots_all // GROUP,)),
            pltpu.SemaphoreType.DMA,
            pltpu.SemaphoreType.DMA((8 * len(early_pairs),)),
            pltpu.SemaphoreType.DMA,
        ],
        compiler_params=ROOMY,
        cost_estimate=cost(4.0),
        name="tile_products",
    )(tile_rows, tile_cols, tile_counts, block_order, tiles, sketch.reshape(blocks, side, wide))

    done_before = [tile_counts]

    def follows(value):
        return lax.optimization_barrier((value, done_before[0]))[0]

    def note(value):
        done_before[0] = value
        return value

    bits = orders[0]
    shared = next(k for k in range(1, len(bits)) if all(o[k:] == bits[k:] for o in orders))
    orders_of = [bit_orders(nx, ny, far_first) for _, _, far_first in table]
    state = {}

    def begin(pair, *arrays):
        kept, quarters = arrays[:4], arrays[4:]
        half = kept[0].shape[0]
        got = {k: swap(quarters[k], bits[0]) for k in (1, 3, 0, 2)}
        terms = [[[(kept[2 * part + upper], 0), (got[2 * part + upper], 0)] for upper in range(2)] for part in range(2)]
        rider = [(quarters[1], half), (got[1], half)] if quarters[1].shape[0] > half else []
        state[pair] = [1, half, terms, rider]

    def wait(pairs):
        found = []
        for pair in pairs:
            _, _, terms, rider = state[pair]
            for array, _ in [terms[part][1][-1] for part in range(2)] + rider[-1:]:
                if not any(array is f for f in found):
                    found.append(array)
        ready = lax.optimization_barrier((*found, done_before[0]))

        def swapped(term):
            return next(((r, term[1]) for f, r in zip(found, ready) if f is term[0]), term)

        for pair in pairs:
            step, size, terms, rider = state[pair]
            terms = [[[swapped(t) for t in upper] for upper in part] for part in terms]
            state[pair] = [step, size, terms, [swapped(t) for t in rider]]

    def combine(groups):
        counts = tuple((len(terms), size) for terms, size in groups)
        specs, arrays = [], []
        for terms, size in groups:
            for array, at in terms:
                specs.append(pl.BlockSpec((size, side, wide), functools.partial(lambda place, _: (place, 0, 0), at // size)))
                arrays.append(array)
        rows = sum(size for _, size in groups)
        return pl.pallas_call(
            functools.partial(combine_kernel, counts),
            grid=(1,),
            out_shape=jax.ShapeDtypeStruct((rows, side, wide), f32),
            in_specs=specs,
            out_specs=pl.BlockSpec((rows, side, wide), lambda _: (0, 0, 0)),
            compiler_params=pltpu.CompilerParams(vmem_limit_bytes=24 * 2**20),
            cost_estimate=cost(0.01),
            name="combine",
        )(*arrays)

    def halves(size, base, got):
        cut = size // 2
        return [[(array, at + upper * cut) for array, at in (base, got)] for upper in range(2)]

    def send_apart(pair):
        step, size, terms, rider = state[pair]
        sent = [combine([(terms[part][1], size)] + ([(rider, 1)] if rider and part == 0 else [])) for part in range(2)]
        got = [swap(note(sent[part]), orders_of[pair][part][step]) for part in range(2)]
        base = [combine([(terms[part][0], size)]) for part in range(2)]
        rider = [(sent[0], size), (got[0], size)] if rider else []
        state[pair] = [step + 1, size // 2, [halves(size, (base[part], 0), (got[part], 0)) for part in range(2)], rider]

    def send_both(pair):
        step, size, terms, rider = state[pair]
        sent = note(combine([(terms[part][1], size) for part in range(2)] + ([(rider, 1)] if rider else [])))
        got = swap(sent, orders_of[pair][0][step])
        base = combine([(terms[part][0], size) for part in range(2)])
        rider = [(sent, 2 * size), (got, 2 * size)] if rider else []
        state[pair] = [step + 1, size // 2, [halves(size, (base, part * size), (got, part * size)) for part in range(2)], rider]

    def finish(pair):
        _, size, terms, _ = state[pair]
        return combine([(terms[part][0], max(1, 2 * size)) for part in range(2)])

    def small_sum(pair):
        return functools.reduce(jnp.add, [array[at] for array, at in state[pair][3]])

    cells_all = CELL_BLOCKS * side * devices

    def late_products(pairs):
        return pl.pallas_call(
            functools.partial(second_kernel, nx, ny, pairs, owned),
            out_shape=piece_shapes(pairs, 0),
            in_specs=[SMEM] * 4 + [ANY] * 2,
            out_specs=[ANY] * (8 * len(pairs)),
            scratch_shapes=[
                pltpu.VMEM((slots_all, side, side), bf16),
                pltpu.VMEM((CELL_BLOCKS, side, 2 * wide), bf16),
                sums_scratch(pairs),
                *list_scratch(),
                pltpu.SemaphoreType.DMA,
                pltpu.SemaphoreType.DMA,
                pltpu.SemaphoreType.DMA((8 * len(pairs),)),
            ],
            compiler_params=pltpu.CompilerParams(vmem_limit_bytes=36 * 2**20),
            cost_estimate=cost(4.0),
            name="late_products",
        )(tile_rows, tile_cols, tile_counts, block_order, tiles, follows(split))

    def cell_inverse(gram):
        return note(
            pl.pallas_call(
                functools.partial(factor_kernel, math.sqrt(cells_all)),
                out_shape=jax.ShapeDtypeStruct((wide, wide), f32),
                in_specs=[VMEM],
                out_specs=VMEM,
                cost_estimate=cost(1.5),
                name="cell_cholesky",
            )(follows(gram))
        )

    def cells(inverse):
        step = 8
        return note(
            pl.pallas_call(
                cell_kernel,
                grid=(CELL_BLOCKS // step,),
                out_shape=jax.ShapeDtypeStruct((CELL_BLOCKS * side, wide), bf16),
                in_specs=[
                    pl.BlockSpec((wide, wide), lambda b: (0, 0)),
                    pl.BlockSpec((step, side, 2 * wide), lambda b: (b, 0, 0)),
                ],
                out_specs=pl.BlockSpec((step * side, wide), lambda b: (b, 0)),
                cost_estimate=cost(1.0),
                name="cell_factor",
            )(follows(inverse), split)
        )

    begin(0, *early[:8])
    if len(table) == 1:
        for step in range(1, len(bits)):
            wait([0])
            send_apart(0) if step < shared else send_both(0)
        wait([0])
        inverse = cell_inverse(small_sum(0))
        finals = [finish(0)]
        cell_factor = cells(inverse)
    else:
        begin(1, *early[8:])
        wait([0])
        send_apart(0)
        wait([1])
        send_both(1)
        late = late_products(late_pairs)
        note(late[0])
        begin(2, *late)
        wait([0, 1])
        send_apart(0)
        send_both(1)
        wait([2])
        send_apart(2)
        wait([0, 1, 2])
        send_both(0)
        send_apart(2)
        send_apart(1)
        wait([0, 1, 2])
        send_both(0)
        send_both(2)
        send_apart(1)
        wait([0, 1, 2])
        send_both(2)
        inverse = cell_inverse(small_sum(0))
        finals = [finish(0), finish(1)]
        cell_factor = cells(inverse)
        wait([2])
        finals.append(finish(2))
    z, gene_gram = pl.pallas_call(
        owned_kernel,
        out_shape=[jax.ShapeDtypeStruct((owned * side, wide), f32), jax.ShapeDtypeStruct((wide, wide), f32)],
        in_specs=[VMEM] * (1 + len(finals)),
        out_specs=[VMEM] * 2,
        name="gene_gram",
    )(inverse, *finals)
    for bit in bits:
        gene_gram = gene_gram + swap(gene_gram, bit)
    gene_factor = pl.pallas_call(
        functools.partial(gene_kernel, math.sqrt(genes)),
        out_shape=jax.ShapeDtypeStruct((owned * side, wide), f32),
        in_specs=[VMEM] * 2,
        out_specs=VMEM,
        name="gene_factor",
    )(gene_gram, z)
    return (cell_factor, gene_factor)


def solution(mesh):
    placed = (
        P(("gx", "gy"), None, None),
        P(("gx", "gy")),
        P(("gx", "gy")),
        P(("gx", "gy")),
        P(),
        P(),
    )
    return jax.shard_map(
        functools.partial(on_device, nx=mesh.shape["gx"], ny=mesh.shape["gy"]),
        mesh=mesh,
        in_specs=placed,
        out_specs=(P(("gx", "gy"), None), P(("gx", "gy"), None)),
        check_vma=False,
    )
```

time: 722 us -> 168 us (0.23)
  waiting for transfers between devices: 517 us -> 66.8 us
  other arithmetic: 88.3 us -> 2.14 us
  local copies, waits for them, and re-layouts: 61.1 us -> 7.09 us
  Pallas kernels: 0 us -> 45.9 us
  starting transfers between devices: 0.34 us -> 43.2 us
  matrix products: 35.9 us -> 0 us
  between operations: 14.5 us -> 1.72 us
    psum x3 -> x0, waiting for transfers between devices: 279 us -> none  [the longest x1 122 us: on_device(): lax.psum(jnp.dot(owned.T, owned, precision=lax.Precision.HIGHEST, preferr...]
    reduce_scatter x1 -> x0, waiting for transfers between devices: 237 us -> none  [on_device(): lax.psum_scatter(ordered, ('gx', 'gy'), scatter_dimension=0, tiled=True)]
    ppermute x0 -> x35, waiting for transfers between devices: none -> 66.8 us  [the longest x8 38.1 us: swap(): return lax.ppermute(value, 'gx', [(i, i ^ partner) for i in range(nx)])]
    gather x11 -> x0, local copies, waits for them, and re-layouts: 49 us -> none  [the longest x5 20.1 us: cell_step(): sketch_blocks[col_block]]
    pallas_call x0 -> x45, Pallas kernels: none -> 45.9 us  [the longest x1 15.9 us: on_device(): pl.pallas_call(functools.partial(first_kernel, nx, ny, early_pairs, owned...]
    another operation x10 -> x0, other arithmetic: 45.7 us -> none  [the longest x3 12.4 us: on_device(): lower = jnp.linalg.cholesky(gram)]
    ppermute x0 -> x35, starting transfers between devices: none -> 43.2 us  [the longest x27 23.6 us: swap(): return lax.ppermute(value, 'gy', [(i, i ^ partner) for i in range(ny)])]
    scatter-add x10 -> x0, other arithmetic: 33.5 us -> none  [the longest x5 17 us: gene_step(): return total.at[col_block].add(product)]
  transfers between devices with their start and end apart: 4 -> 35, of which waited for: 4 -> 18; matrix products, arithmetic and copies ran while one was open for 0% -> 0% of each run, Pallas kernels for 0% -> 12%
where the time goes in v2:
time: 168 us; the launch traced here: 167 us
  waiting for transfers between devices  66.8 us (40%)
  Pallas kernels  45.9 us (27%)
  starting transfers between devices  43.2 us (26%)
  local copies, waits for them, and re-layouts  7.09 us (4%)
  other arithmetic  2.14 us (1%)
  between operations  1.72 us (1%)
    ppermute x8, waiting for transfers between devices, swap(): return lax.ppermute(value, 'gx', [(i, i ^ partner) for i in range(nx)])  38.1 us
    ppermute x27, waiting for transfers between devices, swap(): return lax.ppermute(value, 'gy', [(i, i ^ partner) for i in range(ny)])  28.6 us
    ppermute x27, starting transfers between devices, swap(): return lax.ppermute(value, 'gy', [(i, i ^ partner) for i in range(ny)])  23.6 us
    ppermute x8, starting transfers between devices, swap(): return lax.ppermute(value, 'gx', [(i, i ^ partner) for i in range(nx)])  19.5 us
    pallas_call x1, Pallas kernels, on_device(): pl.pallas_call(functools.partial(first_kernel, nx, ny, early_pairs, owned...  15.9 us
    pallas_call x1, Pallas kernels, cells(): pl.pallas_call(cell_kernel, grid=(CELL_BLOCKS // step,), out_shape=jax.Sh...  7.39 us
    unnamed x36, local copies, waits for them, and re-layouts  7.09 us
    pallas_call x1, Pallas kernels, on_device(): pl.pallas_call(functools.partial(gene_kernel, math.sqrt(genes)), out_shap...  6.83 us
  transfers between devices with their start and end apart: 35, of which 18 were waited for; matrix products, arithmetic and copies ran while one was open for 0% of the time, Pallas kernels for 12%

profile of v2, /device:TPU:0, one launch (start us, length us, event | category | flops | bytes accessed | tf_op | source)
XLA Modules:
  0.0 166.8 jit_solution(17596741272059538451)
XLA Ops:
  1.3 15.9 %tile_products.1 = (f32[16,128,128]{2,1,0:T(8,128)}, f32[16,128,128]{2,1,0:T(8,128)}, f32[16,128,128]{2,1,0:T(8,128)}, f32[16,128,128]{2,1,0:T(8,128)}, f32[16,1...) custom-call(s32[192]{0:T(256)} %rows.3, s32[192]{0:T(256)} %cols.3, ...), custom_call_target="tpu_custom_call" | custom-call | flops 4000000000 | bytes 12000000 | tf_op jit(solution)/shard_map/tile_products/pallas_call | solution.py:322
  17.3 0.5 collective-permute-start.2
  17.9 0.4 collective-permute-start.6
  18.4 3.4 %collective-permute-done.2.refs_1_ = f32[16,128,128]{2,1,0:T(8,128)S(1)} collective-permute-done((f32[16,128,128]{2,1,0:T(8,128)}, f32[16,128,128]{2,1,0:T(8,128)S(1)}, u32[]{:S(2)}, u32[]{:S(2)}) %collective-permute-start.2) | collective-permute-done | bytes 1048608 | tf_op jit(solution)/shard_map/ppermute | solution.py:318
  21.8 0.1 collective-permute-start.12
  21.9 0.4 collective-permute-start.9
  22.3 1.2 copy-done.4
  23.7 0.9 copy-done.11
  24.5 0.2 copy-done.12
  24.7 0.1 combine.42
  24.8 4.5 %collective-permute-start.7 = (f32[16,128,128]{2,1,0:T(8,128)S(1)}, f32[16,128,128]{2,1,0:T(8,128)S(1)}, u32[]{:S(2)}, u32[]{:S(2)}) collective-permute-start(f32[16,128,128]{2,1,0:T(8,128)S(1)} %combine.42), channel_id=1, source_target_pairs={{0,8},{8,0},{16,24},{24,16},{1,9},{9,1},{17,25},{25,17},{2,10},{10... | collective-permute-start | bytes 3145736 | tf_op jit(solution)/shard_map/ppermute | solution.py:320
  29.4 0.1 combine.40.refs_2_
  29.5 2.5 %collective-permute-start.3 = (f32[17,128,128]{2,1,0:T(8,128)S(1)}, f32[17,128,128]{2,1,0:T(8,128)S(1)}, u32[]{:S(2)}, u32[]{:S(2)}) collective-permute-start(f32[17,128,128]{2,1,0:T(8,128)S(1)} %combine.40.refs_2_), channel_id=1, source_target_pairs={{0,2},{1,3},{2,0},{3,1},{4,6},{5,7},{6,4},{7,5},{8,10},{9,11},{10,... | collective-permute-start | bytes 3342344 | tf_op jit(solution)/shard_map/ppermute | solution.py:318
  32.0 1.6 collective-permute-start.4
  33.7 2.8 %copy-done.13 = bf16[192,128,128]{2,1,0:T(8,128)(2,1)S(1)} copy-done((bf16[192,128,128]{2,1,0:T(8,128)(2,1)S(1)}, bf16[192,128,128]{2,1,0:T(8,128)(2,1)}, u32[]{:S(2)}) %copy-start.13) | copy-done | bytes 6291480
  36.5 5.0 %late_products.1 = (f32[8,128,128]{2,1,0:T(8,128)S(1)}, f32[8,128,128]{2,1,0:T(8,128)S(1)}, f32[8,128,128]{2,1,0:T(8,128)S(1)}, f32[8,128,128]{2,1,0:T(8,128)S(1...) custom-call(s32[192]{0:T(256)S(1)} %copy-done.14, ...), custom_call_target="tpu_custom_call" | custom-call | flops 4000000000 | bytes 12000000 | tf_op jit(solution)/shard_map/late_products/pallas_call | solution.py:435
  41.5 1.0 collective-permute-start.14
  42.5 10.4 %collective-permute-done.7.refs_1_.refs_3_ = f32[16,128,128]{2,1,0:T(8,128)S(1)} collective-permute-done((f32[16,128,128]{2,1,0:T(8,128)S(1)}, f32[16,128,128]{2,1,0:T(8,128)S(1)}, u32[]{:S(2)}, u32[]{:S(2)}) %collective-permute-start.7) | collective-permute-done | bytes 1048608 | tf_op jit(solution)/shard_map/ppermute | solution.py:320
  52.8 0.1 combine.47.refs_0_.refs_2_
  53.0 0.1 combine.45.refs_0_
  53.1 3.6 %collective-permute-done.4.refs_1_ = f32[16,128,128]{2,1,0:T(8,128)S(1)} collective-permute-done((f32[16,128,128]{2,1,0:T(8,128)S(1)}, f32[16,128,128]{2,1,0:T(8,128)S(1)}, u32[]{:S(2)}, u32[]{:S(2)}) %collective-permute-start.4) | collective-permute-done | bytes 1048608 | tf_op jit(solution)/shard_map/ppermute | solution.py:318
  56.7 1.7 %collective-permute-start.10 = (f32[8,128,128]{2,1,0:T(8,128)S(1)}, f32[8,128,128]{2,1,0:T(8,128)S(1)}, u32[]{:S(2)}, u32[]{:S(2)}) collective-permute-start(f32[8,128,128]{2,1,0:T(8,128)S(1)} %combine.46), channel_id=1, source_target_pairs={{0,2},{1,3},{2,0},{3,1},{4,6},{5,7},{6,4},{7,5},{8,10},{9,11},{10,... | collective-permute-start | bytes 1572872 | tf_op jit(solution)/shard_map/ppermute | solution.py:318
  58.5 5.6 %collective-permute-start.13 = (f32[8,128,128]{2,1,0:T(8,128)S(1)}, f32[8,128,128]{2,1,0:T(8,128)S(1)}, u32[]{:S(2)}, u32[]{:S(2)}) collective-permute-start(f32[8,128,128]{2,1,0:T(8,128)S(1)} %combine.48), channel_id=1, source_target_pairs={{0,16},{8,24},{16,0},{24,8},{1,17},{9,25},{17,1},{25,9},{2,18},{10... | collective-permute-start | bytes 1572872 | tf_op jit(solution)/shard_map/ppermute | solution.py:320
  64.3 2.2 %collective-permute-start.8 = (f32[9,128,128]{2,1,0:T(8,128)S(1)}, f32[9,128,128]{2,1,0:T(8,128)S(1)}, u32[]{:S(2)}, u32[]{:S(2)}) collective-permute-start(f32[9,128,128]{2,1,0:T(8,128)S(1)} %combine.44.refs_4_), channel_id=1, source_target_pairs={{0,4},{1,5},{2,6},{3,7},{4,0},{5,1},{6,2},{7,3},{8,12},{9,13},{10,... | collective-permute-start | bytes 1769480 | tf_op jit(solution)/shard_map/ppermute | solution.py:318
  66.8 1.6 collective-permute-start.16
  68.3 3.3 %collective-permute-done.10.refs_3_ = f32[8,128,128]{2,1,0:T(8,128)S(1)} collective-permute-done((f32[8,128,128]{2,1,0:T(8,128)S(1)}, f32[8,128,128]{2,1,0:T(8,128)S(1)}, u32[]{:S(2)}, u32[]{:S(2)}) %collective-permute-start.10) | collective-permute-done | bytes 524320 | tf_op jit(solution)/shard_map/ppermute | solution.py:318
  71.7 14.7 %collective-permute-done.13.refs_1_ = f32[8,128,128]{2,1,0:T(8,128)S(1)} collective-permute-done((f32[8,128,128]{2,1,0:T(8,128)S(1)}, f32[8,128,128]{2,1,0:T(8,128)S(1)}, u32[]{:S(2)}, u32[]{:S(2)}) %collective-permute-start.13) | collective-permute-done | bytes 524320 | tf_op jit(solution)/shard_map/ppermute | solution.py:320
  86.5 3.1 %collective-permute-done.17.refs_1_ = f32[8,128,128]{2,1,0:T(8,128)S(1)} collective-permute-done((f32[8,128,128]{2,1,0:T(8,128)S(1)}, f32[8,128,128]{2,1,0:T(8,128)S(1)}, u32[]{:S(2)}, u32[]{:S(2)}) %collective-permute-start.17) | collective-permute-done | bytes 524320 | tf_op jit(solution)/shard_map/ppermute | solution.py:318
  89.7 1.2 collective-permute-start.18
  91.1 1.3 collective-permute-start.24
  92.5 1.0 collective-permute-start.22
  93.5 1.7 collective-permute-start.19
  95.2 0.3 collective-permute-start.20
  95.5 4.5 %collective-permute-done.19.refs_1_ = f32[2,128,128]{2,1,0:T(8,128)S(1)} collective-permute-done((f32[2,128,128]{2,1,0:T(8,128)S(1)}, f32[2,128,128]{2,1,0:T(8,128)S(1)}, u32[]{:S(2)}, u32[]{:S(2)}) %collective-permute-start.19) | collective-permute-done | bytes 131104 | tf_op jit(solution)/shard_map/ppermute | solution.py:318
  100.0 0.9 collective-permute-done.20.refs_1_
  100.9 1.9 %collective-permute-done.18.refs_1_.refs_3_.refs_5_ = f32[9,128,128]{2,1,0:T(8,128)S(1)} collective-permute-done((f32[9,128,128]{2,1,0:T(8,128)S(1)}, f32[9,128,128]{2,1,0:T(8,128)S(1)}, u32[]{:S(2)}, u32[]{:S(2)}) %collective-permute-start.18) | collective-permute-done | bytes 589856 | tf_op jit(solution)/shard_map/ppermute | solution.py:320
  102.9 1.7 collective-permute-start.25
  104.6 1.8 %collective-permute-start.28 = (f32[4,128,128]{2,1,0:T(8,128)S(1)}, f32[4,128,128]{2,1,0:T(8,128)S(1)}, u32[]{:S(2)}, u32[]{:S(2)}) collective-permute-start(f32[4,128,128]{2,1,0:T(8,128)S(1)} %combine.68), channel_id=1, source_target_pairs={{0,8},{8,0},{16,24},{24,16},{1,9},{9,1},{17,25},{25,17},{2,10},{10... | collective-permute-start | bytes 786440 | tf_op jit(solution)/shard_map/ppermute | solution.py:320
  106.5 2.0 %collective-permute-start.26 = (f32[1,128,128]{2,1,0:T(8,128)S(1)}, f32[1,128,128]{2,1,0:T(8,128)S(1)}, u32[]{:S(2)}, u32[]{:S(2)}) collective-permute-start(f32[1,128,128]{2,1,0:T(8,128)S(1)} %combine.63), channel_id=1, source_target_pairs={{0,4},{1,5},{2,6},{3,7},{4,0},{5,1},{6,2},{7,3},{8,12},{9,13},{10,... | collective-permute-start | bytes 196616 | tf_op jit(solution)/shard_map/ppermute | solution.py:318
  108.5 0.5 collective-permute-start.27
  109.1 1.8 %collective-permute-done.26.refs_1_ = f32[1,128,128]{2,1,0:T(8,128)S(1)} collective-permute-done((f32[1,128,128]{2,1,0:T(8,128)S(1)}, f32[1,128,128]{2,1,0:T(8,128)S(1)}, u32[]{:S(2)}, u32[]{:S(2)}) %collective-permute-start.26) | collective-permute-done | bytes 65568 | tf_op jit(solution)/shard_map/ppermute | solution.py:318
  110.8 2.0 %collective-permute-done.27.refs_3_ = f32[1,128,128]{2,1,0:T(8,128)S(1)} collective-permute-done((f32[1,128,128]{2,1,0:T(8,128)S(1)}, f32[1,128,128]{2,1,0:T(8,128)S(1)}, u32[]{:S(2)}, u32[]{:S(2)}) %collective-permute-start.27) | collective-permute-done | bytes 65568 | tf_op jit(solution)/shard_map/ppermute | solution.py:318
  112.8 2.2 %collective-permute-done.28.refs_1_.refs_3_ = f32[4,128,128]{2,1,0:T(8,128)S(1)} collective-permute-done((f32[4,128,128]{2,1,0:T(8,128)S(1)}, f32[4,128,128]{2,1,0:T(8,128)S(1)}, u32[]{:S(2)}, u32[]{:S(2)}) %collective-permute-start.28) | collective-permute-done | bytes 262176 | tf_op jit(solution)/shard_map/ppermute | solution.py:320
  114.9 2.4 %collective-permute-done.25.refs_1_.refs_3_ = f32[5,128,128]{2,1,0:T(8,128)S(1)} collective-permute-done((f32[5,128,128]{2,1,0:T(8,128)S(1)}, f32[5,128,128]{2,1,0:T(8,128)S(1)}, u32[]{:S(2)}, u32[]{:S(2)}) %collective-permute-start.25) | collective-permute-done | bytes 327712 | tf_op jit(solution)/shard_map/ppermute | solution.py:320
  117.3 0.6 fusion.gram
  118.0 0.8 collective-permute-start.29
  118.8 5.7 %cell_cholesky.1.inverse = f32[128,128]{1,0:T(8,128)} custom-call(f32[128,128]{1,0:T(8,128)} %fusion.gram), custom_call_target="tpu_custom_call" | custom-call | flops 1500000000 | bytes 4500000 | tf_op jit(solution)/shard_map/cell_cholesky/pallas_call | solution.py:456
  124.6 0.7 copy-done.5
  125.3 0.6 copy-done.7
  126.0 7.4 %cell_factor.1 = bf16[8192,128]{1,0:T(8,128)(2,1)} custom-call(f32[128,128]{1,0:T(8,128)} %cell_cholesky.1.inverse, bf16[64,128,256]{2,1,0:T(8,128)(2,1)} %get-tuple-element.71.split), custom_call_target="tpu_custom_call" | custom-call | flops 1000000000 | bytes 3000000 | tf_op jit(solution)/shard_map/cell_factor/pallas_call | solution.py:469
  133.4 0.6 copy-done.8
  134.0 3.2 %gene_gram.1 = (f32[1024,128]{1,0:T(8,128)}, f32[128,128]{1,0:T(8,128)}) custom-call(f32[128,128]{1,0:T(8,128)} %cell_cholesky.1.inverse, f32[4,128,128]{2,1,0:T(8,128)} %copy-done.5, f32[2,128,128]{2,1,0:T(8,128)} %copy-done.7, f32[2,128,128]{2,1,0:T(8,128)} %copy-done.8), custom_call_target="tpu_custom_call" | custom-call | tf_op jit(solution)/shard_map/gene_gram/pallas_call | solution.py:521
  137.2 1.5 collective-permute-done.30
  138.7 0.9 add.23
  139.5 2.2 %collective-permute-start.31 = (f32[128,128]{1,0:T(8,128)S(1)}, f32[128,128]{1,0:T(8,128)S(1)}, u32[]{:S(2)}, u32[]{:S(2)}) collective-permute-start(f32[128,128]{1,0:T(8,128)S(1)} %add.23), channel_id=1, source_target_pairs={{0,2},{1,3},{2,0},{3,1},{4,6},{5,7},{6,4},{7,5},{8,10},{9,11},{10,... | collective-permute-start | bytes 196616 | tf_op jit(solution)/shard_map/ppermute | solution.py:318
  141.7 2.4 %collective-permute-done.31 = f32[128,128]{1,0:T(8,128)S(1)} collective-permute-done((f32[128,128]{1,0:T(8,128)S(1)}, f32[128,128]{1,0:T(8,128)S(1)}, u32[]{:S(2)}, u32[]{:S(2)}) %collective-permute-start.31) | collective-permute-done | bytes 65568 | tf_op jit(solution)/shard_map/ppermute | solution.py:318
  144.1 2.4 %collective-permute-start.32 = (f32[128,128]{1,0:T(8,128)S(1)}, f32[128,128]{1,0:T(8,128)S(1)}, u32[]{:S(2)}, u32[]{:S(2)}) collective-permute-start(f32[128,128]{1,0:T(8,128)S(1)} %add.24), channel_id=1, source_target_pairs={{0,4},{1,5},{2,6},{3,7},{4,0},{5,1},{6,2},{7,3},{8,12},{9,13},{10,... | collective-permute-start | bytes 196616 | tf_op jit(solution)/shard_map/ppermute | solution.py:318
  146.5 2.2 %collective-permute-done.32 = f32[128,128]{1,0:T(8,128)S(1)} collective-permute-done((f32[128,128]{1,0:T(8,128)S(1)}, f32[128,128]{1,0:T(8,128)S(1)}, u32[]{:S(2)}, u32[]{:S(2)}) %collective-permute-start.32) | collective-permute-done | bytes 65568 | tf_op jit(solution)/shard_map/ppermute | solution.py:318
  148.8 3.1 %collective-permute-start.33 = (f32[128,128]{1,0:T(8,128)S(1)}, f32[128,128]{1,0:T(8,128)S(1)}, u32[]{:S(2)}, u32[]{:S(2)}) collective-permute-start(f32[128,128]{1,0:T(8,128)S(1)} %add.25), channel_id=1, source_target_pairs={{0,8},{8,0},{16,24},{24,16},{1,9},{9,1},{17,25},{25,17},{2,10},{10... | collective-permute-start | bytes 196616 | tf_op jit(solution)/shard_map/ppermute | solution.py:320
  151.8 2.2 %collective-permute-done.33 = f32[128,128]{1,0:T(8,128)S(1)} collective-permute-done((f32[128,128]{1,0:T(8,128)S(1)}, f32[128,128]{1,0:T(8,128)S(1)}, u32[]{:S(2)}, u32[]{:S(2)}) %collective-permute-start.33) | collective-permute-done | bytes 65568 | tf_op jit(solution)/shard_map/ppermute | solution.py:320
  154.1 0.9 collective-permute-start.34
  155.0 4.3 %collective-permute-done.34 = f32[128,128]{1,0:T(8,128)S(1)} collective-permute-done((f32[128,128]{1,0:T(8,128)S(1)}, f32[128,128]{1,0:T(8,128)S(1)}, u32[]{:S(2)}, u32[]{:S(2)}) %collective-permute-start.34) | collective-permute-done | bytes 65568 | tf_op jit(solution)/shard_map/ppermute | solution.py:320
  159.3 0.6 add.27.gram
  160.0 6.8 %gene_factor.1 = f32[1024,128]{1,0:T(8,128)} custom-call(f32[128,128]{1,0:T(8,128)} %add.27.gram, f32[1024,128]{1,0:T(8,128)} %get-tuple-element.109.z), custom_call_target="tpu_custom_call" | custom-call | tf_op jit(solution)/shard_map/gene_factor/pallas_call | solution.py:530
  (93 shorter events, 1.9 us)
Async XLA Ops:
  17.2 4.7 %collective-permute-start.1 = (f32[17,128,128]{2,1,0:T(8,128)}, f32[17,128,128]{2,1,0:T(8,128)S(1)}, u32[]{:S(2)}, u32[]{:S(2)}) collective-permute-start(f32[17,128,128]{2,1,0:T(8,128)} %get-tuple-element.59.refs_2_), channel_id=1, source_target_pairs={{0,1},{1,0},{2,3},{3,2},{4,5},{5,4},{6,7},{7,6},{8,9},{9,8},{10,11... | collective-permute-start | bytes 3342344 | tf_op jit(solution)/shard_map/ppermute | solution.py:318
  17.3 4.5 %collective-permute-start.2 = (f32[16,128,128]{2,1,0:T(8,128)}, f32[16,128,128]{2,1,0:T(8,128)S(1)}, u32[]{:S(2)}, u32[]{:S(2)}) collective-permute-start(f32[16,128,128]{2,1,0:T(8,128)} %get-tuple-element.60), channel_id=1, source_target_pairs={{0,1},{1,0},{2,3},{3,2},{4,5},{5,4},{6,7},{7,6},{8,9},{9,8},{10,11... | collective-permute-start | bytes 3145736 | tf_op jit(solution)/shard_map/ppermute | solution.py:318
  17.8 5.8 %collective-permute-start.5 = (f32[8,128,128]{2,1,0:T(8,128)}, f32[8,128,128]{2,1,0:T(8,128)S(1)}, u32[]{:S(2)}, u32[]{:S(2)}) collective-permute-start(f32[8,128,128]{2,1,0:T(8,128)} %get-tuple-element.65), channel_id=1, source_target_pairs={{0,1},{1,0},{2,3},{3,2},{4,5},{5,4},{6,7},{7,6},{8,9},{9,8},{10,11... | collective-permute-start | bytes 1572872 | tf_op jit(solution)/shard_map/ppermute | solution.py:318
  17.9 5.8 %collective-permute-start.6 = (f32[8,128,128]{2,1,0:T(8,128)}, f32[8,128,128]{2,1,0:T(8,128)S(1)}, u32[]{:S(2)}, u32[]{:S(2)}) collective-permute-start(f32[8,128,128]{2,1,0:T(8,128)} %get-tuple-element.66), channel_id=1, source_target_pairs={{0,1},{1,0},{2,3},{3,2},{4,5},{5,4},{6,7},{7,6},{8,9},{9,8},{10,11... | collective-permute-start | bytes 1572872 | tf_op jit(solution)/shard_map/ppermute | solution.py:318
  18.3 13.7 %collective-permute-start.11 = (f32[8,128,128]{2,1,0:T(8,128)}, f32[8,128,128]{2,1,0:T(8,128)S(1)}, u32[]{:S(2)}, u32[]{:S(2)}) collective-permute-start(f32[8,128,128]{2,1,0:T(8,128)} %get-tuple-element.78), channel_id=1, source_target_pairs={{0,1},{1,0},{2,3},{3,2},{4,5},{5,4},{6,7},{7,6},{8,9},{9,8},{10,11... | collective-permute-start | bytes 1572872 | tf_op jit(solution)/shard_map/ppermute | solution.py:318
  21.8 11.9 %collective-permute-start.12 = (f32[8,128,128]{2,1,0:T(8,128)}, f32[8,128,128]{2,1,0:T(8,128)S(1)}, u32[]{:S(2)}, u32[]{:S(2)}) collective-permute-start(f32[8,128,128]{2,1,0:T(8,128)} %get-tuple-element.80), channel_id=1, source_target_pairs={{0,1},{1,0},{2,3},{3,2},{4,5},{5,4},{6,7},{7,6},{8,9},{9,8},{10,11... | collective-permute-start | bytes 1572872 | tf_op jit(solution)/shard_map/ppermute | solution.py:318
  21.9 19.6 %collective-permute-start.9 = (f32[16,128,128]{2,1,0:T(8,128)}, f32[16,128,128]{2,1,0:T(8,128)S(1)}, u32[]{:S(2)}, u32[]{:S(2)}) collective-permute-start(f32[16,128,128]{2,1,0:T(8,128)} %get-tuple-element.75), channel_id=1, source_target_pairs={{0,1},{1,0},{2,3},{3,2},{4,5},{5,4},{6,7},{7,6},{8,9},{9,8},{10,11... | collective-permute-start | bytes 3145736 | tf_op jit(solution)/shard_map/ppermute | solution.py:318
  22.3 1.2 copy-start.4
  23.5 1.0 copy-start.11
  23.5 1.2 copy-start.12
  23.6 5.8 %copy-start.1 = (f32[17,128,128]{2,1,0:T(8,128)S(1)}, f32[17,128,128]{2,1,0:T(8,128)}, u32[]{:S(2)}) copy-start(f32[17,128,128]{2,1,0:T(8,128)} %get-tuple-element.59.refs_2_) | copy-start | bytes 3342340
  23.6 5.8 %copy-start.6 = (f32[16,128,128]{2,1,0:T(8,128)S(1)}, f32[16,128,128]{2,1,0:T(8,128)}, u32[]{:S(2)}) copy-start(f32[16,128,128]{2,1,0:T(8,128)} %get-tuple-element.58.refs_0_) | copy-start | bytes 3145732
  24.8 28.0 %collective-permute-start.7 = (f32[16,128,128]{2,1,0:T(8,128)S(1)}, f32[16,128,128]{2,1,0:T(8,128)S(1)}, u32[]{:S(2)}, u32[]{:S(2)}) collective-permute-start(f32[16,128,128]{2,1,0:T(8,128)S(1)} %combine.42), channel_id=1, source_target_pairs={{0,8},{8,0},{16,24},{24,16},{1,9},{9,1},{17,25},{25,17},{2,10},{10... | collective-permute-start | bytes 3145736 | tf_op jit(solution)/shard_map/ppermute | solution.py:320
  29.4 4.2 %copy-start.17 = (f32[16,128,128]{2,1,0:T(8,128)S(1)}, f32[16,128,128]{2,1,0:T(8,128)}, u32[]{:S(2)}) copy-start(f32[16,128,128]{2,1,0:T(8,128)} %get-tuple-element.57) | copy-start | bytes 3145732
  29.4 4.2 %copy-start = (bf16[64,128,256]{2,1,0:T(8,128)(2,1)S(1)}, bf16[64,128,256]{2,1,0:T(8,128)(2,1)}, u32[]{:S(2)}) copy-start(bf16[64,128,256]{2,1,0:T(8,128)(2,1)} %get-tuple-element.71.split) | copy-start | bytes 12582916
  29.4 4.2 %copy-start.14 = (s32[192]{0:T(256)S(1)}, s32[192]{0:T(256)}, u32[]{:S(2)}) copy-start(s32[192]{0:T(256)} %rows.3) | copy-start | bytes 2308
  29.4 4.2 %copy-start.15 = (s32[192]{0:T(256)S(1)}, s32[192]{0:T(256)}, u32[]{:S(2)}) copy-start(s32[192]{0:T(256)} %cols.3) | copy-start | bytes 2308
  29.4 4.2 %copy-start.16 = (s32[256]{0:T(256)S(1)}, s32[256]{0:T(256)}, u32[]{:S(2)}) copy-start(s32[256]{0:T(256)} %order.3) | copy-start | bytes 3076
  29.5 27.1 %collective-permute-start.3 = (f32[17,128,128]{2,1,0:T(8,128)S(1)}, f32[17,128,128]{2,1,0:T(8,128)S(1)}, u32[]{:S(2)}, u32[]{:S(2)}) collective-permute-start(f32[17,128,128]{2,1,0:T(8,128)S(1)} %combine.40.refs_2_), channel_id=1, source_target_pairs={{0,2},{1,3},{2,0},{3,1},{4,6},{5,7},{6,4},{7,5},{8,10},{9,11},{10,... | collective-permute-start | bytes 3342344 | tf_op jit(solution)/shard_map/ppermute | solution.py:318
  32.0 24.6 %collective-permute-start.4 = (f32[16,128,128]{2,1,0:T(8,128)S(1)}, f32[16,128,128]{2,1,0:T(8,128)S(1)}, u32[]{:S(2)}, u32[]{:S(2)}) collective-permute-start(f32[16,128,128]{2,1,0:T(8,128)S(1)} %combine.41), channel_id=1, source_target_pairs={{0,4},{1,5},{2,6},{3,7},{4,0},{5,1},{6,2},{7,3},{8,12},{9,13},{10,... | collective-permute-start | bytes 3145736 | tf_op jit(solution)/shard_map/ppermute | solution.py:318
  33.6 30.5 %collective-permute-start = (f32[16,128,128]{2,1,0:T(8,128)S(1)}, f32[16,128,128]{2,1,0:T(8,128)S(1)}, u32[]{:S(2)}, u32[]{:S(2)}) collective-permute-start(f32[16,128,128]{2,1,0:T(8,128)S(1)} %copy-done.17), channel_id=1, source_target_pairs={{0,1},{1,0},{2,3},{3,2},{4,5},{5,4},{6,7},{7,6},{8,9},{9,8},{10,11... | collective-permute-start | bytes 3145736 | tf_op jit(solution)/shard_map/ppermute | solution.py:318
  33.7 2.8 %copy-start.13 = (bf16[192,128,128]{2,1,0:T(8,128)(2,1)S(1)}, bf16[192,128,128]{2,1,0:T(8,128)(2,1)}, u32[]{:S(2)}) copy-start(bf16[192,128,128]{2,1,0:T(8,128)(2,1)} %tiles.3) | copy-start | bytes 18874372
  36.4 16.4 %copy-start.9 = (f32[8,128,128]{2,1,0:T(8,128)S(1)}, f32[8,128,128]{2,1,0:T(8,128)}, u32[]{:S(2)}) copy-start(f32[8,128,128]{2,1,0:T(8,128)} %get-tuple-element.77.refs_0_) | copy-start | bytes 1572868
  36.5 16.4 %copy-start.10 = (f32[8,128,128]{2,1,0:T(8,128)S(1)}, f32[8,128,128]{2,1,0:T(8,128)}, u32[]{:S(2)}) copy-start(f32[8,128,128]{2,1,0:T(8,128)} %get-tuple-element.79.refs_2_) | copy-start | bytes 1572868
  41.5 11.5 %copy-start.3 = (f32[16,128,128]{2,1,0:T(8,128)S(1)}, f32[16,128,128]{2,1,0:T(8,128)}, u32[]{:S(2)}) copy-start(f32[16,128,128]{2,1,0:T(8,128)} %get-tuple-element.74.refs_0_) | copy-start | bytes 3145732
  41.5 25.0 %collective-permute-start.14 = (f32[8,128,128]{2,1,0:T(8,128)S(1)}, f32[8,128,128]{2,1,0:T(8,128)S(1)}, u32[]{:S(2)}, u32[]{:S(2)}) collective-permute-start(f32[8,128,128]{2,1,0:T(8,128)S(1)} %get-tuple-element.83), channel_id=1, source_target_pairs={{0,1},{1,0},{2,3},{3,2},{4,5},{5,4},{6,7},{7,6},{8,9},{9,8},{10,11... | collective-permute-start | bytes 1572872 | tf_op jit(solution)/shard_map/ppermute | solution.py:318
  52.8 13.7 %collective-permute-start.15 = (f32[8,128,128]{2,1,0:T(8,128)S(1)}, f32[8,128,128]{2,1,0:T(8,128)S(1)}, u32[]{:S(2)}, u32[]{:S(2)}) collective-permute-start(f32[8,128,128]{2,1,0:T(8,128)S(1)} %get-tuple-element.84), channel_id=1, source_target_pairs={{0,1},{1,0},{2,3},{3,2},{4,5},{5,4},{6,7},{7,6},{8,9},{9,8},{10,11... | collective-permute-start | bytes 1572872 | tf_op jit(solution)/shard_map/ppermute | solution.py:318
  56.7 7.4 %copy-start.2 = (f32[16,128,128]{2,1,0:T(8,128)S(1)}, f32[16,128,128]{2,1,0:T(8,128)}, u32[]{:S(2)}) copy-start(f32[16,128,128]{2,1,0:T(8,128)} %get-tuple-element.56.refs_0_) | copy-start | bytes 3145732
  56.7 14.9 %collective-permute-start.10 = (f32[8,128,128]{2,1,0:T(8,128)S(1)}, f32[8,128,128]{2,1,0:T(8,128)S(1)}, u32[]{:S(2)}, u32[]{:S(2)}) collective-permute-start(f32[8,128,128]{2,1,0:T(8,128)S(1)} %combine.46), channel_id=1, source_target_pairs={{0,2},{1,3},{2,0},{3,1},{4,6},{5,7},{6,4},{7,5},{8,10},{9,11},{10,... | collective-permute-start | bytes 1572872 | tf_op jit(solution)/shard_map/ppermute | solution.py:318
  58.5 27.8 %collective-permute-start.13 = (f32[8,128,128]{2,1,0:T(8,128)S(1)}, f32[8,128,128]{2,1,0:T(8,128)S(1)}, u32[]{:S(2)}, u32[]{:S(2)}) collective-permute-start(f32[8,128,128]{2,1,0:T(8,128)S(1)} %combine.48), channel_id=1, source_target_pairs={{0,16},{8,24},{16,0},{24,8},{1,17},{9,25},{17,1},{25,9},{2,18},{10... | collective-permute-start | bytes 1572872 | tf_op jit(solution)/shard_map/ppermute | solution.py:320
  64.3 25.4 %collective-permute-start.8 = (f32[9,128,128]{2,1,0:T(8,128)S(1)}, f32[9,128,128]{2,1,0:T(8,128)S(1)}, u32[]{:S(2)}, u32[]{:S(2)}) collective-permute-start(f32[9,128,128]{2,1,0:T(8,128)S(1)} %combine.44.refs_4_), channel_id=1, source_target_pairs={{0,4},{1,5},{2,6},{3,7},{4,0},{5,1},{6,2},{7,3},{8,12},{9,13},{10,... | collective-permute-start | bytes 1769480 | tf_op jit(solution)/shard_map/ppermute | solution.py:318
  66.6 23.1 %collective-permute-start.17 = (f32[8,128,128]{2,1,0:T(8,128)S(1)}, f32[8,128,128]{2,1,0:T(8,128)S(1)}, u32[]{:S(2)}, u32[]{:S(2)}) collective-permute-start(f32[8,128,128]{2,1,0:T(8,128)S(1)} %combine.50), channel_id=1, source_target_pairs={{0,4},{1,5},{2,6},{3,7},{4,0},{5,1},{6,2},{7,3},{8,12},{9,13},{10,... | collective-permute-start | bytes 1572872 | tf_op jit(solution)/shard_map/ppermute | solution.py:318
  66.8 22.9 %collective-permute-start.16 = (f32[8,128,128]{2,1,0:T(8,128)S(1)}, f32[8,128,128]{2,1,0:T(8,128)S(1)}, u32[]{:S(2)}, u32[]{:S(2)}) collective-permute-start(f32[8,128,128]{2,1,0:T(8,128)S(1)} %combine.49), channel_id=1, source_target_pairs={{0,2},{1,3},{2,0},{3,1},{4,6},{5,7},{6,4},{7,5},{8,10},{9,11},{10,... | collective-permute-start | bytes 1572872 | tf_op jit(solution)/shard_map/ppermute | solution.py:318
  71.7 19.2 %collective-permute-start.21 = (f32[8,128,128]{2,1,0:T(8,128)S(1)}, f32[8,128,128]{2,1,0:T(8,128)S(1)}, u32[]{:S(2)}, u32[]{:S(2)}) collective-permute-start(f32[8,128,128]{2,1,0:T(8,128)S(1)} %get-tuple-element.91), channel_id=1, source_target_pairs={{0,1},{1,0},{2,3},{3,2},{4,5},{5,4},{6,7},{7,6},{8,9},{9,8},{10,11... | collective-permute-start | bytes 1572872 | tf_op jit(solution)/shard_map/ppermute | solution.py:318
  86.4 4.6 %collective-permute-start.23 = (f32[8,128,128]{2,1,0:T(8,128)S(1)}, f32[8,128,128]{2,1,0:T(8,128)S(1)}, u32[]{:S(2)}, u32[]{:S(2)}) collective-permute-start(f32[8,128,128]{2,1,0:T(8,128)S(1)} %get-tuple-element.94), channel_id=1, source_target_pairs={{0,1},{1,0},{2,3},{3,2},{4,5},{5,4},{6,7},{7,6},{8,9},{9,8},{10,11... | collective-permute-start | bytes 1572872 | tf_op jit(solution)/shard_map/ppermute | solution.py:318
  89.7 13.1 %collective-permute-start.18 = (f32[9,128,128]{2,1,0:T(8,128)S(1)}, f32[9,128,128]{2,1,0:T(8,128)S(1)}, u32[]{:S(2)}, u32[]{:S(2)}) collective-permute-start(f32[9,128,128]{2,1,0:T(8,128)S(1)} %combine.53.refs_4_), channel_id=1, source_target_pairs={{0,8},{8,0},{16,24},{24,16},{1,9},{9,1},{17,25},{25,17},{2,10},{10... | collective-permute-start | bytes 1769480 | tf_op jit(solution)/shard_map/ppermute | solution.py:320
  91.1 9.8 %collective-permute-start.24 = (f32[4,128,128]{2,1,0:T(8,128)S(1)}, f32[4,128,128]{2,1,0:T(8,128)S(1)}, u32[]{:S(2)}, u32[]{:S(2)}) collective-permute-start(f32[4,128,128]{2,1,0:T(8,128)S(1)} %combine.60), channel_id=1, source_target_pairs={{0,2},{1,3},{2,0},{3,1},{4,6},{5,7},{6,4},{7,5},{8,10},{9,11},{10,... | collective-permute-start | bytes 786440 | tf_op jit(solution)/shard_map/ppermute | solution.py:318
  92.5 8.4 %collective-permute-start.22 = (f32[4,128,128]{2,1,0:T(8,128)S(1)}, f32[4,128,128]{2,1,0:T(8,128)S(1)}, u32[]{:S(2)}, u32[]{:S(2)}) collective-permute-start(f32[4,128,128]{2,1,0:T(8,128)S(1)} %combine.58), channel_id=1, source_target_pairs={{0,4},{1,5},{2,6},{3,7},{4,0},{5,1},{6,2},{7,3},{8,12},{9,13},{10,... | collective-permute-start | bytes 786440 | tf_op jit(solution)/shard_map/ppermute | solution.py:318
  93.5 6.5 %collective-permute-start.19 = (f32[2,128,128]{2,1,0:T(8,128)S(1)}, f32[2,128,128]{2,1,0:T(8,128)S(1)}, u32[]{:S(2)}, u32[]{:S(2)}) collective-permute-start(f32[2,128,128]{2,1,0:T(8,128)S(1)} %combine.55), channel_id=1, source_target_pairs={{0,2},{1,3},{2,0},{3,1},{4,6},{5,7},{6,4},{7,5},{8,10},{9,11},{10,... | collective-permute-start | bytes 393224 | tf_op jit(solution)/shard_map/ppermute | solution.py:318
  95.2 5.7 %collective-permute-start.20 = (f32[2,128,128]{2,1,0:T(8,128)S(1)}, f32[2,128,128]{2,1,0:T(8,128)S(1)}, u32[]{:S(2)}, u32[]{:S(2)}) collective-permute-start(f32[2,128,128]{2,1,0:T(8,128)S(1)} %combine.56), channel_id=1, source_target_pairs={{0,4},{1,5},{2,6},{3,7},{4,0},{5,1},{6,2},{7,3},{8,12},{9,13},{10,... | collective-permute-start | bytes 393224 | tf_op jit(solution)/shard_map/ppermute | solution.py:318
  102.9 14.5 %collective-permute-start.25 = (f32[5,128,128]{2,1,0:T(8,128)S(1)}, f32[5,128,128]{2,1,0:T(8,128)S(1)}, u32[]{:S(2)}, u32[]{:S(2)}) collective-permute-start(f32[5,128,128]{2,1,0:T(8,128)S(1)} %combine.61), channel_id=1, source_target_pairs={{0,16},{8,24},{16,0},{24,8},{1,17},{9,25},{17,1},{25,9},{2,18},{10... | collective-permute-start | bytes 983048 | tf_op jit(solution)/shard_map/ppermute | solution.py:320
  104.6 10.3 %collective-permute-start.28 = (f32[4,128,128]{2,1,0:T(8,128)S(1)}, f32[4,128,128]{2,1,0:T(8,128)S(1)}, u32[]{:S(2)}, u32[]{:S(2)}) collective-permute-start(f32[4,128,128]{2,1,0:T(8,128)S(1)} %combine.68), channel_id=1, source_target_pairs={{0,8},{8,0},{16,24},{24,16},{1,9},{9,1},{17,25},{25,17},{2,10},{10... | collective-permute-start | bytes 786440 | tf_op jit(solution)/shard_map/ppermute | solution.py:320
  106.5 4.3 %collective-permute-start.26 = (f32[1,128,128]{2,1,0:T(8,128)S(1)}, f32[1,128,128]{2,1,0:T(8,128)S(1)}, u32[]{:S(2)}, u32[]{:S(2)}) collective-permute-start(f32[1,128,128]{2,1,0:T(8,128)S(1)} %combine.63), channel_id=1, source_target_pairs={{0,4},{1,5},{2,6},{3,7},{4,0},{5,1},{6,2},{7,3},{8,12},{9,13},{10,... | collective-permute-start | bytes 196616 | tf_op jit(solution)/shard_map/ppermute | solution.py:318
  108.5 4.3 %collective-permute-start.27 = (f32[1,128,128]{2,1,0:T(8,128)S(1)}, f32[1,128,128]{2,1,0:T(8,128)S(1)}, u32[]{:S(2)}, u32[]{:S(2)}) collective-permute-start(f32[1,128,128]{2,1,0:T(8,128)S(1)} %combine.65), channel_id=1, source_target_pairs={{0,2},{1,3},{2,0},{3,1},{4,6},{5,7},{6,4},{7,5},{8,10},{9,11},{10,... | collective-permute-start | bytes 196616 | tf_op jit(solution)/shard_map/ppermute | solution.py:318
  118.0 15.4 %collective-permute-start.29 = (f32[2,128,128]{2,1,0:T(8,128)S(1)}, f32[2,128,128]{2,1,0:T(8,128)S(1)}, u32[]{:S(2)}, u32[]{:S(2)}) collective-permute-start(f32[2,128,128]{2,1,0:T(8,128)S(1)} %combine.70), channel_id=1, source_target_pairs={{0,16},{8,24},{16,0},{24,8},{1,17},{9,25},{17,1},{25,9},{2,18},{10... | collective-permute-start | bytes 393224 | tf_op jit(solution)/shard_map/ppermute | solution.py:320
  124.6 0.7 copy-start.5
  125.3 0.7 copy-start.7
  133.4 0.7 copy-start.8
  137.2 1.5 collective-permute-start.30
  139.5 4.6 %collective-permute-start.31 = (f32[128,128]{1,0:T(8,128)S(1)}, f32[128,128]{1,0:T(8,128)S(1)}, u32[]{:S(2)}, u32[]{:S(2)}) collective-permute-start(f32[128,128]{1,0:T(8,128)S(1)} %add.23), channel_id=1, source_target_pairs={{0,2},{1,3},{2,0},{3,1},{4,6},{5,7},{6,4},{7,5},{8,10},{9,11},{10,... | collective-permute-start | bytes 196616 | tf_op jit(solution)/shard_map/ppermute | solution.py:318
  144.1 4.6 %collective-permute-start.32 = (f32[128,128]{1,0:T(8,128)S(1)}, f32[128,128]{1,0:T(8,128)S(1)}, u32[]{:S(2)}, u32[]{:S(2)}) collective-permute-start(f32[128,128]{1,0:T(8,128)S(1)} %add.24), channel_id=1, source_target_pairs={{0,4},{1,5},{2,6},{3,7},{4,0},{5,1},{6,2},{7,3},{8,12},{9,13},{10,... | collective-permute-start | bytes 196616 | tf_op jit(solution)/shard_map/ppermute | solution.py:318
  148.8 5.3 %collective-permute-start.33 = (f32[128,128]{1,0:T(8,128)S(1)}, f32[128,128]{1,0:T(8,128)S(1)}, u32[]{:S(2)}, u32[]{:S(2)}) collective-permute-start(f32[128,128]{1,0:T(8,128)S(1)} %add.25), channel_id=1, source_target_pairs={{0,8},{8,0},{16,24},{24,16},{1,9},{9,1},{17,25},{25,17},{2,10},{10... | collective-permute-start | bytes 196616 | tf_op jit(solution)/shard_map/ppermute | solution.py:320
  154.1 5.2 %collective-permute-start.34 = (f32[128,128]{1,0:T(8,128)S(1)}, f32[128,128]{1,0:T(8,128)S(1)}, u32[]{:S(2)}, u32[]{:S(2)}) collective-permute-start(f32[128,128]{1,0:T(8,128)S(1)} %add.26), channel_id=1, source_target_pairs={{0,16},{8,24},{16,0},{24,8},{1,17},{9,25},{17,1},{25,9},{2,18},{10... | collective-permute-start | bytes 196616 | tf_op jit(solution)/shard_map/ppermute | solution.py:320

commit v3 on v2

--- a/solution.py
+++ b/solution.py
@@ -62,27 +62,37 @@
                     slots[order[owner * owned + first + part * each + j]] = place + j
         total += 4 * size
 
+    room = list_tile.shape[0] // len(pairs)
+    ends = [sum(2 * e * devices for _, e, _ in pairs[: k + 1]) for k in range(len(pairs))]
+
     def step(t, found):
         slot = slots[cols[t]]
-        list_tile[found] = t
-        list_row[found] = rows[t]
-        list_slot[found] = slot
-        return found + (slot >= 0).astype(jnp.int32)
-
-    found = lax.fori_loop(0, live, step, jnp.int32(0))
-    for u in range(GROUP):
-        list_tile[found + u] = 0
-        list_row[found + u] = 0
-        list_slot[found + u] = total
+        row = rows[t]
+        later = []
+        for k in range(len(pairs)):
+            at = found[k] + k * room
+            list_tile[at] = t
+            list_row[at] = row
+            list_slot[at] = slot
+            low = ends[k - 1] if k else 0
+            later.append(found[k] + jnp.logical_and(slot >= low, slot < ends[k]).astype(jnp.int32))
+        return tuple(later)
+
+    found = lax.fori_loop(0, live, step, (jnp.int32(0),) * len(pairs))
+    for k in range(len(pairs)):
+        for u in range(GROUP):
+            list_tile[found[k] + k * room + u] = 0
+            list_row[found[k] + k * room + u] = 0
+            list_slot[found[k] + k * room + u] = total
     return found
 
 
-def add_products(found, list_row, list_tile, list_slot, tiles_v, split_v, sums_v):
+def add_products(found, first, list_row, list_tile, list_slot, tiles_v, split_v, sums_v):
     @pl.loop(0, (found + GROUP - 1) // GROUP)
     def _(q):
         products = []
         for u in range(GROUP):
-            k = q * GROUP + u
+            k = first + q * GROUP + u
             product = lax.dot_general(
                 tiles_v[list_tile[k]],
                 split_v[list_row[k]],
@@ -92,7 +102,7 @@
             n = product.shape[-1] // 2
             products.append(product[:, :n] + product[:, n:])
         for u in range(GROUP):
-            sums_v[list_slot[q * GROUP + u]] += products[u]
+            sums_v[list_slot[first + q * GROUP + u]] += products[u]
 
 
 def zero(ref):
@@ -101,19 +111,21 @@
         ref[b] = jnp.zeros(ref.shape[1:], ref.dtype)
 
 
-def save_pieces(pairs, sums_v, pieces, sem):
+def add_and_save(pairs, found, list_row, list_tile, list_slot, tiles_v, split_v, sums_v, pieces, sem):
     saves = []
     base = 0
+    room = list_tile.shape[0] // len(pairs)
     for p in range(len(pairs)):
+        add_products(found[p], p * room, list_row, list_tile, list_slot, tiles_v, split_v, sums_v)
         size = pieces[8 * p].shape[0]
         for k in (5, 7, 4, 6, 1, 3, 0, 2):
             at = pl.ds(base + k * size, size)
             to = pieces[8 * p + k].at[pl.ds(0, size)]
             saves.append(pltpu.make_async_copy(sums_v.at[at], to, sem.at[8 * p + k]))
+            saves[-1].start()
         base += 8 * size
     for s in saves:
-        s.start()
-    return saves
+        s.wait()
 
 
 def first_kernel(nx, ny, pairs, owned, rows, cols, count, order, tiles, sketch, *refs):
@@ -178,9 +190,7 @@
     rider = pieces[5]
     save_gram = pltpu.make_async_copy(gram_v.at[:, :, pl.ds(0, n)], rider.at[pl.ds(rider.shape[0] - 1, 1)], sem_g)
     save_gram.start()
-    add_products(found, list_row, list_tile, list_slot, tiles_v, split_v, sums_v)
-    for s in save_pieces(pairs, sums_v, pieces, sem_p):
-        s.wait()
+    add_and_save(pairs, found, list_row, list_tile, list_slot, tiles_v, split_v, sums_v, pieces, sem_p)
     save_split.wait()
     save_gram.wait()
 
@@ -197,9 +207,7 @@
     found = list_tiles(nx, ny, pairs, owned, rows, cols, live, order, slots, list_row, list_tile, list_slot)
     load_split.wait()
     load_tiles.wait()
-    add_products(found, list_row, list_tile, list_slot, tiles_v, split_v, sums_v)
-    for s in save_pieces(pairs, sums_v, pieces, sem_p):
-        s.wait()
+    add_and_save(pairs, found, list_row, list_tile, list_slot, tiles_v, split_v, sums_v, pieces, sem_p)
 
 
 def combine_kernel(counts, *refs):
@@ -214,7 +222,7 @@
         row += size
 
 
-def inverse_factor(gram):
+def inverse_factor(gram, beside=lambda panel: None):
     n = gram.shape[0]
     row = lax.broadcasted_iota(jnp.int32, (PANEL, n), 0)
     eye = lax.broadcasted_iota(jnp.int32, (n, n), 0) == lax.broadcasted_iota(jnp.int32, (n, n), 1)
@@ -235,6 +243,7 @@
                 w = w - factor * w[s : s + 1]
         a, w = a * scale, w * scale
         done.append(w)
+        beside(p // PANEL)
         if p + PANEL < n:
             update = lax.dot_general(
                 a, jnp.concatenate([a, w], axis=1), (((0,), (0,)), ((), ())),
@@ -248,41 +257,67 @@
     return lax.dot_general(x, w, (((1,), (1,)), ((), ())), precision=EXACT, preferred_element_type=jnp.float32)
 
 
-def factor_kernel(scale, gram, out):
-    out[...] = inverse_factor(gram[...]) * scale
-
-
-def cell_kernel(inverse, split, out):
-    w = inverse[...]
-    high = w.astype(jnp.bfloat16)
-    low = (w - high.astype(jnp.float32)).astype(jnp.bfloat16)
-    y = split[...].reshape(out.shape[0], -1)
-    n = w.shape[0]
-
-    def product(a, b):
-        return lax.dot_general(a, b, (((1,), (1,)), ((), ())), preferred_element_type=jnp.float32)
-
-    both = product(y, jnp.concatenate([high, high], axis=1))
-    out[...] = (both + product(y[:, :n], low)).astype(out.dtype)
-
-
-def owned_kernel(inverse, *refs):
-    terms, (z_out, gram_out) = refs[:-2], refs[-2:]
-    w = inverse[...]
-    gram = None
+def total_of(refs):
+    return functools.reduce(jnp.add, [r[...].reshape(r.shape[-2:]) for r in refs])
+
+
+def factor_kernel(scale, *refs):
+    gram, out = refs[:-1], refs[-1]
+    out[...] = (inverse_factor(total_of(gram)) * scale).T
+
+
+def owned_kernel(counts, has_gram, inverse, *refs):
+    gram, terms, (z_out, gram_out) = refs[:has_gram], refs[has_gram:-2], refs[-2:]
+    rows = []
+    first = 0
+    for k in counts:
+        rows.append(functools.reduce(jnp.add, [t[...] for t in terms[first : first + k]]))
+        first += k
+    raw = jnp.concatenate(rows, axis=0) if len(rows) > 1 else rows[0]
+    raw = raw.reshape(-1, raw.shape[-1])
+    z = jnp.dot(raw, inverse[...], precision=EXACT, preferred_element_type=jnp.float32)
+    z_out[...] = z
+    g = lax.dot_general(z, z, (((0,), (0,)), ((), ())), precision=EXACT, preferred_element_type=jnp.float32)
+    if has_gram:
+        g += gram[0][0]
+    gram_out[0] = g
+
+
+def last_kernel(scale, n_grams, split, inverse, *refs):
+    split_v, out_v, sem_in, sem_out = refs[-4:]
+    grams, zs = refs[:n_grams], refs[n_grams:-6]
+    out, cells = refs[-6:-4]
+    chunks = sem_in.shape[0]
+    blocks, side, both = split_v.shape
+    chunk, n = blocks // chunks, both // 2
+    rows = chunk * side
+    loads, saves = [], []
+    for c in range(chunks):
+        at = pl.ds(c * chunk, chunk)
+        loads.append(pltpu.make_async_copy(split.at[at], split_v.at[at], sem_in.at[c]))
+        at = pl.ds(c * rows, rows)
+        saves.append(pltpu.make_async_copy(out_v.at[at], cells.at[at], sem_out.at[c]))
+        loads[c].start()
+    high = inverse[...].astype(jnp.bfloat16)
+    low = (inverse[...] - high.astype(jnp.float32)).astype(jnp.bfloat16)
+    right = jnp.concatenate(
+        [jnp.concatenate([high, low], axis=1), jnp.concatenate([high, jnp.zeros_like(low)], axis=1)], axis=0
+    )
+
+    def cell_rows(c):
+        loads[c].wait()
+        y = split_v[pl.ds(c * chunk, chunk)].reshape(rows, both)
+        g = jnp.dot(y, right, preferred_element_type=jnp.float32)
+        out_v[pl.ds(c * rows, rows), :] = (g[:, :n] + g[:, n:]).astype(out_v.dtype)
+        saves[c].start()
+
+    w = inverse_factor(total_of(grams), cell_rows) * scale
     at = 0
-    for term in terms:
-        raw = term[...].reshape(-1, term.shape[-1])
-        z = times_transposed(raw, w)
-        z_out[pl.ds(at, raw.shape[0]), :] = z
-        at += raw.shape[0]
-        g = lax.dot_general(z, z, (((0,), (0,)), ((), ())), precision=EXACT, preferred_element_type=jnp.float32)
-        gram = g if gram is None else gram + g
-    gram_out[...] = gram
-
-
-def gene_kernel(scale, gram, z, out):
-    out[...] = times_transposed(z[...], inverse_factor(gram[...]) * scale)
+    for z in zs:
+        out[pl.ds(at, z.shape[0]), :] = times_transposed(z[...], w)
+        at += z.shape[0]
+    for save in saves:
+        save.wait()
 
 
 def cost(microseconds):
@@ -305,9 +340,9 @@
         sizes[5] += rider
         return [jax.ShapeDtypeStruct((n, side, wide), f32) for n in sizes]
 
-    def list_scratch():
+    def list_scratch(pairs):
         room = slots_all + GROUP
-        return [pltpu.SMEM((blocks,), jnp.int32)] + [pltpu.SMEM((room,), jnp.int32)] * 3
+        return [pltpu.SMEM((blocks,), jnp.int32)] + [pltpu.SMEM((len(pairs) * room,), jnp.int32)] * 3
 
     def sums_scratch(pairs):
         return pltpu.VMEM((sum(2 * each for _, each, _ in pairs) * devices + 1, side, wide), f32)
@@ -332,7 +367,7 @@
             pltpu.VMEM((CELL_BLOCKS, side, 2 * wide), bf16),
             sums_scratch(early_pairs),
             pltpu.VMEM((1, wide, 2 * wide), f32),
-            *list_scratch(),
+            *list_scratch(early_pairs),
             pltpu.SemaphoreType.DMA((slots_all // GROUP,)),
             pltpu.SemaphoreType.DMA((slots_all // GROUP,)),
             pltpu.SemaphoreType.DMA,
@@ -361,10 +396,16 @@
     def begin(pair, *arrays):
         kept, quarters = arrays[:4], arrays[4:]
         half = kept[0].shape[0]
-        got = {k: swap(quarters[k], bits[0]) for k in (1, 3, 0, 2)}
-        terms = [[[(kept[2 * part + upper], 0), (got[2 * part + upper], 0)] for upper in range(2)] for part in range(2)]
-        rider = [(quarters[1], half), (got[1], half)] if quarters[1].shape[0] > half else []
-        state[pair] = [1, half, terms, rider]
+        terms = [[[(kept[2 * part + upper], 0)] for upper in range(2)] for part in range(2)]
+        state[pair] = [1, half, terms, []]
+        if quarters[1].shape[0] > half:
+            state[pair][3] = [(quarters[1], half)]
+
+        for k in (1, 3, 0, 2):
+            got = swap(quarters[k], orders_of[pair][0][0])
+            terms[k // 2][k % 2].append((got, 0))
+            if k == 1 and state[pair][3]:
+                state[pair][3].append((got, half))
 
     def wait(pairs):
         found = []
@@ -406,28 +447,64 @@
         cut = size // 2
         return [[(array, at + upper * cut) for array, at in (base, got)] for upper in range(2)]
 
-    def send_apart(pair):
+    def send_upper(pair, part):
         step, size, terms, rider = state[pair]
-        sent = [combine([(terms[part][1], size)] + ([(rider, 1)] if rider and part == 0 else [])) for part in range(2)]
-        got = [swap(note(sent[part]), orders_of[pair][part][step]) for part in range(2)]
+        groups = [(terms[part][1], size)] + ([(rider, 1)] if rider and part == 0 else [])
+        sent = note(combine(groups))
+        return sent, swap(sent, orders_of[pair][part][step])
+
+    def keep_lower(pair, sent, got):
+        step, size, terms, rider = state[pair]
         base = [combine([(terms[part][0], size)]) for part in range(2)]
         rider = [(sent[0], size), (got[0], size)] if rider else []
         state[pair] = [step + 1, size // 2, [halves(size, (base[part], 0), (got[part], 0)) for part in range(2)], rider]
 
-    def send_both(pair):
+    def send_apart(pair):
+        moved = [send_upper(pair, part) for part in range(2)]
+        keep_lower(pair, *zip(*moved))
+
+    def send_both_upper(pair):
         step, size, terms, rider = state[pair]
         sent = note(combine([(terms[part][1], size) for part in range(2)] + ([(rider, 1)] if rider else [])))
-        got = swap(sent, orders_of[pair][0][step])
+        return sent, swap(sent, orders_of[pair][0][step])
+
+    def keep_both_lower(pair, sent, got):
+        step, size, terms, rider = state[pair]
         base = combine([(terms[part][0], size) for part in range(2)])
         rider = [(sent, 2 * size), (got, 2 * size)] if rider else []
         state[pair] = [step + 1, size // 2, [halves(size, (base, part * size), (got, part * size)) for part in range(2)], rider]
 
-    def finish(pair):
-        _, size, terms, _ = state[pair]
-        return combine([(terms[part][0], max(1, 2 * size)) for part in range(2)])
-
-    def small_sum(pair):
-        return functools.reduce(jnp.add, [array[at] for array, at in state[pair][3]])
+    def send_both(pair):
+        keep_both_lower(pair, *send_both_upper(pair))
+
+    def term_specs(groups):
+        specs, arrays = [], []
+        for terms, size in groups:
+            for array, at in terms:
+                specs.append(pl.BlockSpec((size, side, wide), functools.partial(lambda place, _: (place, 0, 0), at // size)))
+                arrays.append(array)
+        return specs, arrays
+
+    def owners(pairs, inverse, gram=()):
+        groups = [(state[p][2][part][0], max(1, 2 * state[p][1])) for p in pairs for part in range(2)]
+        specs, arrays = term_specs(groups)
+        rows = sum(size for _, size in groups) * side
+        whole = pl.BlockSpec((wide, wide), lambda _: (0, 0))
+        square = pl.BlockSpec((1, wide, wide), lambda _: (0, 0, 0))
+        z, gram = pl.pallas_call(
+            functools.partial(owned_kernel, [len(terms) for terms, _ in groups], len(gram)),
+            grid=(1,),
+            out_shape=[jax.ShapeDtypeStruct((rows, wide), f32), jax.ShapeDtypeStruct((1, wide, wide), f32)],
+            in_specs=[whole] + [square] * len(gram) + specs,
+            out_specs=[pl.BlockSpec((rows, wide), lambda _: (0, 0)), square],
+            compiler_params=pltpu.CompilerParams(vmem_limit_bytes=24 * 2**20),
+            cost_estimate=cost(0.5),
+            name="owned_gram",
+        )(inverse, *gram, *arrays)
+        return z, note(gram)
+
+    def small_terms(pair):
+        return [array[at : at + 1] for array, at in state[pair][3]]
 
     cells_all = CELL_BLOCKS * side * devices
 
@@ -441,7 +518,7 @@
                 pltpu.VMEM((slots_all, side, side), bf16),
                 pltpu.VMEM((CELL_BLOCKS, side, 2 * wide), bf16),
                 sums_scratch(pairs),
-                *list_scratch(),
+                *list_scratch(pairs),
                 pltpu.SemaphoreType.DMA,
                 pltpu.SemaphoreType.DMA,
                 pltpu.SemaphoreType.DMA((8 * len(pairs),)),
@@ -451,33 +528,16 @@
             name="late_products",
         )(tile_rows, tile_cols, tile_counts, block_order, tiles, follows(split))
 
-    def cell_inverse(gram):
+    def cell_inverse(*grams):
         return note(
             pl.pallas_call(
                 functools.partial(factor_kernel, math.sqrt(cells_all)),
                 out_shape=jax.ShapeDtypeStruct((wide, wide), f32),
-                in_specs=[VMEM],
+                in_specs=[VMEM] * len(grams),
                 out_specs=VMEM,
                 cost_estimate=cost(1.5),
                 name="cell_cholesky",
-            )(follows(gram))
-        )
-
-    def cells(inverse):
-        step = 8
-        return note(
-            pl.pallas_call(
-                cell_kernel,
-                grid=(CELL_BLOCKS // step,),
-                out_shape=jax.ShapeDtypeStruct((CELL_BLOCKS * side, wide), bf16),
-                in_specs=[
-                    pl.BlockSpec((wide, wide), lambda b: (0, 0)),
-                    pl.BlockSpec((step, side, 2 * wide), lambda b: (b, 0, 0)),
-                ],
-                out_specs=pl.BlockSpec((step * side, wide), lambda b: (b, 0)),
-                cost_estimate=cost(1.0),
-                name="cell_factor",
-            )(follows(inverse), split)
+            )(follows(grams[0]), *grams[1:])
         )
 
     begin(0, *early[:8])
@@ -486,9 +546,9 @@
             wait([0])
             send_apart(0) if step < shared else send_both(0)
         wait([0])
-        inverse = cell_inverse(small_sum(0))
-        finals = [finish(0)]
-        cell_factor = cells(inverse)
+        inverse = cell_inverse(*small_terms(0))
+        zs, gene_gram = [None], None
+        zs[0], gene_gram = owners([0], inverse)
     else:
         begin(1, *early[8:])
         wait([0])
@@ -513,27 +573,35 @@
         send_apart(1)
         wait([0, 1, 2])
         send_both(2)
-        inverse = cell_inverse(small_sum(0))
-        finals = [finish(0), finish(1)]
-        cell_factor = cells(inverse)
+        inverse = cell_inverse(*small_terms(0))
+        z_early, gene_gram = owners([0, 1], inverse)
         wait([2])
-        finals.append(finish(2))
-    z, gene_gram = pl.pallas_call(
-        owned_kernel,
-        out_shape=[jax.ShapeDtypeStruct((owned * side, wide), f32), jax.ShapeDtypeStruct((wide, wide), f32)],
-        in_specs=[VMEM] * (1 + len(finals)),
-        out_specs=[VMEM] * 2,
-        name="gene_gram",
-    )(inverse, *finals)
-    for bit in bits:
-        gene_gram = gene_gram + swap(gene_gram, bit)
-    gene_factor = pl.pallas_call(
-        functools.partial(gene_kernel, math.sqrt(genes)),
-        out_shape=jax.ShapeDtypeStruct((owned * side, wide), f32),
-        in_specs=[VMEM] * 2,
-        out_specs=VMEM,
-        name="gene_factor",
-    )(gene_gram, z)
+        z_late, gene_gram = owners([2], inverse, (gene_gram,))
+        zs = [z_early, z_late]
+
+    grams = [gene_gram]
+    for k, bit in enumerate(bits):
+        if k:
+            grams = [combine([([(g, 0) for g in grams], 1)])]
+        grams.append(swap(grams[0], bit))
+    chunks = wide // PANEL
+    gene_factor, cell_factor = pl.pallas_call(
+        functools.partial(last_kernel, math.sqrt(genes), len(grams)),
+        out_shape=[
+            jax.ShapeDtypeStruct((owned * side, wide), f32),
+            jax.ShapeDtypeStruct((CELL_BLOCKS * side, wide), bf16),
+        ],
+        in_specs=[ANY] + [VMEM] * (1 + len(grams) + len(zs)),
+        out_specs=[VMEM, ANY],
+        scratch_shapes=[
+            pltpu.VMEM((CELL_BLOCKS, side, 2 * wide), bf16),
+            pltpu.VMEM((CELL_BLOCKS * side, wide), bf16),
+            pltpu.SemaphoreType.DMA((chunks,)),
+            pltpu.SemaphoreType.DMA((chunks,)),
+        ],
+        compiler_params=ROOMY,
+        name="factors",
+    )(split, inverse, *grams, *zs)
     return (cell_factor, gene_factor)
 
 

time: 168 us -> 160 us (0.952)
  Pallas kernels: 45.9 us -> 39.4 us
  other arithmetic: 2.14 us -> 0 us
    pallas_call x3, Pallas kernels: 17.4 us -> 10.7 us  [the longest x1 8.54 us: on_device(): pl.pallas_call(functools.partial(last_kernel, math.sqrt(genes), len(grams...]
    ppermute x27, waiting for transfers between devices: 28.6 us -> 30.9 us  [swap(): return lax.ppermute(value, 'gy', [(i, i ^ partner) for i in range(ny)])]
    add x6 -> x0, other arithmetic: 2.14 us -> none  [the longest x5 1.51 us: on_device(): gene_gram = gene_gram + swap(gene_gram, bit)]
    ppermute x8, starting transfers between devices: 19.5 us -> 17.4 us  [swap(): return lax.ppermute(value, 'gx', [(i, i ^ partner) for i in range(nx)])]
    ppermute x8, waiting for transfers between devices: 38.1 us -> 36.2 us  [swap(): return lax.ppermute(value, 'gx', [(i, i ^ partner) for i in range(nx)])]
    unnamed x36 -> x40, local copies, waits for them, and re-layouts: 7.09 us -> 7.31 us
  transfers between devices with their start and end apart: 35 -> 35, of which waited for: 18 -> 18; matrix products, arithmetic and copies ran while one was open for 0% -> 0% of each run, Pallas kernels for 12% -> 9%
where the time goes in v3:
time: 160 us; the launch traced here: 159 us
  waiting for transfers between devices  67 us (42%)
  starting transfers between devices  41.9 us (26%)
  Pallas kernels  39.4 us (25%)
  local copies, waits for them, and re-layouts  8.58 us (5%)
  between operations  1.88 us (1%)
    ppermute x8, waiting for transfers between devices, swap(): return lax.ppermute(value, 'gx', [(i, i ^ partner) for i in range(nx)])  36.2 us
    ppermute x27, waiting for transfers between devices, swap(): return lax.ppermute(value, 'gy', [(i, i ^ partner) for i in range(ny)])  30.9 us
    ppermute x27, starting transfers between devices, swap(): return lax.ppermute(value, 'gy', [(i, i ^ partner) for i in range(ny)])  24.5 us
    ppermute x8, starting transfers between devices, swap(): return lax.ppermute(value, 'gx', [(i, i ^ partner) for i in range(nx)])  17.4 us
    pallas_call x1, Pallas kernels, on_device(): pl.pallas_call(functools.partial(first_kernel, nx, ny, early_pairs, owned...  15.7 us
    pallas_call x1, Pallas kernels, on_device(): pl.pallas_call(functools.partial(last_kernel, math.sqrt(genes), len(grams...  8.54 us
    unnamed x40, local copies, waits for them, and re-layouts  7.31 us
    pallas_call x1, Pallas kernels, cell_inverse(): pl.pallas_call(functools.partial(factor_kernel, math.sqrt(cells_all)), ou...  5.78 us
  transfers between devices with their start and end apart: 35, of which 18 were waited for; matrix products, arithmetic and copies ran while one was open for 0% of the time, Pallas kernels for 9%

profile of v3, /device:TPU:0, one launch (start us, length us, event | category | flops | bytes accessed | tf_op | source)
XLA Modules:
  0.0 158.8 jit_solution(14497557809972594372)
XLA Ops:
  1.3 15.7 %tile_products.1 = (f32[16,128,128]{2,1,0:T(8,128)}, f32[16,128,128]{2,1,0:T(8,128)}, f32[16,128,128]{2,1,0:T(8,128)}, f32[16,128,128]{2,1,0:T(8,128)}, f32[16,1...) custom-call(s32[192]{0:T(256)} %rows.3, s32[192]{0:T(256)} %cols.3, ...), custom_call_target="tpu_custom_call" | custom-call | flops 4000000000 | bytes 12000000 | tf_op jit(solution)/shard_map/tile_products/pallas_call | solution.py:357
  17.0 1.0 collective-permute-start.1
  18.1 0.4 collective-permute-start.5
  18.6 0.4 collective-permute-start.11
  19.0 3.1 %collective-permute-done.2.refs_1_ = f32[16,128,128]{2,1,0:T(8,128)S(1)} collective-permute-done((f32[16,128,128]{2,1,0:T(8,128)}, f32[16,128,128]{2,1,0:T(8,128)S(1)}, u32[]{:S(2)}, u32[]{:S(2)}) %collective-permute-start.2) | collective-permute-done | bytes 1048608 | tf_op jit(solution)/shard_map/ppermute | solution.py:353
  22.1 0.4 collective-permute-start.12
  22.5 0.1 collective-permute-start.9
  22.6 1.2 copy-done.4
  24.0 0.9 copy-done.8
  24.9 0.2 copy-done.9
  25.0 0.1 combine.43
  25.2 3.8 %collective-permute-start.7 = (f32[16,128,128]{2,1,0:T(8,128)S(1)}, f32[16,128,128]{2,1,0:T(8,128)S(1)}, u32[]{:S(2)}, u32[]{:S(2)}) collective-permute-start(f32[16,128,128]{2,1,0:T(8,128)S(1)} %combine.43), channel_id=1, source_target_pairs={{0,8},{8,0},{16,24},{24,16},{1,9},{9,1},{17,25},{25,17},{2,10},{10... | collective-permute-start | bytes 3145736 | tf_op jit(solution)/shard_map/ppermute | solution.py:355
  29.0 0.1 combine.41.refs_2_
  29.1 2.5 %collective-permute-start.3 = (f32[17,128,128]{2,1,0:T(8,128)S(1)}, f32[17,128,128]{2,1,0:T(8,128)S(1)}, u32[]{:S(2)}, u32[]{:S(2)}) collective-permute-start(f32[17,128,128]{2,1,0:T(8,128)S(1)} %combine.41.refs_2_), channel_id=1, source_target_pairs={{0,2},{1,3},{2,0},{3,1},{4,6},{5,7},{6,4},{7,5},{8,10},{9,11},{10,... | collective-permute-start | bytes 3342344 | tf_op jit(solution)/shard_map/ppermute | solution.py:353
  31.6 2.5 %collective-permute-start.4 = (f32[16,128,128]{2,1,0:T(8,128)S(1)}, f32[16,128,128]{2,1,0:T(8,128)S(1)}, u32[]{:S(2)}, u32[]{:S(2)}) collective-permute-start(f32[16,128,128]{2,1,0:T(8,128)S(1)} %combine.42), channel_id=1, source_target_pairs={{0,4},{1,5},{2,6},{3,7},{4,0},{5,1},{6,2},{7,3},{8,12},{9,13},{10,... | collective-permute-start | bytes 3145736 | tf_op jit(solution)/shard_map/ppermute | solution.py:353
  34.2 2.8 %copy-done.14 = bf16[192,128,128]{2,1,0:T(8,128)(2,1)S(1)} copy-done((bf16[192,128,128]{2,1,0:T(8,128)(2,1)S(1)}, bf16[192,128,128]{2,1,0:T(8,128)(2,1)}, u32[]{:S(2)}) %copy-start.14) | copy-done | bytes 6291480
  37.0 5.3 %late_products.1 = (f32[8,128,128]{2,1,0:T(8,128)S(1)}, f32[8,128,128]{2,1,0:T(8,128)S(1)}, f32[8,128,128]{2,1,0:T(8,128)S(1)}, f32[8,128,128]{2,1,0:T(8,128)S(1...) custom-call(s32[192]{0:T(256)S(1)} %copy-done.15, ...), custom_call_target="tpu_custom_call" | custom-call | flops 4000000000 | bytes 12000000 | tf_op jit(solution)/shard_map/late_products/pallas_call | solution.py:512
  42.4 1.1 collective-permute-start.14
  43.5 9.1 %collective-permute-done.7.refs_1_.refs_3_ = f32[16,128,128]{2,1,0:T(8,128)S(1)} collective-permute-done((f32[16,128,128]{2,1,0:T(8,128)S(1)}, f32[16,128,128]{2,1,0:T(8,128)S(1)}, u32[]{:S(2)}, u32[]{:S(2)}) %collective-permute-start.7) | collective-permute-done | bytes 1048608 | tf_op jit(solution)/shard_map/ppermute | solution.py:355
  52.6 0.1 combine.48.refs_0_.refs_2_
  52.7 0.1 combine.46.refs_0_
  52.8 4.2 %collective-permute-done.4.refs_1_ = f32[16,128,128]{2,1,0:T(8,128)S(1)} collective-permute-done((f32[16,128,128]{2,1,0:T(8,128)S(1)}, f32[16,128,128]{2,1,0:T(8,128)S(1)}, u32[]{:S(2)}, u32[]{:S(2)}) %collective-permute-start.4) | collective-permute-done | bytes 1048608 | tf_op jit(solution)/shard_map/ppermute | solution.py:353
  57.1 0.9 collective-permute-start.10
  58.1 5.4 %collective-permute-start.13 = (f32[8,128,128]{2,1,0:T(8,128)S(1)}, f32[8,128,128]{2,1,0:T(8,128)S(1)}, u32[]{:S(2)}, u32[]{:S(2)}) collective-permute-start(f32[8,128,128]{2,1,0:T(8,128)S(1)} %combine.49), channel_id=1, source_target_pairs={{0,16},{8,24},{16,0},{24,8},{1,17},{9,25},{17,1},{25,9},{2,18},{10... | collective-permute-start | bytes 1572872 | tf_op jit(solution)/shard_map/ppermute | solution.py:355
  63.7 2.7 %collective-permute-start.8 = (f32[9,128,128]{2,1,0:T(8,128)S(1)}, f32[9,128,128]{2,1,0:T(8,128)S(1)}, u32[]{:S(2)}, u32[]{:S(2)}) collective-permute-start(f32[9,128,128]{2,1,0:T(8,128)S(1)} %combine.45.refs_4_), channel_id=1, source_target_pairs={{0,4},{1,5},{2,6},{3,7},{4,0},{5,1},{6,2},{7,3},{8,12},{9,13},{10,... | collective-permute-start | bytes 1769480 | tf_op jit(solution)/shard_map/ppermute | solution.py:353
  66.7 0.7 collective-permute-start.16
  67.3 4.7 %collective-permute-done.10.refs_3_ = f32[8,128,128]{2,1,0:T(8,128)S(1)} collective-permute-done((f32[8,128,128]{2,1,0:T(8,128)S(1)}, f32[8,128,128]{2,1,0:T(8,128)S(1)}, u32[]{:S(2)}, u32[]{:S(2)}) %collective-permute-start.10) | collective-permute-done | bytes 524320 | tf_op jit(solution)/shard_map/ppermute | solution.py:353
  72.1 13.5 %collective-permute-done.13.refs_1_ = f32[8,128,128]{2,1,0:T(8,128)S(1)} collective-permute-done((f32[8,128,128]{2,1,0:T(8,128)S(1)}, f32[8,128,128]{2,1,0:T(8,128)S(1)}, u32[]{:S(2)}, u32[]{:S(2)}) %collective-permute-start.13) | collective-permute-done | bytes 524320 | tf_op jit(solution)/shard_map/ppermute | solution.py:355
  85.7 3.9 %collective-permute-done.17.refs_1_ = f32[8,128,128]{2,1,0:T(8,128)S(1)} collective-permute-done((f32[8,128,128]{2,1,0:T(8,128)S(1)}, f32[8,128,128]{2,1,0:T(8,128)S(1)}, u32[]{:S(2)}, u32[]{:S(2)}) %collective-permute-start.17) | collective-permute-done | bytes 524320 | tf_op jit(solution)/shard_map/ppermute | solution.py:353
  89.7 1.2 collective-permute-start.18
  91.0 0.7 collective-permute-start.24
  91.7 1.8 %collective-permute-start.22 = (f32[4,128,128]{2,1,0:T(8,128)S(1)}, f32[4,128,128]{2,1,0:T(8,128)S(1)}, u32[]{:S(2)}, u32[]{:S(2)}) collective-permute-start(f32[4,128,128]{2,1,0:T(8,128)S(1)} %combine.59), channel_id=1, source_target_pairs={{0,4},{1,5},{2,6},{3,7},{4,0},{5,1},{6,2},{7,3},{8,12},{9,13},{10,... | collective-permute-start | bytes 786440 | tf_op jit(solution)/shard_map/ppermute | solution.py:353
  93.6 1.5 collective-permute-start.19
  95.1 0.3 collective-permute-start.20
  95.5 4.5 %collective-permute-done.19.refs_1_ = f32[2,128,128]{2,1,0:T(8,128)S(1)} collective-permute-done((f32[2,128,128]{2,1,0:T(8,128)S(1)}, f32[2,128,128]{2,1,0:T(8,128)S(1)}, u32[]{:S(2)}, u32[]{:S(2)}) %collective-permute-start.19) | collective-permute-done | bytes 131104 | tf_op jit(solution)/shard_map/ppermute | solution.py:353
  99.9 0.4 collective-permute-done.20.refs_1_
  100.3 2.4 %collective-permute-done.18.refs_1_.refs_3_.refs_5_ = f32[9,128,128]{2,1,0:T(8,128)S(1)} collective-permute-done((f32[9,128,128]{2,1,0:T(8,128)S(1)}, f32[9,128,128]{2,1,0:T(8,128)S(1)}, u32[]{:S(2)}, u32[]{:S(2)}) %collective-permute-start.18) | collective-permute-done | bytes 589856 | tf_op jit(solution)/shard_map/ppermute | solution.py:355
  102.8 0.9 collective-permute-start.25
  103.8 1.8 %collective-permute-start.28 = (f32[4,128,128]{2,1,0:T(8,128)S(1)}, f32[4,128,128]{2,1,0:T(8,128)S(1)}, u32[]{:S(2)}, u32[]{:S(2)}) collective-permute-start(f32[4,128,128]{2,1,0:T(8,128)S(1)} %combine.70), channel_id=1, source_target_pairs={{0,8},{8,0},{16,24},{24,16},{1,9},{9,1},{17,25},{25,17},{2,10},{10... | collective-permute-start | bytes 786440 | tf_op jit(solution)/shard_map/ppermute | solution.py:355
  105.7 2.7 %collective-permute-start.26 = (f32[1,128,128]{2,1,0:T(8,128)S(1)}, f32[1,128,128]{2,1,0:T(8,128)S(1)}, u32[]{:S(2)}, u32[]{:S(2)}) collective-permute-start(f32[1,128,128]{2,1,0:T(8,128)S(1)} %combine.67), channel_id=1, source_target_pairs={{0,4},{1,5},{2,6},{3,7},{4,0},{5,1},{6,2},{7,3},{8,12},{9,13},{10,... | collective-permute-start | bytes 196616 | tf_op jit(solution)/shard_map/ppermute | solution.py:353
  108.4 0.7 collective-permute-start.27
  109.1 0.6 slice.8.refs_0_
  109.8 0.8 collective-permute-done.26.refs_5_
  110.6 2.1 %collective-permute-done.27.refs_7_ = f32[1,128,128]{2,1,0:T(8,128)S(1)} collective-permute-done((f32[1,128,128]{2,1,0:T(8,128)S(1)}, f32[1,128,128]{2,1,0:T(8,128)S(1)}, u32[]{:S(2)}, u32[]{:S(2)}) %collective-permute-start.27) | collective-permute-done | bytes 65568 | tf_op jit(solution)/shard_map/ppermute | solution.py:353
  112.7 1.6 %collective-permute-done.28.refs_1_.refs_3_ = f32[4,128,128]{2,1,0:T(8,128)S(1)} collective-permute-done((f32[4,128,128]{2,1,0:T(8,128)S(1)}, f32[4,128,128]{2,1,0:T(8,128)S(1)}, u32[]{:S(2)}, u32[]{:S(2)}) %collective-permute-start.28) | collective-permute-done | bytes 262176 | tf_op jit(solution)/shard_map/ppermute | solution.py:355
  114.4 2.9 %collective-permute-done.25.refs_1_.refs_3_ = f32[5,128,128]{2,1,0:T(8,128)S(1)} collective-permute-done((f32[5,128,128]{2,1,0:T(8,128)S(1)}, f32[5,128,128]{2,1,0:T(8,128)S(1)}, u32[]{:S(2)}, u32[]{:S(2)}) %collective-permute-start.25) | collective-permute-done | bytes 327712 | tf_op jit(solution)/shard_map/ppermute | solution.py:355
  117.3 0.6 slice.7.refs_1_
  117.9 0.4 collective-permute-start.29
  118.3 5.8 %cell_cholesky.1.inverse = f32[128,128]{1,0:T(8,128)} custom-call(f32[1,128,128]{2,1,0:T(8,128)} %slice.8.refs_0_, f32[1,128,128]{2,1,0:T(8,128)} %slice.7.refs_1_), custom_call_target="tpu_custom_call" | custom-call | flops 1500000000 | bytes 4500000 | tf_op jit(solution)/shard_map/cell_cholesky/pallas_call | solution.py:533
  124.1 0.8 copy-done.13
  125.0 1.5 owned_gram.2
  126.4 0.7 copy-done.10
  127.2 0.7 owned_gram.3
  128.0 1.2 collective-permute-done.30.refs_1_
  129.2 0.6 collective-permute-start.31
  129.9 3.7 %collective-permute-done.31.refs_1_ = f32[1,128,128]{2,1,0:T(8,128)S(1)} collective-permute-done((f32[1,128,128]{2,1,0:T(8,128)S(1)}, f32[1,128,128]{2,1,0:T(8,128)S(1)}, u32[]{:S(2)}, u32[]{:S(2)}) %collective-permute-start.31) | collective-permute-done | bytes 65568 | tf_op jit(solution)/shard_map/ppermute | solution.py:353
  133.6 3.0 %collective-permute-start.32 = (f32[1,128,128]{2,1,0:T(8,128)S(1)}, f32[1,128,128]{2,1,0:T(8,128)S(1)}, u32[]{:S(2)}, u32[]{:S(2)}) collective-permute-start(f32[1,128,128]{2,1,0:T(8,128)S(1)} %combine.77.refs_0_), channel_id=1, source_target_pairs={{0,4},{1,5},{2,6},{3,7},{4,0},{5,1},{6,2},{7,3},{8,12},{9,13},{10,... | collective-permute-start | bytes 196616 | tf_op jit(solution)/shard_map/ppermute | solution.py:353
  136.6 2.2 %collective-permute-done.32.refs_1_ = f32[1,128,128]{2,1,0:T(8,128)S(1)} collective-permute-done((f32[1,128,128]{2,1,0:T(8,128)S(1)}, f32[1,128,128]{2,1,0:T(8,128)S(1)}, u32[]{:S(2)}, u32[]{:S(2)}) %collective-permute-start.32) | collective-permute-done | bytes 65568 | tf_op jit(solution)/shard_map/ppermute | solution.py:353
  138.9 3.1 %collective-permute-start.33 = (f32[1,128,128]{2,1,0:T(8,128)S(1)}, f32[1,128,128]{2,1,0:T(8,128)S(1)}, u32[]{:S(2)}, u32[]{:S(2)}) collective-permute-start(f32[1,128,128]{2,1,0:T(8,128)S(1)} %combine.78.refs_0_), channel_id=1, source_target_pairs={{0,8},{8,0},{16,24},{24,16},{1,9},{9,1},{17,25},{25,17},{2,10},{10... | collective-permute-start | bytes 196616 | tf_op jit(solution)/shard_map/ppermute | solution.py:355
  141.9 2.2 %collective-permute-done.33.refs_1_ = f32[1,128,128]{2,1,0:T(8,128)S(1)} collective-permute-done((f32[1,128,128]{2,1,0:T(8,128)S(1)}, f32[1,128,128]{2,1,0:T(8,128)S(1)}, u32[]{:S(2)}, u32[]{:S(2)}) %collective-permute-start.33) | collective-permute-done | bytes 65568 | tf_op jit(solution)/shard_map/ppermute | solution.py:355
  144.2 0.9 collective-permute-start.34
  145.1 4.3 %collective-permute-done.34.refs_1_ = f32[1,128,128]{2,1,0:T(8,128)S(1)} collective-permute-done((f32[1,128,128]{2,1,0:T(8,128)S(1)}, f32[1,128,128]{2,1,0:T(8,128)S(1)}, u32[]{:S(2)}, u32[]{:S(2)}) %collective-permute-start.34) | collective-permute-done | bytes 65568 | tf_op jit(solution)/shard_map/ppermute | solution.py:355
  149.4 0.6 copy-done.18
  150.1 8.5 %factors.1 = (f32[1024,128]{1,0:T(8,128)}, bf16[8192,128]{1,0:T(8,128)(2,1)}) custom-call(bf16[64,128,256]{2,1,0:T(8,128)(2,1)} %get-tuple-element.74.split, f32[128,128]{1,0:T(8,128)} %cell_cholesky.1.inverse, f32[1,128,128]{2,1,0:T(8,128)} %copy-done.11, f32[1,128,128]{2,1,0:T(8,128)} %copy-done.18, f32[768,128]{1,0:T(8,128)} %copy-done.10, ...), custom_call_target="tpu_custom_call" | custom-call | tf_op jit(solution)/shard_map/factors/pallas_call | solution.py:588
  (94 shorter events, 1.8 us)
Async XLA Ops:
  17.0 5.5 %collective-permute-start.1 = (f32[17,128,128]{2,1,0:T(8,128)}, f32[17,128,128]{2,1,0:T(8,128)S(1)}, u32[]{:S(2)}, u32[]{:S(2)}) collective-permute-start(f32[17,128,128]{2,1,0:T(8,128)} %get-tuple-element.63.refs_2_), channel_id=1, source_target_pairs={{0,1},{1,0},{2,3},{3,2},{4,5},{5,4},{6,7},{7,6},{8,9},{9,8},{10,11... | collective-permute-start | bytes 3342344 | tf_op jit(solution)/shard_map/ppermute | solution.py:353
  18.0 4.1 %collective-permute-start.2 = (f32[16,128,128]{2,1,0:T(8,128)}, f32[16,128,128]{2,1,0:T(8,128)S(1)}, u32[]{:S(2)}, u32[]{:S(2)}) collective-permute-start(f32[16,128,128]{2,1,0:T(8,128)} %get-tuple-element.64), channel_id=1, source_target_pairs={{0,1},{1,0},{2,3},{3,2},{4,5},{5,4},{6,7},{7,6},{8,9},{9,8},{10,11... | collective-permute-start | bytes 3145736 | tf_op jit(solution)/shard_map/ppermute | solution.py:353
  18.1 5.9 %collective-permute-start.5 = (f32[8,128,128]{2,1,0:T(8,128)}, f32[8,128,128]{2,1,0:T(8,128)S(1)}, u32[]{:S(2)}, u32[]{:S(2)}) collective-permute-start(f32[8,128,128]{2,1,0:T(8,128)} %get-tuple-element.69), channel_id=1, source_target_pairs={{0,1},{1,0},{2,3},{3,2},{4,5},{5,4},{6,7},{7,6},{8,9},{9,8},{10,11... | collective-permute-start | bytes 1572872 | tf_op jit(solution)/shard_map/ppermute | solution.py:353
  18.5 5.5 %collective-permute-start.6 = (f32[8,128,128]{2,1,0:T(8,128)}, f32[8,128,128]{2,1,0:T(8,128)S(1)}, u32[]{:S(2)}, u32[]{:S(2)}) collective-permute-start(f32[8,128,128]{2,1,0:T(8,128)} %get-tuple-element.70), channel_id=1, source_target_pairs={{0,1},{1,0},{2,3},{3,2},{4,5},{5,4},{6,7},{7,6},{8,9},{9,8},{10,11... | collective-permute-start | bytes 1572872 | tf_op jit(solution)/shard_map/ppermute | solution.py:353
  18.6 13.0 %collective-permute-start.11 = (f32[8,128,128]{2,1,0:T(8,128)}, f32[8,128,128]{2,1,0:T(8,128)S(1)}, u32[]{:S(2)}, u32[]{:S(2)}) collective-permute-start(f32[8,128,128]{2,1,0:T(8,128)} %get-tuple-element.81), channel_id=1, source_target_pairs={{0,1},{1,0},{2,3},{3,2},{4,5},{5,4},{6,7},{7,6},{8,9},{9,8},{10,11... | collective-permute-start | bytes 1572872 | tf_op jit(solution)/shard_map/ppermute | solution.py:353
  22.1 12.1 %collective-permute-start.12 = (f32[8,128,128]{2,1,0:T(8,128)}, f32[8,128,128]{2,1,0:T(8,128)S(1)}, u32[]{:S(2)}, u32[]{:S(2)}) collective-permute-start(f32[8,128,128]{2,1,0:T(8,128)} %get-tuple-element.83), channel_id=1, source_target_pairs={{0,1},{1,0},{2,3},{3,2},{4,5},{5,4},{6,7},{7,6},{8,9},{9,8},{10,11... | collective-permute-start | bytes 1572872 | tf_op jit(solution)/shard_map/ppermute | solution.py:353
  22.5 19.9 %collective-permute-start.9 = (f32[16,128,128]{2,1,0:T(8,128)}, f32[16,128,128]{2,1,0:T(8,128)S(1)}, u32[]{:S(2)}, u32[]{:S(2)}) collective-permute-start(f32[16,128,128]{2,1,0:T(8,128)} %get-tuple-element.78), channel_id=1, source_target_pairs={{0,1},{1,0},{2,3},{3,2},{4,5},{5,4},{6,7},{7,6},{8,9},{9,8},{10,11... | collective-permute-start | bytes 3145736 | tf_op jit(solution)/shard_map/ppermute | solution.py:353
  22.6 1.2 copy-start.4
  23.8 1.0 copy-start.8
  23.8 1.2 copy-start.9
  23.9 5.0 %copy-start.1 = (f32[17,128,128]{2,1,0:T(8,128)S(1)}, f32[17,128,128]{2,1,0:T(8,128)}, u32[]{:S(2)}) copy-start(f32[17,128,128]{2,1,0:T(8,128)} %get-tuple-element.63.refs_2_) | copy-start | bytes 3342340
  23.9 5.0 %copy-start.5 = (f32[16,128,128]{2,1,0:T(8,128)S(1)}, f32[16,128,128]{2,1,0:T(8,128)}, u32[]{:S(2)}) copy-start(f32[16,128,128]{2,1,0:T(8,128)} %get-tuple-element.62.refs_0_) | copy-start | bytes 3145732
  25.2 27.4 %collective-permute-start.7 = (f32[16,128,128]{2,1,0:T(8,128)S(1)}, f32[16,128,128]{2,1,0:T(8,128)S(1)}, u32[]{:S(2)}, u32[]{:S(2)}) collective-permute-start(f32[16,128,128]{2,1,0:T(8,128)S(1)} %combine.43), channel_id=1, source_target_pairs={{0,8},{8,0},{16,24},{24,16},{1,9},{9,1},{17,25},{25,17},{2,10},{10... | collective-permute-start | bytes 3145736 | tf_op jit(solution)/shard_map/ppermute | solution.py:355
  28.9 5.3 %copy-start.19 = (f32[16,128,128]{2,1,0:T(8,128)S(1)}, f32[16,128,128]{2,1,0:T(8,128)}, u32[]{:S(2)}) copy-start(f32[16,128,128]{2,1,0:T(8,128)} %get-tuple-element.61) | copy-start | bytes 3145732
  28.9 5.3 %copy-start = (bf16[64,128,256]{2,1,0:T(8,128)(2,1)S(1)}, bf16[64,128,256]{2,1,0:T(8,128)(2,1)}, u32[]{:S(2)}) copy-start(bf16[64,128,256]{2,1,0:T(8,128)(2,1)} %get-tuple-element.74.split) | copy-start | bytes 12582916
  28.9 5.3 %copy-start.15 = (s32[192]{0:T(256)S(1)}, s32[192]{0:T(256)}, u32[]{:S(2)}) copy-start(s32[192]{0:T(256)} %rows.3) | copy-start | bytes 2308
  28.9 5.3 %copy-start.16 = (s32[192]{0:T(256)S(1)}, s32[192]{0:T(256)}, u32[]{:S(2)}) copy-start(s32[192]{0:T(256)} %cols.3) | copy-start | bytes 2308
  28.9 5.3 %copy-start.17 = (s32[256]{0:T(256)S(1)}, s32[256]{0:T(256)}, u32[]{:S(2)}) copy-start(s32[256]{0:T(256)} %order.3) | copy-start | bytes 3076
  29.1 28.0 %collective-permute-start.3 = (f32[17,128,128]{2,1,0:T(8,128)S(1)}, f32[17,128,128]{2,1,0:T(8,128)S(1)}, u32[]{:S(2)}, u32[]{:S(2)}) collective-permute-start(f32[17,128,128]{2,1,0:T(8,128)S(1)} %combine.41.refs_2_), channel_id=1, source_target_pairs={{0,2},{1,3},{2,0},{3,1},{4,6},{5,7},{6,4},{7,5},{8,10},{9,11},{10,... | collective-permute-start | bytes 3342344 | tf_op jit(solution)/shard_map/ppermute | solution.py:353
  31.6 25.4 %collective-permute-start.4 = (f32[16,128,128]{2,1,0:T(8,128)S(1)}, f32[16,128,128]{2,1,0:T(8,128)S(1)}, u32[]{:S(2)}, u32[]{:S(2)}) collective-permute-start(f32[16,128,128]{2,1,0:T(8,128)S(1)} %combine.42), channel_id=1, source_target_pairs={{0,4},{1,5},{2,6},{3,7},{4,0},{5,1},{6,2},{7,3},{8,12},{9,13},{10,... | collective-permute-start | bytes 3145736 | tf_op jit(solution)/shard_map/ppermute | solution.py:353
  34.2 29.4 %collective-permute-start = (f32[16,128,128]{2,1,0:T(8,128)S(1)}, f32[16,128,128]{2,1,0:T(8,128)S(1)}, u32[]{:S(2)}, u32[]{:S(2)}) collective-permute-start(f32[16,128,128]{2,1,0:T(8,128)S(1)} %copy-done.19), channel_id=1, source_target_pairs={{0,1},{1,0},{2,3},{3,2},{4,5},{5,4},{6,7},{7,6},{8,9},{9,8},{10,11... | collective-permute-start | bytes 3145736 | tf_op jit(solution)/shard_map/ppermute | solution.py:353
  34.2 2.8 %copy-start.14 = (bf16[192,128,128]{2,1,0:T(8,128)(2,1)S(1)}, bf16[192,128,128]{2,1,0:T(8,128)(2,1)}, u32[]{:S(2)}) copy-start(bf16[192,128,128]{2,1,0:T(8,128)(2,1)} %tiles.3) | copy-start | bytes 18874372
  37.0 15.6 %copy-start.6 = (f32[8,128,128]{2,1,0:T(8,128)S(1)}, f32[8,128,128]{2,1,0:T(8,128)}, u32[]{:S(2)}) copy-start(f32[8,128,128]{2,1,0:T(8,128)} %get-tuple-element.80.refs_0_) | copy-start | bytes 1572868
  37.0 15.6 %copy-start.7 = (f32[8,128,128]{2,1,0:T(8,128)S(1)}, f32[8,128,128]{2,1,0:T(8,128)}, u32[]{:S(2)}) copy-start(f32[8,128,128]{2,1,0:T(8,128)} %get-tuple-element.82.refs_2_) | copy-start | bytes 1572868
  42.3 10.4 %copy-start.3 = (f32[16,128,128]{2,1,0:T(8,128)S(1)}, f32[16,128,128]{2,1,0:T(8,128)}, u32[]{:S(2)}) copy-start(f32[16,128,128]{2,1,0:T(8,128)} %get-tuple-element.77.refs_0_) | copy-start | bytes 3145732
  42.4 24.1 %collective-permute-start.14 = (f32[8,128,128]{2,1,0:T(8,128)S(1)}, f32[8,128,128]{2,1,0:T(8,128)S(1)}, u32[]{:S(2)}, u32[]{:S(2)}) collective-permute-start(f32[8,128,128]{2,1,0:T(8,128)S(1)} %get-tuple-element.86), channel_id=1, source_target_pairs={{0,1},{1,0},{2,3},{3,2},{4,5},{5,4},{6,7},{7,6},{8,9},{9,8},{10,11... | collective-permute-start | bytes 1572872 | tf_op jit(solution)/shard_map/ppermute | solution.py:353
  52.6 13.8 %collective-permute-start.15 = (f32[8,128,128]{2,1,0:T(8,128)S(1)}, f32[8,128,128]{2,1,0:T(8,128)S(1)}, u32[]{:S(2)}, u32[]{:S(2)}) collective-permute-start(f32[8,128,128]{2,1,0:T(8,128)S(1)} %get-tuple-element.87), channel_id=1, source_target_pairs={{0,1},{1,0},{2,3},{3,2},{4,5},{5,4},{6,7},{7,6},{8,9},{9,8},{10,11... | collective-permute-start | bytes 1572872 | tf_op jit(solution)/shard_map/ppermute | solution.py:353
  57.1 6.4 %copy-start.2 = (f32[16,128,128]{2,1,0:T(8,128)S(1)}, f32[16,128,128]{2,1,0:T(8,128)}, u32[]{:S(2)}) copy-start(f32[16,128,128]{2,1,0:T(8,128)} %get-tuple-element.60.refs_0_) | copy-start | bytes 3145732
  57.1 14.9 %collective-permute-start.10 = (f32[8,128,128]{2,1,0:T(8,128)S(1)}, f32[8,128,128]{2,1,0:T(8,128)S(1)}, u32[]{:S(2)}, u32[]{:S(2)}) collective-permute-start(f32[8,128,128]{2,1,0:T(8,128)S(1)} %combine.47), channel_id=1, source_target_pairs={{0,2},{1,3},{2,0},{3,1},{4,6},{5,7},{6,4},{7,5},{8,10},{9,11},{10,... | collective-permute-start | bytes 1572872 | tf_op jit(solution)/shard_map/ppermute | solution.py:353
  58.1 27.4 %collective-permute-start.13 = (f32[8,128,128]{2,1,0:T(8,128)S(1)}, f32[8,128,128]{2,1,0:T(8,128)S(1)}, u32[]{:S(2)}, u32[]{:S(2)}) collective-permute-start(f32[8,128,128]{2,1,0:T(8,128)S(1)} %combine.49), channel_id=1, source_target_pairs={{0,16},{8,24},{16,0},{24,8},{1,17},{9,25},{17,1},{25,9},{2,18},{10... | collective-permute-start | bytes 1572872 | tf_op jit(solution)/shard_map/ppermute | solution.py:355
  63.7 25.9 %collective-permute-start.8 = (f32[9,128,128]{2,1,0:T(8,128)S(1)}, f32[9,128,128]{2,1,0:T(8,128)S(1)}, u32[]{:S(2)}, u32[]{:S(2)}) collective-permute-start(f32[9,128,128]{2,1,0:T(8,128)S(1)} %combine.45.refs_4_), channel_id=1, source_target_pairs={{0,4},{1,5},{2,6},{3,7},{4,0},{5,1},{6,2},{7,3},{8,12},{9,13},{10,... | collective-permute-start | bytes 1769480 | tf_op jit(solution)/shard_map/ppermute | solution.py:353
  66.5 23.1 %collective-permute-start.17 = (f32[8,128,128]{2,1,0:T(8,128)S(1)}, f32[8,128,128]{2,1,0:T(8,128)S(1)}, u32[]{:S(2)}, u32[]{:S(2)}) collective-permute-start(f32[8,128,128]{2,1,0:T(8,128)S(1)} %combine.51), channel_id=1, source_target_pairs={{0,4},{1,5},{2,6},{3,7},{4,0},{5,1},{6,2},{7,3},{8,12},{9,13},{10,... | collective-permute-start | bytes 1572872 | tf_op jit(solution)/shard_map/ppermute | solution.py:353
  66.7 22.9 %collective-permute-start.16 = (f32[8,128,128]{2,1,0:T(8,128)S(1)}, f32[8,128,128]{2,1,0:T(8,128)S(1)}, u32[]{:S(2)}, u32[]{:S(2)}) collective-permute-start(f32[8,128,128]{2,1,0:T(8,128)S(1)} %combine.50), channel_id=1, source_target_pairs={{0,2},{1,3},{2,0},{3,1},{4,6},{5,7},{6,4},{7,5},{8,10},{9,11},{10,... | collective-permute-start | bytes 1572872 | tf_op jit(solution)/shard_map/ppermute | solution.py:353
  72.1 18.7 %collective-permute-start.21 = (f32[8,128,128]{2,1,0:T(8,128)S(1)}, f32[8,128,128]{2,1,0:T(8,128)S(1)}, u32[]{:S(2)}, u32[]{:S(2)}) collective-permute-start(f32[8,128,128]{2,1,0:T(8,128)S(1)} %get-tuple-element.94), channel_id=1, source_target_pairs={{0,1},{1,0},{2,3},{3,2},{4,5},{5,4},{6,7},{7,6},{8,9},{9,8},{10,11... | collective-permute-start | bytes 1572872 | tf_op jit(solution)/shard_map/ppermute | solution.py:353
  85.6 5.3 %collective-permute-start.23 = (f32[8,128,128]{2,1,0:T(8,128)S(1)}, f32[8,128,128]{2,1,0:T(8,128)S(1)}, u32[]{:S(2)}, u32[]{:S(2)}) collective-permute-start(f32[8,128,128]{2,1,0:T(8,128)S(1)} %get-tuple-element.97), channel_id=1, source_target_pairs={{0,1},{1,0},{2,3},{3,2},{4,5},{5,4},{6,7},{7,6},{8,9},{9,8},{10,11... | collective-permute-start | bytes 1572872 | tf_op jit(solution)/shard_map/ppermute | solution.py:353
  89.7 13.1 %collective-permute-start.18 = (f32[9,128,128]{2,1,0:T(8,128)S(1)}, f32[9,128,128]{2,1,0:T(8,128)S(1)}, u32[]{:S(2)}, u32[]{:S(2)}) collective-permute-start(f32[9,128,128]{2,1,0:T(8,128)S(1)} %combine.54.refs_4_), channel_id=1, source_target_pairs={{0,8},{8,0},{16,24},{24,16},{1,9},{9,1},{17,25},{25,17},{2,10},{10... | collective-permute-start | bytes 1769480 | tf_op jit(solution)/shard_map/ppermute | solution.py:355
  91.0 9.3 %collective-permute-start.24 = (f32[4,128,128]{2,1,0:T(8,128)S(1)}, f32[4,128,128]{2,1,0:T(8,128)S(1)}, u32[]{:S(2)}, u32[]{:S(2)}) collective-permute-start(f32[4,128,128]{2,1,0:T(8,128)S(1)} %combine.61), channel_id=1, source_target_pairs={{0,2},{1,3},{2,0},{3,1},{4,6},{5,7},{6,4},{7,5},{8,10},{9,11},{10,... | collective-permute-start | bytes 786440 | tf_op jit(solution)/shard_map/ppermute | solution.py:353
  91.7 8.6 %collective-permute-start.22 = (f32[4,128,128]{2,1,0:T(8,128)S(1)}, f32[4,128,128]{2,1,0:T(8,128)S(1)}, u32[]{:S(2)}, u32[]{:S(2)}) collective-permute-start(f32[4,128,128]{2,1,0:T(8,128)S(1)} %combine.59), channel_id=1, source_target_pairs={{0,4},{1,5},{2,6},{3,7},{4,0},{5,1},{6,2},{7,3},{8,12},{9,13},{10,... | collective-permute-start | bytes 786440 | tf_op jit(solution)/shard_map/ppermute | solution.py:353
  93.6 6.3 %collective-permute-start.19 = (f32[2,128,128]{2,1,0:T(8,128)S(1)}, f32[2,128,128]{2,1,0:T(8,128)S(1)}, u32[]{:S(2)}, u32[]{:S(2)}) collective-permute-start(f32[2,128,128]{2,1,0:T(8,128)S(1)} %combine.56), channel_id=1, source_target_pairs={{0,2},{1,3},{2,0},{3,1},{4,6},{5,7},{6,4},{7,5},{8,10},{9,11},{10,... | collective-permute-start | bytes 393224 | tf_op jit(solution)/shard_map/ppermute | solution.py:353
  95.1 5.2 %collective-permute-start.20 = (f32[2,128,128]{2,1,0:T(8,128)S(1)}, f32[2,128,128]{2,1,0:T(8,128)S(1)}, u32[]{:S(2)}, u32[]{:S(2)}) collective-permute-start(f32[2,128,128]{2,1,0:T(8,128)S(1)} %combine.57), channel_id=1, source_target_pairs={{0,4},{1,5},{2,6},{3,7},{4,0},{5,1},{6,2},{7,3},{8,12},{9,13},{10,... | collective-permute-start | bytes 393224 | tf_op jit(solution)/shard_map/ppermute | solution.py:353
  102.8 14.5 %collective-permute-start.25 = (f32[5,128,128]{2,1,0:T(8,128)S(1)}, f32[5,128,128]{2,1,0:T(8,128)S(1)}, u32[]{:S(2)}, u32[]{:S(2)}) collective-permute-start(f32[5,128,128]{2,1,0:T(8,128)S(1)} %combine.62), channel_id=1, source_target_pairs={{0,16},{8,24},{16,0},{24,8},{1,17},{9,25},{17,1},{25,9},{2,18},{10... | collective-permute-start | bytes 983048 | tf_op jit(solution)/shard_map/ppermute | solution.py:355
  103.8 10.5 %collective-permute-start.28 = (f32[4,128,128]{2,1,0:T(8,128)S(1)}, f32[4,128,128]{2,1,0:T(8,128)S(1)}, u32[]{:S(2)}, u32[]{:S(2)}) collective-permute-start(f32[4,128,128]{2,1,0:T(8,128)S(1)} %combine.70), channel_id=1, source_target_pairs={{0,8},{8,0},{16,24},{24,16},{1,9},{9,1},{17,25},{25,17},{2,10},{10... | collective-permute-start | bytes 786440 | tf_op jit(solution)/shard_map/ppermute | solution.py:355
  105.7 4.9 %collective-permute-start.26 = (f32[1,128,128]{2,1,0:T(8,128)S(1)}, f32[1,128,128]{2,1,0:T(8,128)S(1)}, u32[]{:S(2)}, u32[]{:S(2)}) collective-permute-start(f32[1,128,128]{2,1,0:T(8,128)S(1)} %combine.67), channel_id=1, source_target_pairs={{0,4},{1,5},{2,6},{3,7},{4,0},{5,1},{6,2},{7,3},{8,12},{9,13},{10,... | collective-permute-start | bytes 196616 | tf_op jit(solution)/shard_map/ppermute | solution.py:353
  108.4 4.3 %collective-permute-start.27 = (f32[1,128,128]{2,1,0:T(8,128)S(1)}, f32[1,128,128]{2,1,0:T(8,128)S(1)}, u32[]{:S(2)}, u32[]{:S(2)}) collective-permute-start(f32[1,128,128]{2,1,0:T(8,128)S(1)} %combine.69), channel_id=1, source_target_pairs={{0,2},{1,3},{2,0},{3,1},{4,6},{5,7},{6,4},{7,5},{8,10},{9,11},{10,... | collective-permute-start | bytes 196616 | tf_op jit(solution)/shard_map/ppermute | solution.py:353
  117.9 9.3 %collective-permute-start.29 = (f32[2,128,128]{2,1,0:T(8,128)S(1)}, f32[2,128,128]{2,1,0:T(8,128)S(1)}, u32[]{:S(2)}, u32[]{:S(2)}) collective-permute-start(f32[2,128,128]{2,1,0:T(8,128)S(1)} %combine.71), channel_id=1, source_target_pairs={{0,16},{8,24},{16,0},{24,8},{1,17},{9,25},{17,1},{25,9},{2,18},{10... | collective-permute-start | bytes 393224 | tf_op jit(solution)/shard_map/ppermute | solution.py:355
  124.1 0.8 copy-start.13
  126.4 0.8 copy-start.10
  127.9 21.5 %copy-start.12 = (f32[256,128]{1,0:T(8,128)}, f32[256,128]{1,0:T(8,128)S(1)}, u32[]{:S(2)}) copy-start(f32[256,128]{1,0:T(8,128)S(1)} %get-tuple-element.113.refs_3_) | copy-start | bytes 393220
  127.9 1.3 collective-permute-start.30
  129.2 4.3 %collective-permute-start.31 = (f32[1,128,128]{2,1,0:T(8,128)S(1)}, f32[1,128,128]{2,1,0:T(8,128)S(1)}, u32[]{:S(2)}, u32[]{:S(2)}) collective-permute-start(f32[1,128,128]{2,1,0:T(8,128)S(1)} %combine.76.refs_0_), channel_id=1, source_target_pairs={{0,2},{1,3},{2,0},{3,1},{4,6},{5,7},{6,4},{7,5},{8,10},{9,11},{10,... | collective-permute-start | bytes 196616 | tf_op jit(solution)/shard_map/ppermute | solution.py:353
  133.6 5.3 %collective-permute-start.32 = (f32[1,128,128]{2,1,0:T(8,128)S(1)}, f32[1,128,128]{2,1,0:T(8,128)S(1)}, u32[]{:S(2)}, u32[]{:S(2)}) collective-permute-start(f32[1,128,128]{2,1,0:T(8,128)S(1)} %combine.77.refs_0_), channel_id=1, source_target_pairs={{0,4},{1,5},{2,6},{3,7},{4,0},{5,1},{6,2},{7,3},{8,12},{9,13},{10,... | collective-permute-start | bytes 196616 | tf_op jit(solution)/shard_map/ppermute | solution.py:353
  138.9 5.3 %collective-permute-start.33 = (f32[1,128,128]{2,1,0:T(8,128)S(1)}, f32[1,128,128]{2,1,0:T(8,128)S(1)}, u32[]{:S(2)}, u32[]{:S(2)}) collective-permute-start(f32[1,128,128]{2,1,0:T(8,128)S(1)} %combine.78.refs_0_), channel_id=1, source_target_pairs={{0,8},{8,0},{16,24},{24,16},{1,9},{9,1},{17,25},{25,17},{2,10},{10... | collective-permute-start | bytes 196616 | tf_op jit(solution)/shard_map/ppermute | solution.py:355
  144.2 5.2 %copy-start.11 = (f32[1,128,128]{2,1,0:T(8,128)}, f32[1,128,128]{2,1,0:T(8,128)S(1)}, u32[]{:S(2)}) copy-start(f32[1,128,128]{2,1,0:T(8,128)S(1)} %combine.79.refs_0_) | copy-start | bytes 196612
  144.2 5.2 %collective-permute-start.34 = (f32[1,128,128]{2,1,0:T(8,128)S(1)}, f32[1,128,128]{2,1,0:T(8,128)S(1)}, u32[]{:S(2)}, u32[]{:S(2)}) collective-permute-start(f32[1,128,128]{2,1,0:T(8,128)S(1)} %combine.79.refs_0_), channel_id=1, source_target_pairs={{0,16},{8,24},{16,0},{24,8},{1,17},{9,25},{17,1},{25,9},{2,18},{10... | collective-permute-start | bytes 196616 | tf_op jit(solution)/shard_map/ppermute | solution.py:355
  149.4 0.6 copy-start.18

commit v4 on v3

--- a/solution.py
+++ b/solution.py
@@ -187,7 +187,7 @@
     n = y_v.shape[-1]
     cross = gram_v[0, :, n:]
     gram_v[0, :, :n] += cross + cross.T
-    rider = pieces[5]
+    rider = pieces[-3]
     save_gram = pltpu.make_async_copy(gram_v.at[:, :, pl.ds(0, n)], rider.at[pl.ds(rider.shape[0] - 1, 1)], sem_g)
     save_gram.start()
     add_and_save(pairs, found, list_row, list_tile, list_slot, tiles_v, split_v, sums_v, pieces, sem_p)
@@ -337,7 +337,7 @@
 
     def piece_shapes(pairs, rider):
         sizes = [devices * each // 4 for _, each, _ in pairs for _ in range(8)]
-        sizes[5] += rider
+        sizes[-3] += rider
         return [jax.ShapeDtypeStruct((n, side, wide), f32) for n in sizes]
 
     def list_scratch(pairs):
@@ -447,21 +447,19 @@
         cut = size // 2
         return [[(array, at + upper * cut) for array, at in (base, got)] for upper in range(2)]
 
-    def send_upper(pair, part):
+    def send_apart(pair, carrier=0):
         step, size, terms, rider = state[pair]
-        groups = [(terms[part][1], size)] + ([(rider, 1)] if rider and part == 0 else [])
-        sent = note(combine(groups))
-        return sent, swap(sent, orders_of[pair][part][step])
-
-    def keep_lower(pair, sent, got):
-        step, size, terms, rider = state[pair]
+        sent, got = [], []
+        for part in range(2):
+            groups = [(terms[part][1], size)] + ([(rider, 1)] if rider and part == carrier else [])
+            sent.append(note(combine(groups)))
+            got.append(swap(sent[part], orders_of[pair][part][step]))
         base = [combine([(terms[part][0], size)]) for part in range(2)]
-        rider = [(sent[0], size), (got[0], size)] if rider else []
+        rider = [(sent[carrier], size), (got[carrier], size)] if rider else []
         state[pair] = [step + 1, size // 2, [halves(size, (base[part], 0), (got[part], 0)) for part in range(2)], rider]
 
-    def send_apart(pair):
-        moved = [send_upper(pair, part) for part in range(2)]
-        keep_lower(pair, *zip(*moved))
+    def hand_over(pair, other):
+        state[other][3], state[pair][3] = state[pair][3], []
 
     def send_both_upper(pair):
         step, size, terms, rider = state[pair]
@@ -502,9 +500,6 @@
             name="owned_gram",
         )(inverse, *gram, *arrays)
         return z, note(gram)
-
-    def small_terms(pair):
-        return [array[at : at + 1] for array, at in state[pair][3]]
 
     cells_all = CELL_BLOCKS * side * devices
 
@@ -528,16 +523,18 @@
             name="late_products",
         )(tile_rows, tile_cols, tile_counts, block_order, tiles, follows(split))
 
-    def cell_inverse(*grams):
+    def cell_inverse(pair):
+        specs, arrays = term_specs([(state[pair][3], 1)])
         return note(
             pl.pallas_call(
                 functools.partial(factor_kernel, math.sqrt(cells_all)),
+                grid=(1,),
                 out_shape=jax.ShapeDtypeStruct((wide, wide), f32),
-                in_specs=[VMEM] * len(grams),
-                out_specs=VMEM,
+                in_specs=specs,
+                out_specs=pl.BlockSpec((wide, wide), lambda _: (0, 0)),
                 cost_estimate=cost(1.5),
                 name="cell_cholesky",
-            )(follows(grams[0]), *grams[1:])
+            )(follows(arrays[0]), *arrays[1:])
         )
 
     begin(0, *early[:8])
@@ -546,7 +543,7 @@
             wait([0])
             send_apart(0) if step < shared else send_both(0)
         wait([0])
-        inverse = cell_inverse(*small_terms(0))
+        inverse = cell_inverse(0)
         zs, gene_gram = [None], None
         zs[0], gene_gram = owners([0], inverse)
     else:
@@ -558,22 +555,25 @@
         late = late_products(late_pairs)
         note(late[0])
         begin(2, *late)
-        wait([0, 1])
+        wait([0])
         send_apart(0)
+        wait([1])
         send_both(1)
         wait([2])
         send_apart(2)
         wait([0, 1, 2])
+        hand_over(1, 2)
         send_both(0)
         send_apart(2)
         send_apart(1)
         wait([0, 1, 2])
+        hand_over(2, 1)
         send_both(0)
         send_both(2)
-        send_apart(1)
+        send_apart(1, 1)
         wait([0, 1, 2])
         send_both(2)
-        inverse = cell_inverse(*small_terms(0))
+        inverse = cell_inverse(1)
         z_early, gene_gram = owners([0, 1], inverse)
         wait([2])
         z_late, gene_gram = owners([2], inverse, (gene_gram,))
@@ -599,7 +599,7 @@
             pltpu.SemaphoreType.DMA((chunks,)),
             pltpu.SemaphoreType.DMA((chunks,)),
         ],
-        compiler_params=ROOMY,
+        compiler_params=pltpu.CompilerParams(vmem_limit_bytes=20 * 2**20),
         name="factors",
     )(split, inverse, *grams, *zs)
     return (cell_factor, gene_factor)

time: 160 us -> 158 us (0.988)
  waiting for transfers between devices: 67 us -> 73.2 us
  starting transfers between devices: 41.9 us -> 38.5 us
  Pallas kernels: 39.4 us -> 36.8 us
    ppermute x27, waiting for transfers between devices: 30.9 us -> 50.9 us  [swap(): return lax.ppermute(value, 'gy', [(i, i ^ partner) for i in range(ny)])]
    ppermute x8, waiting for transfers between devices: 36.2 us -> 22.3 us  [swap(): return lax.ppermute(value, 'gx', [(i, i ^ partner) for i in range(nx)])]
    ppermute x27, starting transfers between devices: 24.5 us -> 19.1 us  [swap(): return lax.ppermute(value, 'gy', [(i, i ^ partner) for i in range(ny)])]
    ppermute x8, starting transfers between devices: 17.4 us -> 19.4 us  [swap(): return lax.ppermute(value, 'gx', [(i, i ^ partner) for i in range(nx)])]
    unnamed x40 -> x44, local copies, waits for them, and re-layouts: 7.31 us -> 7.09 us
  transfers between devices with their start and end apart: 35 -> 35, of which waited for: 18 -> 22; matrix products, arithmetic and copies ran while one was open for 0% -> 0% of each run, Pallas kernels for 9% -> 9%
where the time goes in v4:
time: 158 us; the launch traced here: 157 us
  waiting for transfers between devices  73.2 us (46%)
  starting transfers between devices  38.5 us (24%)
  Pallas kernels  36.8 us (23%)
  local copies, waits for them, and re-layouts  7.09 us (4%)
  between operations  1.89 us (1%)
    ppermute x27, waiting for transfers between devices, swap(): return lax.ppermute(value, 'gy', [(i, i ^ partner) for i in range(ny)])  50.9 us
    ppermute x8, waiting for transfers between devices, swap(): return lax.ppermute(value, 'gx', [(i, i ^ partner) for i in range(nx)])  22.3 us
    ppermute x8, starting transfers between devices, swap(): return lax.ppermute(value, 'gx', [(i, i ^ partner) for i in range(nx)])  19.4 us
    ppermute x27, starting transfers between devices, swap(): return lax.ppermute(value, 'gy', [(i, i ^ partner) for i in range(ny)])  19.1 us
    pallas_call x1, Pallas kernels, on_device(): pl.pallas_call(functools.partial(first_kernel, nx, ny, early_pairs, owned...  14.6 us
    pallas_call x1, Pallas kernels, on_device(): pl.pallas_call(functools.partial(last_kernel, math.sqrt(genes), len(grams...  7.35 us
    unnamed x44, local copies, waits for them, and re-layouts  7.09 us
    pallas_call x1, Pallas kernels, cell_inverse(): pl.pallas_call(functools.partial(factor_kernel, math.sqrt(cells_all)), gr...  5.78 us
  transfers between devices with their start and end apart: 35, of which 22 were waited for; matrix products, arithmetic and copies ran while one was open for 0% of the time, Pallas kernels for 9%

profile of v4, /device:TPU:0, one launch (start us, length us, event | category | flops | bytes accessed | tf_op | source)
XLA Modules:
  0.0 157.5 jit_solution(6713981843992130410)
XLA Ops:
  1.3 14.6 %tile_products.1 = (f32[16,128,128]{2,1,0:T(8,128)}, f32[16,128,128]{2,1,0:T(8,128)}, f32[16,128,128]{2,1,0:T(8,128)}, f32[16,128,128]{2,1,0:T(8,128)}, f32[16,1...) custom-call(s32[192]{0:T(256)} %rows.3, s32[192]{0:T(256)} %cols.3, ...), custom_call_target="tpu_custom_call" | custom-call | flops 4000000000 | bytes 12000000 | tf_op jit(solution)/shard_map/tile_products/pallas_call | solution.py:357
  15.9 1.1 collective-permute-start.4
  17.1 0.4 collective-permute-start.3
  17.6 0.4 collective-permute-start.10
  18.0 1.5 collective-permute-done.4.refs_1_
  19.5 0.4 collective-permute-start
  19.9 1.1 collective-permute-done.5.refs_1_
  21.0 1.2 copy-done.5
  22.3 0.1 combine.44
  22.4 3.8 %collective-permute-start.8 = (f32[16,128,128]{2,1,0:T(8,128)S(1)}, f32[16,128,128]{2,1,0:T(8,128)S(1)}, u32[]{:S(2)}, u32[]{:S(2)}) collective-permute-start(f32[16,128,128]{2,1,0:T(8,128)S(1)} %combine.44), channel_id=1, source_target_pairs={{0,2},{1,3},{2,0},{3,1},{4,6},{5,7},{6,4},{7,5},{8,10},{9,11},{10,... | collective-permute-start | bytes 3145736 | tf_op jit(solution)/shard_map/ppermute | solution.py:353
  26.2 1.2 copy-done.4
  27.5 0.1 combine.41
  27.6 2.8 %collective-permute-start.9 = (f32[16,128,128]{2,1,0:T(8,128)S(1)}, f32[16,128,128]{2,1,0:T(8,128)S(1)}, u32[]{:S(2)}, u32[]{:S(2)}) collective-permute-start(f32[16,128,128]{2,1,0:T(8,128)S(1)} %combine.41), channel_id=1, source_target_pairs={{0,4},{1,5},{2,6},{3,7},{4,0},{5,1},{6,2},{7,3},{8,12},{9,13},{10,... | collective-permute-start | bytes 3145736 | tf_op jit(solution)/shard_map/ppermute | solution.py:353
  30.4 0.1 combine.42.refs_4_
  30.6 2.6 %collective-permute-start.6 = (f32[17,128,128]{2,1,0:T(8,128)S(1)}, f32[17,128,128]{2,1,0:T(8,128)S(1)}, u32[]{:S(2)}, u32[]{:S(2)}) collective-permute-start(f32[17,128,128]{2,1,0:T(8,128)S(1)} %combine.42.refs_4_), channel_id=1, source_target_pairs={{0,8},{8,0},{16,24},{24,16},{1,9},{9,1},{17,25},{25,17},{2,10},{10... | collective-permute-start | bytes 3342344 | tf_op jit(solution)/shard_map/ppermute | solution.py:355
  33.1 0.3 collective-permute-start.1
  33.4 2.8 %copy-done.14 = bf16[192,128,128]{2,1,0:T(8,128)(2,1)S(1)} copy-done((bf16[192,128,128]{2,1,0:T(8,128)(2,1)S(1)}, bf16[192,128,128]{2,1,0:T(8,128)(2,1)}, u32[]{:S(2)}) %copy-start.14) | copy-done | bytes 6291480
  36.2 5.1 %late_products.1 = (f32[8,128,128]{2,1,0:T(8,128)S(1)}, f32[8,128,128]{2,1,0:T(8,128)S(1)}, f32[8,128,128]{2,1,0:T(8,128)S(1)}, f32[8,128,128]{2,1,0:T(8,128)S(1...) custom-call(s32[192]{0:T(256)S(1)} %copy-done.17, ...), custom_call_target="tpu_custom_call" | custom-call | flops 4000000000 | bytes 12000000 | tf_op jit(solution)/shard_map/late_products/pallas_call | solution.py:507
  41.3 8.4 %collective-permute-done.8.refs_1_ = f32[16,128,128]{2,1,0:T(8,128)S(1)} collective-permute-done((f32[16,128,128]{2,1,0:T(8,128)S(1)}, f32[16,128,128]{2,1,0:T(8,128)S(1)}, u32[]{:S(2)}, u32[]{:S(2)}) %collective-permute-start.8) | collective-permute-done | bytes 1048608 | tf_op jit(solution)/shard_map/ppermute | solution.py:353
  49.7 4.1 %collective-permute-done.9.refs_1_ = f32[16,128,128]{2,1,0:T(8,128)S(1)} collective-permute-done((f32[16,128,128]{2,1,0:T(8,128)S(1)}, f32[16,128,128]{2,1,0:T(8,128)S(1)}, u32[]{:S(2)}, u32[]{:S(2)}) %collective-permute-start.9) | collective-permute-done | bytes 1048608 | tf_op jit(solution)/shard_map/ppermute | solution.py:353
  53.8 0.1 combine.47.refs_0_
  54.0 1.8 %collective-permute-start.11 = (f32[8,128,128]{2,1,0:T(8,128)S(1)}, f32[8,128,128]{2,1,0:T(8,128)S(1)}, u32[]{:S(2)}, u32[]{:S(2)}) collective-permute-start(f32[8,128,128]{2,1,0:T(8,128)S(1)} %combine.48), channel_id=1, source_target_pairs={{0,4},{1,5},{2,6},{3,7},{4,0},{5,1},{6,2},{7,3},{8,12},{9,13},{10,... | collective-permute-start | bytes 1572872 | tf_op jit(solution)/shard_map/ppermute | solution.py:353
  56.0 0.3 collective-permute-start.12
  56.4 1.9 %collective-permute-done.6.refs_1_.refs_3_.refs_5_ = f32[17,128,128]{2,1,0:T(8,128)S(1)} collective-permute-done((f32[17,128,128]{2,1,0:T(8,128)S(1)}, f32[17,128,128]{2,1,0:T(8,128)S(1)}, u32[]{:S(2)}, u32[]{:S(2)}) %collective-permute-start.6) | collective-permute-done | bytes 1114144 | tf_op jit(solution)/shard_map/ppermute | solution.py:355
  58.4 6.0 %collective-permute-start.13 = (f32[9,128,128]{2,1,0:T(8,128)S(1)}, f32[9,128,128]{2,1,0:T(8,128)S(1)}, u32[]{:S(2)}, u32[]{:S(2)}) collective-permute-start(f32[9,128,128]{2,1,0:T(8,128)S(1)} %combine.49.refs_2_), channel_id=1, source_target_pairs={{0,16},{8,24},{16,0},{24,8},{1,17},{9,25},{17,1},{25,9},{2,18},{10... | collective-permute-start | bytes 1769480 | tf_op jit(solution)/shard_map/ppermute | solution.py:355
  64.5 0.2 collective-permute-start.17
  64.7 1.3 collective-permute-start.16
  66.0 2.8 %collective-permute-done.11.refs_1_ = f32[8,128,128]{2,1,0:T(8,128)S(1)} collective-permute-done((f32[8,128,128]{2,1,0:T(8,128)S(1)}, f32[8,128,128]{2,1,0:T(8,128)S(1)}, u32[]{:S(2)}, u32[]{:S(2)}) %collective-permute-start.11) | collective-permute-done | bytes 524320 | tf_op jit(solution)/shard_map/ppermute | solution.py:353
  68.8 2.0 %collective-permute-done.12.refs_3_ = f32[8,128,128]{2,1,0:T(8,128)S(1)} collective-permute-done((f32[8,128,128]{2,1,0:T(8,128)S(1)}, f32[8,128,128]{2,1,0:T(8,128)S(1)}, u32[]{:S(2)}, u32[]{:S(2)}) %collective-permute-start.12) | collective-permute-done | bytes 524320 | tf_op jit(solution)/shard_map/ppermute | solution.py:353
  71.0 8.7 %collective-permute-done.17.refs_1_ = f32[8,128,128]{2,1,0:T(8,128)S(1)} collective-permute-done((f32[8,128,128]{2,1,0:T(8,128)S(1)}, f32[8,128,128]{2,1,0:T(8,128)S(1)}, u32[]{:S(2)}, u32[]{:S(2)}) %collective-permute-start.17) | collective-permute-done | bytes 524320 | tf_op jit(solution)/shard_map/ppermute | solution.py:353
  79.7 1.7 %collective-permute-done.16.refs_1_ = f32[8,128,128]{2,1,0:T(8,128)S(1)} collective-permute-done((f32[8,128,128]{2,1,0:T(8,128)S(1)}, f32[8,128,128]{2,1,0:T(8,128)S(1)}, u32[]{:S(2)}, u32[]{:S(2)}) %collective-permute-start.16) | collective-permute-done | bytes 524320 | tf_op jit(solution)/shard_map/ppermute | solution.py:353
  81.4 9.1 %collective-permute-done.13.refs_1_.refs_3_ = f32[9,128,128]{2,1,0:T(8,128)S(1)} collective-permute-done((f32[9,128,128]{2,1,0:T(8,128)S(1)}, f32[9,128,128]{2,1,0:T(8,128)S(1)}, u32[]{:S(2)}, u32[]{:S(2)}) %collective-permute-start.13) | collective-permute-done | bytes 589856 | tf_op jit(solution)/shard_map/ppermute | solution.py:355
  90.5 0.8 collective-permute-start.18
  91.4 0.1 collective-permute-start.22
  91.7 1.3 collective-permute-start.24
  93.1 0.8 collective-permute-start.19
  93.9 1.9 %collective-permute-start.20 = (f32[2,128,128]{2,1,0:T(8,128)S(1)}, f32[2,128,128]{2,1,0:T(8,128)S(1)}, u32[]{:S(2)}, u32[]{:S(2)}) collective-permute-start(f32[2,128,128]{2,1,0:T(8,128)S(1)} %combine.57), channel_id=1, source_target_pairs={{0,4},{1,5},{2,6},{3,7},{4,0},{5,1},{6,2},{7,3},{8,12},{9,13},{10,... | collective-permute-start | bytes 393224 | tf_op jit(solution)/shard_map/ppermute | solution.py:353
  96.0 6.4 %collective-permute-done.19.refs_1_ = f32[2,128,128]{2,1,0:T(8,128)S(1)} collective-permute-done((f32[2,128,128]{2,1,0:T(8,128)S(1)}, f32[2,128,128]{2,1,0:T(8,128)S(1)}, u32[]{:S(2)}, u32[]{:S(2)}) %collective-permute-start.19) | collective-permute-done | bytes 131104 | tf_op jit(solution)/shard_map/ppermute | solution.py:353
  102.4 1.2 collective-permute-done.20.refs_1_
  103.6 0.1 collective-permute-done.18.refs_1_.refs_3_
  103.8 3.3 %collective-permute-start.25 = (f32[4,128,128]{2,1,0:T(8,128)S(1)}, f32[4,128,128]{2,1,0:T(8,128)S(1)}, u32[]{:S(2)}, u32[]{:S(2)}) collective-permute-start(f32[4,128,128]{2,1,0:T(8,128)S(1)} %combine.67), channel_id=1, source_target_pairs={{0,16},{8,24},{16,0},{24,8},{1,17},{9,25},{17,1},{25,9},{2,18},{10... | collective-permute-start | bytes 786440 | tf_op jit(solution)/shard_map/ppermute | solution.py:355
  107.2 1.6 collective-permute-start.28
  108.8 0.2 collective-permute-start.27
  109.0 1.2 collective-permute-start.26
  110.4 3.0 %collective-permute-done.26.refs_5_ = f32[1,128,128]{2,1,0:T(8,128)S(1)} collective-permute-done((f32[1,128,128]{2,1,0:T(8,128)S(1)}, f32[1,128,128]{2,1,0:T(8,128)S(1)}, u32[]{:S(2)}, u32[]{:S(2)}) %collective-permute-start.26) | collective-permute-done | bytes 65568 | tf_op jit(solution)/shard_map/ppermute | solution.py:353
  113.4 0.4 collective-permute-done.27.refs_1_.refs_7_
  113.8 4.8 %collective-permute-done.25.refs_1_.refs_3_ = f32[4,128,128]{2,1,0:T(8,128)S(1)} collective-permute-done((f32[4,128,128]{2,1,0:T(8,128)S(1)}, f32[4,128,128]{2,1,0:T(8,128)S(1)}, u32[]{:S(2)}, u32[]{:S(2)}) %collective-permute-start.25) | collective-permute-done | bytes 262176 | tf_op jit(solution)/shard_map/ppermute | solution.py:355
  118.6 0.5 collective-permute-done.28.refs_1_.refs_3_
  119.1 0.9 collective-permute-start.29
  120.0 5.8 %cell_cholesky.1.inverse = f32[128,128]{1,0:T(8,128)} custom-call(f32[2,128,128]{2,1,0:T(8,128)} %copy-done.11, f32[2,128,128]{2,1,0:T(8,128)} %copy-done.15), custom_call_target="tpu_custom_call" | custom-call | flops 1500000000 | bytes 4500000 | tf_op jit(solution)/shard_map/cell_cholesky/pallas_call | solution.py:529
  125.8 0.8 copy-done.12
  126.7 0.9 copy-done.16
  127.6 1.5 owned_gram.2
  129.0 0.7 owned_gram.3
  129.8 1.2 collective-permute-done.30.refs_1_
  131.1 0.2 collective-permute-start.31
  131.3 4.1 %collective-permute-done.31.refs_1_ = f32[1,128,128]{2,1,0:T(8,128)S(1)} collective-permute-done((f32[1,128,128]{2,1,0:T(8,128)S(1)}, f32[1,128,128]{2,1,0:T(8,128)S(1)}, u32[]{:S(2)}, u32[]{:S(2)}) %collective-permute-start.31) | collective-permute-done | bytes 65568 | tf_op jit(solution)/shard_map/ppermute | solution.py:353
  135.4 0.1 collective-permute-start.32
  135.6 4.2 %collective-permute-done.32.refs_1_ = f32[1,128,128]{2,1,0:T(8,128)S(1)} collective-permute-done((f32[1,128,128]{2,1,0:T(8,128)S(1)}, f32[1,128,128]{2,1,0:T(8,128)S(1)}, u32[]{:S(2)}, u32[]{:S(2)}) %collective-permute-start.32) | collective-permute-done | bytes 65568 | tf_op jit(solution)/shard_map/ppermute | solution.py:353
  139.8 2.7 %collective-permute-start.33 = (f32[1,128,128]{2,1,0:T(8,128)S(1)}, f32[1,128,128]{2,1,0:T(8,128)S(1)}, u32[]{:S(2)}, u32[]{:S(2)}) collective-permute-start(f32[1,128,128]{2,1,0:T(8,128)S(1)} %combine.78.refs_0_), channel_id=1, source_target_pairs={{0,8},{8,0},{16,24},{24,16},{1,9},{9,1},{17,25},{25,17},{2,10},{10... | collective-permute-start | bytes 196616 | tf_op jit(solution)/shard_map/ppermute | solution.py:355
  142.4 2.2 %collective-permute-done.33.refs_1_ = f32[1,128,128]{2,1,0:T(8,128)S(1)} collective-permute-done((f32[1,128,128]{2,1,0:T(8,128)S(1)}, f32[1,128,128]{2,1,0:T(8,128)S(1)}, u32[]{:S(2)}, u32[]{:S(2)}) %collective-permute-start.33) | collective-permute-done | bytes 65568 | tf_op jit(solution)/shard_map/ppermute | solution.py:355
  144.7 1.5 collective-permute-start.34
  146.2 3.7 %collective-permute-done.34.refs_1_ = f32[1,128,128]{2,1,0:T(8,128)S(1)} collective-permute-done((f32[1,128,128]{2,1,0:T(8,128)S(1)}, f32[1,128,128]{2,1,0:T(8,128)S(1)}, u32[]{:S(2)}, u32[]{:S(2)}) %collective-permute-start.34) | collective-permute-done | bytes 65568 | tf_op jit(solution)/shard_map/ppermute | solution.py:355
  149.9 7.4 %factors.1 = (f32[1024,128]{1,0:T(8,128)}, bf16[8192,128]{1,0:T(8,128)(2,1)}) custom-call(bf16[64,128,256]{2,1,0:T(8,128)(2,1)S(1)} %copy-done.1, f32[128,128]{1,0:T(8,128)S(1)} %copy-done.13, f32[1,128,128]{2,1,0:T(8,128)S(1)} %combine.79.refs_0_, f32[1,128,128]{2,1,0:T(8,128)S(1)} %collective-permute-done.34.refs_1_, ...), custom_call_target="tpu_custom_call" | custom-call | tf_op jit(solution)/shard_map/factors/pallas_call | solution.py:588
  (96 shorter events, 1.7 us)
Async XLA Ops:
  15.9 3.6 %collective-permute-start.4 = (f32[16,128,128]{2,1,0:T(8,128)}, f32[16,128,128]{2,1,0:T(8,128)S(1)}, u32[]{:S(2)}, u32[]{:S(2)}) collective-permute-start(f32[16,128,128]{2,1,0:T(8,128)} %get-tuple-element.68), channel_id=1, source_target_pairs={{0,1},{1,0},{2,3},{3,2},{4,5},{5,4},{6,7},{7,6},{8,9},{9,8},{10,11... | collective-permute-start | bytes 3145736 | tf_op jit(solution)/shard_map/ppermute | solution.py:353
  17.0 4.0 %collective-permute-start.5 = (f32[16,128,128]{2,1,0:T(8,128)}, f32[16,128,128]{2,1,0:T(8,128)S(1)}, u32[]{:S(2)}, u32[]{:S(2)}) collective-permute-start(f32[16,128,128]{2,1,0:T(8,128)} %get-tuple-element.69), channel_id=1, source_target_pairs={{0,1},{1,0},{2,3},{3,2},{4,5},{5,4},{6,7},{7,6},{8,9},{9,8},{10,11... | collective-permute-start | bytes 3145736 | tf_op jit(solution)/shard_map/ppermute | solution.py:353
  17.1 10.5 %collective-permute-start.3 = (f32[8,128,128]{2,1,0:T(8,128)}, f32[8,128,128]{2,1,0:T(8,128)S(1)}, u32[]{:S(2)}, u32[]{:S(2)}) collective-permute-start(f32[8,128,128]{2,1,0:T(8,128)} %get-tuple-element.66), channel_id=1, source_target_pairs={{0,1},{1,0},{2,3},{3,2},{4,5},{5,4},{6,7},{7,6},{8,9},{9,8},{10,11... | collective-permute-start | bytes 1572872 | tf_op jit(solution)/shard_map/ppermute | solution.py:353
  17.5 12.9 %collective-permute-start.2 = (f32[9,128,128]{2,1,0:T(8,128)}, f32[9,128,128]{2,1,0:T(8,128)S(1)}, u32[]{:S(2)}, u32[]{:S(2)}) collective-permute-start(f32[9,128,128]{2,1,0:T(8,128)} %get-tuple-element.65.refs_4_), channel_id=1, source_target_pairs={{0,1},{1,0},{2,3},{3,2},{4,5},{5,4},{6,7},{7,6},{8,9},{9,8},{10,11... | collective-permute-start | bytes 1769480 | tf_op jit(solution)/shard_map/ppermute | solution.py:353
  17.6 15.5 %collective-permute-start.10 = (f32[16,128,128]{2,1,0:T(8,128)}, f32[16,128,128]{2,1,0:T(8,128)S(1)}, u32[]{:S(2)}, u32[]{:S(2)}) collective-permute-start(f32[16,128,128]{2,1,0:T(8,128)} %get-tuple-element.83), channel_id=1, source_target_pairs={{0,1},{1,0},{2,3},{3,2},{4,5},{5,4},{6,7},{7,6},{8,9},{9,8},{10,11... | collective-permute-start | bytes 3145736 | tf_op jit(solution)/shard_map/ppermute | solution.py:353
  19.5 11.0 %collective-permute-start = (f32[8,128,128]{2,1,0:T(8,128)}, f32[8,128,128]{2,1,0:T(8,128)S(1)}, u32[]{:S(2)}, u32[]{:S(2)}) collective-permute-start(f32[8,128,128]{2,1,0:T(8,128)} %get-tuple-element.61), channel_id=1, source_target_pairs={{0,1},{1,0},{2,3},{3,2},{4,5},{5,4},{6,7},{7,6},{8,9},{9,8},{10,11... | collective-permute-start | bytes 1572872 | tf_op jit(solution)/shard_map/ppermute | solution.py:353
  21.0 1.2 copy-start.5
  22.2 8.1 %copy-start.20 = (f32[16,128,128]{2,1,0:T(8,128)S(1)}, f32[16,128,128]{2,1,0:T(8,128)}, u32[]{:S(2)}) copy-start(f32[16,128,128]{2,1,0:T(8,128)} %get-tuple-element.75) | copy-start | bytes 3145732
  22.2 8.2 %copy-start.6 = (f32[9,128,128]{2,1,0:T(8,128)S(1)}, f32[9,128,128]{2,1,0:T(8,128)}, u32[]{:S(2)}) copy-start(f32[9,128,128]{2,1,0:T(8,128)} %get-tuple-element.65.refs_4_) | copy-start | bytes 1769476
  22.2 8.2 %copy-start.7 = (f32[8,128,128]{2,1,0:T(8,128)S(1)}, f32[8,128,128]{2,1,0:T(8,128)}, u32[]{:S(2)}) copy-start(f32[8,128,128]{2,1,0:T(8,128)} %get-tuple-element.64.refs_0_) | copy-start | bytes 1572868
  22.2 8.2 %copy-start.8 = (f32[8,128,128]{2,1,0:T(8,128)S(1)}, f32[8,128,128]{2,1,0:T(8,128)}, u32[]{:S(2)}) copy-start(f32[8,128,128]{2,1,0:T(8,128)} %get-tuple-element.72.refs_2_) | copy-start | bytes 1572868
  22.3 11.1 %copy-start.17 = (s32[192]{0:T(256)S(1)}, s32[192]{0:T(256)}, u32[]{:S(2)}) copy-start(s32[192]{0:T(256)} %rows.3) | copy-start | bytes 2308
  22.3 11.1 %copy-start.18 = (s32[192]{0:T(256)S(1)}, s32[192]{0:T(256)}, u32[]{:S(2)}) copy-start(s32[192]{0:T(256)} %cols.3) | copy-start | bytes 2308
  22.3 11.1 %copy-start.19 = (s32[256]{0:T(256)S(1)}, s32[256]{0:T(256)}, u32[]{:S(2)}) copy-start(s32[256]{0:T(256)} %order.3) | copy-start | bytes 3076
  22.4 11.0 %copy-start = (bf16[64,128,256]{2,1,0:T(8,128)(2,1)S(1)}, bf16[64,128,256]{2,1,0:T(8,128)(2,1)}, u32[]{:S(2)}) copy-start(bf16[64,128,256]{2,1,0:T(8,128)(2,1)} %get-tuple-element.78.split) | copy-start | bytes 12582916
  22.4 27.3 %collective-permute-start.8 = (f32[16,128,128]{2,1,0:T(8,128)S(1)}, f32[16,128,128]{2,1,0:T(8,128)S(1)}, u32[]{:S(2)}, u32[]{:S(2)}) collective-permute-start(f32[16,128,128]{2,1,0:T(8,128)S(1)} %combine.44), channel_id=1, source_target_pairs={{0,2},{1,3},{2,0},{3,1},{4,6},{5,7},{6,4},{7,5},{8,10},{9,11},{10,... | collective-permute-start | bytes 3145736 | tf_op jit(solution)/shard_map/ppermute | solution.py:353
  26.2 1.2 copy-start.4
  27.5 5.7 %copy-start.21 = (f32[8,128,128]{2,1,0:T(8,128)S(1)}, f32[8,128,128]{2,1,0:T(8,128)}, u32[]{:S(2)}) copy-start(f32[8,128,128]{2,1,0:T(8,128)} %get-tuple-element.63) | copy-start | bytes 1572868
  27.6 26.2 %collective-permute-start.9 = (f32[16,128,128]{2,1,0:T(8,128)S(1)}, f32[16,128,128]{2,1,0:T(8,128)S(1)}, u32[]{:S(2)}, u32[]{:S(2)}) collective-permute-start(f32[16,128,128]{2,1,0:T(8,128)S(1)} %combine.41), channel_id=1, source_target_pairs={{0,4},{1,5},{2,6},{3,7},{4,0},{5,1},{6,2},{7,3},{8,12},{9,13},{10,... | collective-permute-start | bytes 3145736 | tf_op jit(solution)/shard_map/ppermute | solution.py:353
  30.4 23.6 %collective-permute-start.7 = (f32[16,128,128]{2,1,0:T(8,128)S(1)}, f32[16,128,128]{2,1,0:T(8,128)S(1)}, u32[]{:S(2)}, u32[]{:S(2)}) collective-permute-start(f32[16,128,128]{2,1,0:T(8,128)S(1)} %copy-done.20), channel_id=1, source_target_pairs={{0,1},{1,0},{2,3},{3,2},{4,5},{5,4},{6,7},{7,6},{8,9},{9,8},{10,11... | collective-permute-start | bytes 3145736 | tf_op jit(solution)/shard_map/ppermute | solution.py:353
  30.6 27.8 %collective-permute-start.6 = (f32[17,128,128]{2,1,0:T(8,128)S(1)}, f32[17,128,128]{2,1,0:T(8,128)S(1)}, u32[]{:S(2)}, u32[]{:S(2)}) collective-permute-start(f32[17,128,128]{2,1,0:T(8,128)S(1)} %combine.42.refs_4_), channel_id=1, source_target_pairs={{0,8},{8,0},{16,24},{24,16},{1,9},{9,1},{17,25},{25,17},{2,10},{10... | collective-permute-start | bytes 3342344 | tf_op jit(solution)/shard_map/ppermute | solution.py:355
  33.1 20.7 %copy-start.3 = (f32[16,128,128]{2,1,0:T(8,128)S(1)}, f32[16,128,128]{2,1,0:T(8,128)}, u32[]{:S(2)}) copy-start(f32[16,128,128]{2,1,0:T(8,128)} %get-tuple-element.82.refs_0_) | copy-start | bytes 3145732
  33.1 22.9 %collective-permute-start.1 = (f32[8,128,128]{2,1,0:T(8,128)S(1)}, f32[8,128,128]{2,1,0:T(8,128)S(1)}, u32[]{:S(2)}, u32[]{:S(2)}) collective-permute-start(f32[8,128,128]{2,1,0:T(8,128)S(1)} %copy-done.21), channel_id=1, source_target_pairs={{0,1},{1,0},{2,3},{3,2},{4,5},{5,4},{6,7},{7,6},{8,9},{9,8},{10,11... | collective-permute-start | bytes 1572872 | tf_op jit(solution)/shard_map/ppermute | solution.py:353
  33.4 2.8 %copy-start.14 = (bf16[192,128,128]{2,1,0:T(8,128)(2,1)S(1)}, bf16[192,128,128]{2,1,0:T(8,128)(2,1)}, u32[]{:S(2)}) copy-start(bf16[192,128,128]{2,1,0:T(8,128)(2,1)} %tiles.3) | copy-start | bytes 18874372
  41.3 14.5 %copy-start.2 = (f32[16,128,128]{2,1,0:T(8,128)S(1)}, f32[16,128,128]{2,1,0:T(8,128)}, u32[]{:S(2)}) copy-start(f32[16,128,128]{2,1,0:T(8,128)} %get-tuple-element.74.refs_0_) | copy-start | bytes 3145732
  49.7 14.7 %collective-permute-start.14 = (f32[8,128,128]{2,1,0:T(8,128)S(1)}, f32[8,128,128]{2,1,0:T(8,128)S(1)}, u32[]{:S(2)}, u32[]{:S(2)}) collective-permute-start(f32[8,128,128]{2,1,0:T(8,128)S(1)} %get-tuple-element.86), channel_id=1, source_target_pairs={{0,1},{1,0},{2,3},{3,2},{4,5},{5,4},{6,7},{7,6},{8,9},{9,8},{10,11... | collective-permute-start | bytes 1572872 | tf_op jit(solution)/shard_map/ppermute | solution.py:353
  53.8 10.6 %collective-permute-start.15 = (f32[8,128,128]{2,1,0:T(8,128)S(1)}, f32[8,128,128]{2,1,0:T(8,128)S(1)}, u32[]{:S(2)}, u32[]{:S(2)}) collective-permute-start(f32[8,128,128]{2,1,0:T(8,128)S(1)} %get-tuple-element.87), channel_id=1, source_target_pairs={{0,1},{1,0},{2,3},{3,2},{4,5},{5,4},{6,7},{7,6},{8,9},{9,8},{10,11... | collective-permute-start | bytes 1572872 | tf_op jit(solution)/shard_map/ppermute | solution.py:353
  53.9 2.4 %copy-start.9 = (f32[8,128,128]{2,1,0:T(8,128)S(1)}, f32[8,128,128]{2,1,0:T(8,128)}, u32[]{:S(2)}) copy-start(f32[8,128,128]{2,1,0:T(8,128)} %get-tuple-element.60.refs_0_) | copy-start | bytes 1572868
  53.9 2.4 %copy-start.10 = (f32[8,128,128]{2,1,0:T(8,128)S(1)}, f32[8,128,128]{2,1,0:T(8,128)}, u32[]{:S(2)}) copy-start(f32[8,128,128]{2,1,0:T(8,128)} %get-tuple-element.62.refs_2_) | copy-start | bytes 1572868
  54.0 14.8 %collective-permute-start.11 = (f32[8,128,128]{2,1,0:T(8,128)S(1)}, f32[8,128,128]{2,1,0:T(8,128)S(1)}, u32[]{:S(2)}, u32[]{:S(2)}) collective-permute-start(f32[8,128,128]{2,1,0:T(8,128)S(1)} %combine.48), channel_id=1, source_target_pairs={{0,4},{1,5},{2,6},{3,7},{4,0},{5,1},{6,2},{7,3},{8,12},{9,13},{10,... | collective-permute-start | bytes 1572872 | tf_op jit(solution)/shard_map/ppermute | solution.py:353
  56.0 14.8 %collective-permute-start.12 = (f32[8,128,128]{2,1,0:T(8,128)S(1)}, f32[8,128,128]{2,1,0:T(8,128)S(1)}, u32[]{:S(2)}, u32[]{:S(2)}) collective-permute-start(f32[8,128,128]{2,1,0:T(8,128)S(1)} %combine.45), channel_id=1, source_target_pairs={{0,2},{1,3},{2,0},{3,1},{4,6},{5,7},{6,4},{7,5},{8,10},{9,11},{10,... | collective-permute-start | bytes 1572872 | tf_op jit(solution)/shard_map/ppermute | solution.py:353
  58.4 32.1 %collective-permute-start.13 = (f32[9,128,128]{2,1,0:T(8,128)S(1)}, f32[9,128,128]{2,1,0:T(8,128)S(1)}, u32[]{:S(2)}, u32[]{:S(2)}) collective-permute-start(f32[9,128,128]{2,1,0:T(8,128)S(1)} %combine.49.refs_2_), channel_id=1, source_target_pairs={{0,16},{8,24},{16,0},{24,8},{1,17},{9,25},{17,1},{25,9},{2,18},{10... | collective-permute-start | bytes 1769480 | tf_op jit(solution)/shard_map/ppermute | solution.py:355
  64.5 15.2 %collective-permute-start.17 = (f32[8,128,128]{2,1,0:T(8,128)S(1)}, f32[8,128,128]{2,1,0:T(8,128)S(1)}, u32[]{:S(2)}, u32[]{:S(2)}) collective-permute-start(f32[8,128,128]{2,1,0:T(8,128)S(1)} %combine.51), channel_id=1, source_target_pairs={{0,4},{1,5},{2,6},{3,7},{4,0},{5,1},{6,2},{7,3},{8,12},{9,13},{10,... | collective-permute-start | bytes 1572872 | tf_op jit(solution)/shard_map/ppermute | solution.py:353
  64.7 16.6 %collective-permute-start.16 = (f32[8,128,128]{2,1,0:T(8,128)S(1)}, f32[8,128,128]{2,1,0:T(8,128)S(1)}, u32[]{:S(2)}, u32[]{:S(2)}) collective-permute-start(f32[8,128,128]{2,1,0:T(8,128)S(1)} %combine.50), channel_id=1, source_target_pairs={{0,2},{1,3},{2,0},{3,1},{4,6},{5,7},{6,4},{7,5},{8,10},{9,11},{10,... | collective-permute-start | bytes 1572872 | tf_op jit(solution)/shard_map/ppermute | solution.py:353
  68.8 22.5 %collective-permute-start.21 = (f32[8,128,128]{2,1,0:T(8,128)S(1)}, f32[8,128,128]{2,1,0:T(8,128)S(1)}, u32[]{:S(2)}, u32[]{:S(2)}) collective-permute-start(f32[8,128,128]{2,1,0:T(8,128)S(1)} %get-tuple-element.94), channel_id=1, source_target_pairs={{0,1},{1,0},{2,3},{3,2},{4,5},{5,4},{6,7},{7,6},{8,9},{9,8},{10,11... | collective-permute-start | bytes 1572872 | tf_op jit(solution)/shard_map/ppermute | solution.py:353
  70.8 20.7 %collective-permute-start.23 = (f32[8,128,128]{2,1,0:T(8,128)S(1)}, f32[8,128,128]{2,1,0:T(8,128)S(1)}, u32[]{:S(2)}, u32[]{:S(2)}) collective-permute-start(f32[8,128,128]{2,1,0:T(8,128)S(1)} %get-tuple-element.97), channel_id=1, source_target_pairs={{0,1},{1,0},{2,3},{3,2},{4,5},{5,4},{6,7},{7,6},{8,9},{9,8},{10,11... | collective-permute-start | bytes 1572872 | tf_op jit(solution)/shard_map/ppermute | solution.py:353
  90.5 13.3 %collective-permute-start.18 = (f32[8,128,128]{2,1,0:T(8,128)S(1)}, f32[8,128,128]{2,1,0:T(8,128)S(1)}, u32[]{:S(2)}, u32[]{:S(2)}) collective-permute-start(f32[8,128,128]{2,1,0:T(8,128)S(1)} %combine.55), channel_id=1, source_target_pairs={{0,8},{8,0},{16,24},{24,16},{1,9},{9,1},{17,25},{25,17},{2,10},{10... | collective-permute-start | bytes 1572872 | tf_op jit(solution)/shard_map/ppermute | solution.py:355
  91.4 12.2 %collective-permute-start.22 = (f32[5,128,128]{2,1,0:T(8,128)S(1)}, f32[5,128,128]{2,1,0:T(8,128)S(1)}, u32[]{:S(2)}, u32[]{:S(2)}) collective-permute-start(f32[5,128,128]{2,1,0:T(8,128)S(1)} %combine.59.refs_2_), channel_id=1, source_target_pairs={{0,4},{1,5},{2,6},{3,7},{4,0},{5,1},{6,2},{7,3},{8,12},{9,13},{10,... | collective-permute-start | bytes 983048 | tf_op jit(solution)/shard_map/ppermute | solution.py:353
  91.7 12.0 %collective-permute-start.24 = (f32[4,128,128]{2,1,0:T(8,128)S(1)}, f32[4,128,128]{2,1,0:T(8,128)S(1)}, u32[]{:S(2)}, u32[]{:S(2)}) collective-permute-start(f32[4,128,128]{2,1,0:T(8,128)S(1)} %combine.61), channel_id=1, source_target_pairs={{0,2},{1,3},{2,0},{3,1},{4,6},{5,7},{6,4},{7,5},{8,10},{9,11},{10,... | collective-permute-start | bytes 786440 | tf_op jit(solution)/shard_map/ppermute | solution.py:353
  93.1 9.3 %collective-permute-start.19 = (f32[2,128,128]{2,1,0:T(8,128)S(1)}, f32[2,128,128]{2,1,0:T(8,128)S(1)}, u32[]{:S(2)}, u32[]{:S(2)}) collective-permute-start(f32[2,128,128]{2,1,0:T(8,128)S(1)} %combine.56), channel_id=1, source_target_pairs={{0,2},{1,3},{2,0},{3,1},{4,6},{5,7},{6,4},{7,5},{8,10},{9,11},{10,... | collective-permute-start | bytes 393224 | tf_op jit(solution)/shard_map/ppermute | solution.py:353
  93.9 9.7 %collective-permute-start.20 = (f32[2,128,128]{2,1,0:T(8,128)S(1)}, f32[2,128,128]{2,1,0:T(8,128)S(1)}, u32[]{:S(2)}, u32[]{:S(2)}) collective-permute-start(f32[2,128,128]{2,1,0:T(8,128)S(1)} %combine.57), channel_id=1, source_target_pairs={{0,4},{1,5},{2,6},{3,7},{4,0},{5,1},{6,2},{7,3},{8,12},{9,13},{10,... | collective-permute-start | bytes 393224 | tf_op jit(solution)/shard_map/ppermute | solution.py:353
  103.8 14.8 %collective-permute-start.25 = (f32[4,128,128]{2,1,0:T(8,128)S(1)}, f32[4,128,128]{2,1,0:T(8,128)S(1)}, u32[]{:S(2)}, u32[]{:S(2)}) collective-permute-start(f32[4,128,128]{2,1,0:T(8,128)S(1)} %combine.67), channel_id=1, source_target_pairs={{0,16},{8,24},{16,0},{24,8},{1,17},{9,25},{17,1},{25,9},{2,18},{10... | collective-permute-start | bytes 786440 | tf_op jit(solution)/shard_map/ppermute | solution.py:355
  107.2 11.9 %collective-permute-start.28 = (f32[4,128,128]{2,1,0:T(8,128)S(1)}, f32[4,128,128]{2,1,0:T(8,128)S(1)}, u32[]{:S(2)}, u32[]{:S(2)}) collective-permute-start(f32[4,128,128]{2,1,0:T(8,128)S(1)} %combine.70), channel_id=1, source_target_pairs={{0,8},{8,0},{16,24},{24,16},{1,9},{9,1},{17,25},{25,17},{2,10},{10... | collective-permute-start | bytes 786440 | tf_op jit(solution)/shard_map/ppermute | solution.py:355
  108.8 11.3 %copy-start.11 = (f32[2,128,128]{2,1,0:T(8,128)}, f32[2,128,128]{2,1,0:T(8,128)S(1)}, u32[]{:S(2)}) copy-start(f32[2,128,128]{2,1,0:T(8,128)S(1)} %combine.62.refs_0_) | copy-start | bytes 393220
  108.8 5.0 %collective-permute-start.27 = (f32[2,128,128]{2,1,0:T(8,128)S(1)}, f32[2,128,128]{2,1,0:T(8,128)S(1)}, u32[]{:S(2)}, u32[]{:S(2)}) collective-permute-start(f32[2,128,128]{2,1,0:T(8,128)S(1)} %combine.62.refs_0_), channel_id=1, source_target_pairs={{0,2},{1,3},{2,0},{3,1},{4,6},{5,7},{6,4},{7,5},{8,10},{9,11},{10,... | collective-permute-start | bytes 393224 | tf_op jit(solution)/shard_map/ppermute | solution.py:353
  109.0 4.3 %collective-permute-start.26 = (f32[1,128,128]{2,1,0:T(8,128)S(1)}, f32[1,128,128]{2,1,0:T(8,128)S(1)}, u32[]{:S(2)}, u32[]{:S(2)}) collective-permute-start(f32[1,128,128]{2,1,0:T(8,128)S(1)} %combine.69), channel_id=1, source_target_pairs={{0,4},{1,5},{2,6},{3,7},{4,0},{5,1},{6,2},{7,3},{8,12},{9,13},{10,... | collective-permute-start | bytes 196616 | tf_op jit(solution)/shard_map/ppermute | solution.py:353
  113.8 6.2 %copy-start.15 = (f32[2,128,128]{2,1,0:T(8,128)}, f32[2,128,128]{2,1,0:T(8,128)S(1)}, u32[]{:S(2)}) copy-start(f32[2,128,128]{2,1,0:T(8,128)S(1)} %collective-permute-done.27.refs_1_.refs_7_) | copy-start | bytes 393220
  119.1 9.9 %collective-permute-start.29 = (f32[2,128,128]{2,1,0:T(8,128)S(1)}, f32[2,128,128]{2,1,0:T(8,128)S(1)}, u32[]{:S(2)}, u32[]{:S(2)}) collective-permute-start(f32[2,128,128]{2,1,0:T(8,128)S(1)} %combine.71), channel_id=1, source_target_pairs={{0,16},{8,24},{16,0},{24,8},{1,17},{9,25},{17,1},{25,9},{2,18},{10... | collective-permute-start | bytes 393224 | tf_op jit(solution)/shard_map/ppermute | solution.py:355
  125.8 0.8 copy-start.12
  126.7 0.9 copy-start.16
  127.6 22.4 %copy-start.1 = (bf16[64,128,256]{2,1,0:T(8,128)(2,1)S(1)}, bf16[64,128,256]{2,1,0:T(8,128)(2,1)}, u32[]{:S(2)}) copy-start(bf16[64,128,256]{2,1,0:T(8,128)(2,1)} %get-tuple-element.78.split) | copy-start | bytes 12582916
  127.6 22.4 %copy-start.13 = (f32[128,128]{1,0:T(8,128)S(1)}, f32[128,128]{1,0:T(8,128)}, u32[]{:S(2)}) copy-start(f32[128,128]{1,0:T(8,128)} %cell_cholesky.1.inverse) | copy-start | bytes 196612
  129.8 1.3 collective-permute-start.30
  131.1 4.3 %collective-permute-start.31 = (f32[1,128,128]{2,1,0:T(8,128)S(1)}, f32[1,128,128]{2,1,0:T(8,128)S(1)}, u32[]{:S(2)}, u32[]{:S(2)}) collective-permute-start(f32[1,128,128]{2,1,0:T(8,128)S(1)} %combine.76.refs_0_), channel_id=1, source_target_pairs={{0,2},{1,3},{2,0},{3,1},{4,6},{5,7},{6,4},{7,5},{8,10},{9,11},{10,... | collective-permute-start | bytes 196616 | tf_op jit(solution)/shard_map/ppermute | solution.py:353
  135.4 4.3 %collective-permute-start.32 = (f32[1,128,128]{2,1,0:T(8,128)S(1)}, f32[1,128,128]{2,1,0:T(8,128)S(1)}, u32[]{:S(2)}, u32[]{:S(2)}) collective-permute-start(f32[1,128,128]{2,1,0:T(8,128)S(1)} %combine.77.refs_0_), channel_id=1, source_target_pairs={{0,4},{1,5},{2,6},{3,7},{4,0},{5,1},{6,2},{7,3},{8,12},{9,13},{10,... | collective-permute-start | bytes 196616 | tf_op jit(solution)/shard_map/ppermute | solution.py:353
  139.8 4.9 %collective-permute-start.33 = (f32[1,128,128]{2,1,0:T(8,128)S(1)}, f32[1,128,128]{2,1,0:T(8,128)S(1)}, u32[]{:S(2)}, u32[]{:S(2)}) collective-permute-start(f32[1,128,128]{2,1,0:T(8,128)S(1)} %combine.78.refs_0_), channel_id=1, source_target_pairs={{0,8},{8,0},{16,24},{24,16},{1,9},{9,1},{17,25},{25,17},{2,10},{10... | collective-permute-start | bytes 196616 | tf_op jit(solution)/shard_map/ppermute | solution.py:355
  144.7 5.2 %collective-permute-start.34 = (f32[1,128,128]{2,1,0:T(8,128)S(1)}, f32[1,128,128]{2,1,0:T(8,128)S(1)}, u32[]{:S(2)}, u32[]{:S(2)}) collective-permute-start(f32[1,128,128]{2,1,0:T(8,128)S(1)} %combine.79.refs_0_), channel_id=1, source_target_pairs={{0,16},{8,24},{16,0},{24,8},{1,17},{9,25},{17,1},{25,9},{2,18},{10... | collective-permute-start | bytes 196616 | tf_op jit(solution)/shard_map/ppermute | solution.py:355

commit v5 on v4

--- a/solution.py
+++ b/solution.py
@@ -46,9 +46,10 @@
     devices = nx * ny
     me = lax.axis_index("gx") * ny + lax.axis_index("gy")
 
-    @pl.loop(0, slots.shape[0])
+    @pl.loop(0, slots.shape[0] // 16)
     def _(b):
-        slots[b] = -1
+        for j in range(16):
+            slots[b * 16 + j] = -1
 
     total = 0
     for first, each, far_first in pairs:
@@ -151,7 +152,6 @@
             pltpu.make_async_copy(sketch.at[cols[t]], sketch_v.at[t], sem_s.at[g]).start()
 
     zero(y_v)
-    zero(sums_v)
     found = list_tiles(nx, ny, pairs, owned, rows, cols, live, order, slots, list_row, list_tile, list_slot)
 
     @pl.loop(0, groups)
@@ -169,8 +169,13 @@
 
     gram_v[...] = jnp.zeros_like(gram_v)
 
-    @pl.loop(0, cell_blocks // 8)
+    turns = cell_blocks // 8
+    share = sums_v.shape[0] // turns
+
+    @pl.loop(0, turns)
     def _(b):
+        for j in range(share):
+            sums_v[b * share + j] = jnp.zeros(sums_v.shape[1:], sums_v.dtype)
         at = pl.ds(b * 8, 8)
         y = y_v[at]
         high = y.astype(jnp.bfloat16)
@@ -345,7 +350,7 @@
         return [pltpu.SMEM((blocks,), jnp.int32)] + [pltpu.SMEM((len(pairs) * room,), jnp.int32)] * 3
 
     def sums_scratch(pairs):
-        return pltpu.VMEM((sum(2 * each for _, each, _ in pairs) * devices + 1, side, wide), f32)
+        return pltpu.VMEM((sum(2 * each for _, each, _ in pairs) * devices + 8, side, wide), f32)
 
     def swap(value, bit):
         partner = 1 << bit

time: 158 us -> 156 us (0.987)
  starting transfers between devices: 38.5 us -> 35.3 us
  waiting for transfers between devices: 73.2 us -> 76.2 us
    ppermute x27, starting transfers between devices: 19.1 us -> 15.1 us  [swap(): return lax.ppermute(value, 'gy', [(i, i ^ partner) for i in range(ny)])]
    ppermute x27, waiting for transfers between devices: 50.9 us -> 52.9 us  [swap(): return lax.ppermute(value, 'gy', [(i, i ^ partner) for i in range(ny)])]
where the time goes in v5:
time: 156 us
  waiting for transfers between devices  76.2 us (49%)
  Pallas kernels  35.4 us (23%)
  starting transfers between devices  35.3 us (23%)
  local copies, waits for them, and re-layouts  7.09 us (5%)
  between operations  1.91 us (1%)
    ppermute x27, waiting for transfers between devices, swap(): return lax.ppermute(value, 'gy', [(i, i ^ partner) for i in range(ny)])  52.9 us
    ppermute x8, waiting for transfers between devices, swap(): return lax.ppermute(value, 'gx', [(i, i ^ partner) for i in range(nx)])  23.3 us
    ppermute x8, starting transfers between devices, swap(): return lax.ppermute(value, 'gx', [(i, i ^ partner) for i in range(nx)])  20.2 us
    ppermute x27, starting transfers between devices, swap(): return lax.ppermute(value, 'gy', [(i, i ^ partner) for i in range(ny)])  15.1 us
    pallas_call x1, Pallas kernels, on_device(): pl.pallas_call(functools.partial(first_kernel, nx, ny, early_pairs, owned...  13.9 us
    pallas_call x1, Pallas kernels, on_device(): pl.pallas_call(functools.partial(last_kernel, math.sqrt(genes), len(grams...  7.35 us
    unnamed x44, local copies, waits for them, and re-layouts  7.09 us
    pallas_call x1, Pallas kernels, cell_inverse(): pl.pallas_call(functools.partial(factor_kernel, math.sqrt(cells_all)), gr...  5.78 us
  transfers between devices with their start and end apart: 35, of which 22 were waited for; matrix products, arithmetic and copies ran while one was open for 0% of the time, Pallas kernels for 9%

profile of v5, /device:TPU:0, one launch (start us, length us, event | category | flops | bytes accessed | tf_op | source)
XLA Modules:
  0.0 155.9 jit_solution(8048150454854225986)
XLA Ops:
  1.3 13.9 %tile_products.1 = (f32[16,128,128]{2,1,0:T(8,128)}, f32[16,128,128]{2,1,0:T(8,128)}, f32[16,128,128]{2,1,0:T(8,128)}, f32[16,128,128]{2,1,0:T(8,128)}, f32[16,1...) custom-call(s32[192]{0:T(256)} %rows.3, s32[192]{0:T(256)} %cols.3, ...), custom_call_target="tpu_custom_call" | custom-call | flops 4000000000 | bytes 12000000 | tf_op jit(solution)/shard_map/tile_products/pallas_call | solution.py:362
  15.3 0.5 collective-permute-start.5
  15.9 0.4 collective-permute-start.2
  16.4 1.8 %collective-permute-done.4.refs_1_ = f32[16,128,128]{2,1,0:T(8,128)S(1)} collective-permute-done((f32[16,128,128]{2,1,0:T(8,128)}, f32[16,128,128]{2,1,0:T(8,128)S(1)}, u32[]{:S(2)}, u32[]{:S(2)}) %collective-permute-start.4) | collective-permute-done | bytes 1048608 | tf_op jit(solution)/shard_map/ppermute | solution.py:358
  18.1 0.1 collective-permute-start
  18.3 1.4 collective-permute-done.5.refs_1_
  19.6 1.2 copy-done.5
  20.9 0.1 combine.44
  21.0 3.5 %collective-permute-start.8 = (f32[16,128,128]{2,1,0:T(8,128)S(1)}, f32[16,128,128]{2,1,0:T(8,128)S(1)}, u32[]{:S(2)}, u32[]{:S(2)}) collective-permute-start(f32[16,128,128]{2,1,0:T(8,128)S(1)} %combine.44), channel_id=1, source_target_pairs={{0,2},{1,3},{2,0},{3,1},{4,6},{5,7},{6,4},{7,5},{8,10},{9,11},{10,... | collective-permute-start | bytes 3145736 | tf_op jit(solution)/shard_map/ppermute | solution.py:358
  24.6 1.2 copy-done.4
  25.8 0.1 combine.41
  25.9 2.1 %collective-permute-start.9 = (f32[16,128,128]{2,1,0:T(8,128)S(1)}, f32[16,128,128]{2,1,0:T(8,128)S(1)}, u32[]{:S(2)}, u32[]{:S(2)}) collective-permute-start(f32[16,128,128]{2,1,0:T(8,128)S(1)} %combine.41), channel_id=1, source_target_pairs={{0,4},{1,5},{2,6},{3,7},{4,0},{5,1},{6,2},{7,3},{8,12},{9,13},{10,... | collective-permute-start | bytes 3145736 | tf_op jit(solution)/shard_map/ppermute | solution.py:358
  28.0 0.1 combine.42.refs_4_
  28.2 2.7 %collective-permute-start.6 = (f32[17,128,128]{2,1,0:T(8,128)S(1)}, f32[17,128,128]{2,1,0:T(8,128)S(1)}, u32[]{:S(2)}, u32[]{:S(2)}) collective-permute-start(f32[17,128,128]{2,1,0:T(8,128)S(1)} %combine.42.refs_4_), channel_id=1, source_target_pairs={{0,8},{8,0},{16,24},{24,16},{1,9},{9,1},{17,25},{25,17},{2,10},{10... | collective-permute-start | bytes 3342344 | tf_op jit(solution)/shard_map/ppermute | solution.py:360
  30.9 0.3 collective-permute-start.1
  31.2 2.8 %copy-done.14 = bf16[192,128,128]{2,1,0:T(8,128)(2,1)S(1)} copy-done((bf16[192,128,128]{2,1,0:T(8,128)(2,1)S(1)}, bf16[192,128,128]{2,1,0:T(8,128)(2,1)}, u32[]{:S(2)}) %copy-start.14) | copy-done | bytes 6291480
  34.0 4.4 %late_products.1 = (f32[8,128,128]{2,1,0:T(8,128)S(1)}, f32[8,128,128]{2,1,0:T(8,128)S(1)}, f32[8,128,128]{2,1,0:T(8,128)S(1)}, f32[8,128,128]{2,1,0:T(8,128)S(1...) custom-call(s32[192]{0:T(256)S(1)} %copy-done.17, ...), custom_call_target="tpu_custom_call" | custom-call | flops 4000000000 | bytes 12000000 | tf_op jit(solution)/shard_map/late_products/pallas_call | solution.py:512
  38.5 9.6 %collective-permute-done.8.refs_1_ = f32[16,128,128]{2,1,0:T(8,128)S(1)} collective-permute-done((f32[16,128,128]{2,1,0:T(8,128)S(1)}, f32[16,128,128]{2,1,0:T(8,128)S(1)}, u32[]{:S(2)}, u32[]{:S(2)}) %collective-permute-start.8) | collective-permute-done | bytes 1048608 | tf_op jit(solution)/shard_map/ppermute | solution.py:358
  48.0 3.4 %collective-permute-done.9.refs_1_ = f32[16,128,128]{2,1,0:T(8,128)S(1)} collective-permute-done((f32[16,128,128]{2,1,0:T(8,128)S(1)}, f32[16,128,128]{2,1,0:T(8,128)S(1)}, u32[]{:S(2)}, u32[]{:S(2)}) %collective-permute-start.9) | collective-permute-done | bytes 1048608 | tf_op jit(solution)/shard_map/ppermute | solution.py:358
  51.5 0.1 combine.47.refs_0_
  51.7 1.8 %collective-permute-start.11 = (f32[8,128,128]{2,1,0:T(8,128)S(1)}, f32[8,128,128]{2,1,0:T(8,128)S(1)}, u32[]{:S(2)}, u32[]{:S(2)}) collective-permute-start(f32[8,128,128]{2,1,0:T(8,128)S(1)} %combine.48), channel_id=1, source_target_pairs={{0,4},{1,5},{2,6},{3,7},{4,0},{5,1},{6,2},{7,3},{8,12},{9,13},{10,... | collective-permute-start | bytes 1572872 | tf_op jit(solution)/shard_map/ppermute | solution.py:358
  53.5 0.1 combine.43.refs_0_
  53.7 0.2 collective-permute-start.12
  53.8 0.1 combine.40.refs_0_.refs_2_
  53.9 2.2 %collective-permute-done.6.refs_1_.refs_3_.refs_5_ = f32[17,128,128]{2,1,0:T(8,128)S(1)} collective-permute-done((f32[17,128,128]{2,1,0:T(8,128)S(1)}, f32[17,128,128]{2,1,0:T(8,128)S(1)}, u32[]{:S(2)}, u32[]{:S(2)}) %collective-permute-start.6) | collective-permute-done | bytes 1114144 | tf_op jit(solution)/shard_map/ppermute | solution.py:360
  56.2 6.7 %collective-permute-start.13 = (f32[9,128,128]{2,1,0:T(8,128)S(1)}, f32[9,128,128]{2,1,0:T(8,128)S(1)}, u32[]{:S(2)}, u32[]{:S(2)}) collective-permute-start(f32[9,128,128]{2,1,0:T(8,128)S(1)} %combine.49.refs_2_), channel_id=1, source_target_pairs={{0,16},{8,24},{16,0},{24,8},{1,17},{9,25},{17,1},{25,9},{2,18},{10... | collective-permute-start | bytes 1769480 | tf_op jit(solution)/shard_map/ppermute | solution.py:360
  62.9 0.4 collective-permute-start.17
  63.3 0.2 collective-permute-start.16
  63.6 2.9 %collective-permute-done.11.refs_1_ = f32[8,128,128]{2,1,0:T(8,128)S(1)} collective-permute-done((f32[8,128,128]{2,1,0:T(8,128)S(1)}, f32[8,128,128]{2,1,0:T(8,128)S(1)}, u32[]{:S(2)}, u32[]{:S(2)}) %collective-permute-start.11) | collective-permute-done | bytes 524320 | tf_op jit(solution)/shard_map/ppermute | solution.py:358
  66.5 2.0 %collective-permute-done.12.refs_3_ = f32[8,128,128]{2,1,0:T(8,128)S(1)} collective-permute-done((f32[8,128,128]{2,1,0:T(8,128)S(1)}, f32[8,128,128]{2,1,0:T(8,128)S(1)}, u32[]{:S(2)}, u32[]{:S(2)}) %collective-permute-start.12) | collective-permute-done | bytes 524320 | tf_op jit(solution)/shard_map/ppermute | solution.py:358
  68.6 8.7 %collective-permute-done.17.refs_1_ = f32[8,128,128]{2,1,0:T(8,128)S(1)} collective-permute-done((f32[8,128,128]{2,1,0:T(8,128)S(1)}, f32[8,128,128]{2,1,0:T(8,128)S(1)}, u32[]{:S(2)}, u32[]{:S(2)}) %collective-permute-start.17) | collective-permute-done | bytes 524320 | tf_op jit(solution)/shard_map/ppermute | solution.py:358
  77.3 1.7 %collective-permute-done.16.refs_1_ = f32[8,128,128]{2,1,0:T(8,128)S(1)} collective-permute-done((f32[8,128,128]{2,1,0:T(8,128)S(1)}, f32[8,128,128]{2,1,0:T(8,128)S(1)}, u32[]{:S(2)}, u32[]{:S(2)}) %collective-permute-start.16) | collective-permute-done | bytes 524320 | tf_op jit(solution)/shard_map/ppermute | solution.py:358
  79.0 9.9 %collective-permute-done.13.refs_1_.refs_3_ = f32[9,128,128]{2,1,0:T(8,128)S(1)} collective-permute-done((f32[9,128,128]{2,1,0:T(8,128)S(1)}, f32[9,128,128]{2,1,0:T(8,128)S(1)}, u32[]{:S(2)}, u32[]{:S(2)}) %collective-permute-start.13) | collective-permute-done | bytes 589856 | tf_op jit(solution)/shard_map/ppermute | solution.py:360
  88.9 0.8 collective-permute-start.18
  89.8 0.4 collective-permute-start.22
  90.5 2.1 %collective-permute-start.19 = (f32[2,128,128]{2,1,0:T(8,128)S(1)}, f32[2,128,128]{2,1,0:T(8,128)S(1)}, u32[]{:S(2)}, u32[]{:S(2)}) collective-permute-start(f32[2,128,128]{2,1,0:T(8,128)S(1)} %combine.56), channel_id=1, source_target_pairs={{0,2},{1,3},{2,0},{3,1},{4,6},{5,7},{6,4},{7,5},{8,10},{9,11},{10,... | collective-permute-start | bytes 393224 | tf_op jit(solution)/shard_map/ppermute | solution.py:358
  92.6 1.7 %collective-permute-start.20 = (f32[2,128,128]{2,1,0:T(8,128)S(1)}, f32[2,128,128]{2,1,0:T(8,128)S(1)}, u32[]{:S(2)}, u32[]{:S(2)}) collective-permute-start(f32[2,128,128]{2,1,0:T(8,128)S(1)} %combine.57), channel_id=1, source_target_pairs={{0,4},{1,5},{2,6},{3,7},{4,0},{5,1},{6,2},{7,3},{8,12},{9,13},{10,... | collective-permute-start | bytes 393224 | tf_op jit(solution)/shard_map/ppermute | solution.py:358
  94.4 6.4 %collective-permute-done.19.refs_1_ = f32[2,128,128]{2,1,0:T(8,128)S(1)} collective-permute-done((f32[2,128,128]{2,1,0:T(8,128)S(1)}, f32[2,128,128]{2,1,0:T(8,128)S(1)}, u32[]{:S(2)}, u32[]{:S(2)}) %collective-permute-start.19) | collective-permute-done | bytes 131104 | tf_op jit(solution)/shard_map/ppermute | solution.py:358
  100.9 1.2 collective-permute-done.20.refs_1_
  102.1 0.1 collective-permute-done.18.refs_1_.refs_3_
  102.2 3.3 %collective-permute-start.25 = (f32[4,128,128]{2,1,0:T(8,128)S(1)}, f32[4,128,128]{2,1,0:T(8,128)S(1)}, u32[]{:S(2)}, u32[]{:S(2)}) collective-permute-start(f32[4,128,128]{2,1,0:T(8,128)S(1)} %combine.67), channel_id=1, source_target_pairs={{0,16},{8,24},{16,0},{24,8},{1,17},{9,25},{17,1},{25,9},{2,18},{10... | collective-permute-start | bytes 786440 | tf_op jit(solution)/shard_map/ppermute | solution.py:360
  105.6 1.6 collective-permute-start.28
  107.2 0.2 collective-permute-start.27
  107.5 0.2 collective-permute-start.26
  107.8 4.0 %collective-permute-done.26.refs_5_ = f32[1,128,128]{2,1,0:T(8,128)S(1)} collective-permute-done((f32[1,128,128]{2,1,0:T(8,128)S(1)}, f32[1,128,128]{2,1,0:T(8,128)S(1)}, u32[]{:S(2)}, u32[]{:S(2)}) %collective-permute-start.26) | collective-permute-done | bytes 65568 | tf_op jit(solution)/shard_map/ppermute | solution.py:358
  111.8 0.4 collective-permute-done.27.refs_1_.refs_7_
  112.2 4.8 %collective-permute-done.25.refs_1_.refs_3_ = f32[4,128,128]{2,1,0:T(8,128)S(1)} collective-permute-done((f32[4,128,128]{2,1,0:T(8,128)S(1)}, f32[4,128,128]{2,1,0:T(8,128)S(1)}, u32[]{:S(2)}, u32[]{:S(2)}) %collective-permute-start.25) | collective-permute-done | bytes 262176 | tf_op jit(solution)/shard_map/ppermute | solution.py:360
  117.0 0.5 collective-permute-done.28.refs_1_.refs_3_
  117.5 0.9 collective-permute-start.29
  118.5 5.8 %cell_cholesky.1.inverse = f32[128,128]{1,0:T(8,128)} custom-call(f32[2,128,128]{2,1,0:T(8,128)} %copy-done.11, f32[2,128,128]{2,1,0:T(8,128)} %copy-done.15), custom_call_target="tpu_custom_call" | custom-call | flops 1500000000 | bytes 4500000 | tf_op jit(solution)/shard_map/cell_cholesky/pallas_call | solution.py:534
  124.2 0.8 copy-done.12
  125.1 0.9 copy-done.16
  126.0 1.5 owned_gram.2
  127.5 0.7 owned_gram.3
  128.3 1.2 collective-permute-done.30.refs_1_
  129.5 0.2 collective-permute-start.31
  129.7 4.1 %collective-permute-done.31.refs_1_ = f32[1,128,128]{2,1,0:T(8,128)S(1)} collective-permute-done((f32[1,128,128]{2,1,0:T(8,128)S(1)}, f32[1,128,128]{2,1,0:T(8,128)S(1)}, u32[]{:S(2)}, u32[]{:S(2)}) %collective-permute-start.31) | collective-permute-done | bytes 65568 | tf_op jit(solution)/shard_map/ppermute | solution.py:358
  133.9 0.4 collective-permute-start.32
  134.2 4.0 %collective-permute-done.32.refs_1_ = f32[1,128,128]{2,1,0:T(8,128)S(1)} collective-permute-done((f32[1,128,128]{2,1,0:T(8,128)S(1)}, f32[1,128,128]{2,1,0:T(8,128)S(1)}, u32[]{:S(2)}, u32[]{:S(2)}) %collective-permute-start.32) | collective-permute-done | bytes 65568 | tf_op jit(solution)/shard_map/ppermute | solution.py:358
  138.2 2.7 %collective-permute-start.33 = (f32[1,128,128]{2,1,0:T(8,128)S(1)}, f32[1,128,128]{2,1,0:T(8,128)S(1)}, u32[]{:S(2)}, u32[]{:S(2)}) collective-permute-start(f32[1,128,128]{2,1,0:T(8,128)S(1)} %combine.78.refs_0_), channel_id=1, source_target_pairs={{0,8},{8,0},{16,24},{24,16},{1,9},{9,1},{17,25},{25,17},{2,10},{10... | collective-permute-start | bytes 196616 | tf_op jit(solution)/shard_map/ppermute | solution.py:360
  140.9 2.2 %collective-permute-done.33.refs_1_ = f32[1,128,128]{2,1,0:T(8,128)S(1)} collective-permute-done((f32[1,128,128]{2,1,0:T(8,128)S(1)}, f32[1,128,128]{2,1,0:T(8,128)S(1)}, u32[]{:S(2)}, u32[]{:S(2)}) %collective-permute-start.33) | collective-permute-done | bytes 65568 | tf_op jit(solution)/shard_map/ppermute | solution.py:360
  143.1 1.5 collective-permute-start.34
  144.7 3.7 %collective-permute-done.34.refs_1_ = f32[1,128,128]{2,1,0:T(8,128)S(1)} collective-permute-done((f32[1,128,128]{2,1,0:T(8,128)S(1)}, f32[1,128,128]{2,1,0:T(8,128)S(1)}, u32[]{:S(2)}, u32[]{:S(2)}) %collective-permute-start.34) | collective-permute-done | bytes 65568 | tf_op jit(solution)/shard_map/ppermute | solution.py:360
  148.4 7.4 %factors.1 = (f32[1024,128]{1,0:T(8,128)}, bf16[8192,128]{1,0:T(8,128)(2,1)}) custom-call(bf16[64,128,256]{2,1,0:T(8,128)(2,1)S(1)} %copy-done.1, f32[128,128]{1,0:T(8,128)S(1)} %copy-done.13, f32[1,128,128]{2,1,0:T(8,128)S(1)} %combine.79.refs_0_, f32[1,128,128]{2,1,0:T(8,128)S(1)} %collective-permute-done.34.refs_1_, ...), custom_call_target="tpu_custom_call" | custom-call | tf_op jit(solution)/shard_map/factors/pallas_call | solution.py:593
  (96 shorter events, 1.6 us)
Async XLA Ops:
  15.2 2.9 %collective-permute-start.4 = (f32[16,128,128]{2,1,0:T(8,128)}, f32[16,128,128]{2,1,0:T(8,128)S(1)}, u32[]{:S(2)}, u32[]{:S(2)}) collective-permute-start(f32[16,128,128]{2,1,0:T(8,128)} %get-tuple-element.68), channel_id=1, source_target_pairs={{0,1},{1,0},{2,3},{3,2},{4,5},{5,4},{6,7},{7,6},{8,9},{9,8},{10,11... | collective-permute-start | bytes 3145736 | tf_op jit(solution)/shard_map/ppermute | solution.py:358
  15.3 4.4 %collective-permute-start.5 = (f32[16,128,128]{2,1,0:T(8,128)}, f32[16,128,128]{2,1,0:T(8,128)S(1)}, u32[]{:S(2)}, u32[]{:S(2)}) collective-permute-start(f32[16,128,128]{2,1,0:T(8,128)} %get-tuple-element.69), channel_id=1, source_target_pairs={{0,1},{1,0},{2,3},{3,2},{4,5},{5,4},{6,7},{7,6},{8,9},{9,8},{10,11... | collective-permute-start | bytes 3145736 | tf_op jit(solution)/shard_map/ppermute | solution.py:358
  15.8 10.1 %collective-permute-start.3 = (f32[8,128,128]{2,1,0:T(8,128)}, f32[8,128,128]{2,1,0:T(8,128)S(1)}, u32[]{:S(2)}, u32[]{:S(2)}) collective-permute-start(f32[8,128,128]{2,1,0:T(8,128)} %get-tuple-element.66), channel_id=1, source_target_pairs={{0,1},{1,0},{2,3},{3,2},{4,5},{5,4},{6,7},{7,6},{8,9},{9,8},{10,11... | collective-permute-start | bytes 1572872 | tf_op jit(solution)/shard_map/ppermute | solution.py:358
  15.9 12.1 %collective-permute-start.2 = (f32[9,128,128]{2,1,0:T(8,128)}, f32[9,128,128]{2,1,0:T(8,128)S(1)}, u32[]{:S(2)}, u32[]{:S(2)}) collective-permute-start(f32[9,128,128]{2,1,0:T(8,128)} %get-tuple-element.65.refs_4_), channel_id=1, source_target_pairs={{0,1},{1,0},{2,3},{3,2},{4,5},{5,4},{6,7},{7,6},{8,9},{9,8},{10,11... | collective-permute-start | bytes 1769480 | tf_op jit(solution)/shard_map/ppermute | solution.py:358
  16.3 14.6 %collective-permute-start.10 = (f32[16,128,128]{2,1,0:T(8,128)}, f32[16,128,128]{2,1,0:T(8,128)S(1)}, u32[]{:S(2)}, u32[]{:S(2)}) collective-permute-start(f32[16,128,128]{2,1,0:T(8,128)} %get-tuple-element.83), channel_id=1, source_target_pairs={{0,1},{1,0},{2,3},{3,2},{4,5},{5,4},{6,7},{7,6},{8,9},{9,8},{10,11... | collective-permute-start | bytes 3145736 | tf_op jit(solution)/shard_map/ppermute | solution.py:358
  18.1 10.0 %collective-permute-start = (f32[8,128,128]{2,1,0:T(8,128)}, f32[8,128,128]{2,1,0:T(8,128)S(1)}, u32[]{:S(2)}, u32[]{:S(2)}) collective-permute-start(f32[8,128,128]{2,1,0:T(8,128)} %get-tuple-element.61), channel_id=1, source_target_pairs={{0,1},{1,0},{2,3},{3,2},{4,5},{5,4},{6,7},{7,6},{8,9},{9,8},{10,11... | collective-permute-start | bytes 1572872 | tf_op jit(solution)/shard_map/ppermute | solution.py:358
  19.6 1.2 copy-start.5
  20.9 7.1 %copy-start.20 = (f32[16,128,128]{2,1,0:T(8,128)S(1)}, f32[16,128,128]{2,1,0:T(8,128)}, u32[]{:S(2)}) copy-start(f32[16,128,128]{2,1,0:T(8,128)} %get-tuple-element.75) | copy-start | bytes 3145732
  20.9 7.1 %copy-start.6 = (f32[9,128,128]{2,1,0:T(8,128)S(1)}, f32[9,128,128]{2,1,0:T(8,128)}, u32[]{:S(2)}) copy-start(f32[9,128,128]{2,1,0:T(8,128)} %get-tuple-element.65.refs_4_) | copy-start | bytes 1769476
  20.9 7.1 %copy-start.7 = (f32[8,128,128]{2,1,0:T(8,128)S(1)}, f32[8,128,128]{2,1,0:T(8,128)}, u32[]{:S(2)}) copy-start(f32[8,128,128]{2,1,0:T(8,128)} %get-tuple-element.64.refs_0_) | copy-start | bytes 1572868
  20.9 7.2 %copy-start.8 = (f32[8,128,128]{2,1,0:T(8,128)S(1)}, f32[8,128,128]{2,1,0:T(8,128)}, u32[]{:S(2)}) copy-start(f32[8,128,128]{2,1,0:T(8,128)} %get-tuple-element.72.refs_2_) | copy-start | bytes 1572868
  20.9 10.3 %copy-start.17 = (s32[192]{0:T(256)S(1)}, s32[192]{0:T(256)}, u32[]{:S(2)}) copy-start(s32[192]{0:T(256)} %rows.3) | copy-start | bytes 2308
  20.9 10.3 %copy-start.18 = (s32[192]{0:T(256)S(1)}, s32[192]{0:T(256)}, u32[]{:S(2)}) copy-start(s32[192]{0:T(256)} %cols.3) | copy-start | bytes 2308
  20.9 10.3 %copy-start.19 = (s32[256]{0:T(256)S(1)}, s32[256]{0:T(256)}, u32[]{:S(2)}) copy-start(s32[256]{0:T(256)} %order.3) | copy-start | bytes 3076
  21.0 10.1 %copy-start = (bf16[64,128,256]{2,1,0:T(8,128)(2,1)S(1)}, bf16[64,128,256]{2,1,0:T(8,128)(2,1)}, u32[]{:S(2)}) copy-start(bf16[64,128,256]{2,1,0:T(8,128)(2,1)} %get-tuple-element.78.split) | copy-start | bytes 12582916
  21.0 27.0 %collective-permute-start.8 = (f32[16,128,128]{2,1,0:T(8,128)S(1)}, f32[16,128,128]{2,1,0:T(8,128)S(1)}, u32[]{:S(2)}, u32[]{:S(2)}) collective-permute-start(f32[16,128,128]{2,1,0:T(8,128)S(1)} %combine.44), channel_id=1, source_target_pairs={{0,2},{1,3},{2,0},{3,1},{4,6},{5,7},{6,4},{7,5},{8,10},{9,11},{10,... | collective-permute-start | bytes 3145736 | tf_op jit(solution)/shard_map/ppermute | solution.py:358
  24.6 1.2 copy-start.4
  25.8 5.1 %copy-start.21 = (f32[8,128,128]{2,1,0:T(8,128)S(1)}, f32[8,128,128]{2,1,0:T(8,128)}, u32[]{:S(2)}) copy-start(f32[8,128,128]{2,1,0:T(8,128)} %get-tuple-element.63) | copy-start | bytes 1572868
  25.9 25.6 %collective-permute-start.9 = (f32[16,128,128]{2,1,0:T(8,128)S(1)}, f32[16,128,128]{2,1,0:T(8,128)S(1)}, u32[]{:S(2)}, u32[]{:S(2)}) collective-permute-start(f32[16,128,128]{2,1,0:T(8,128)S(1)} %combine.41), channel_id=1, source_target_pairs={{0,4},{1,5},{2,6},{3,7},{4,0},{5,1},{6,2},{7,3},{8,12},{9,13},{10,... | collective-permute-start | bytes 3145736 | tf_op jit(solution)/shard_map/ppermute | solution.py:358
  28.0 23.7 %collective-permute-start.7 = (f32[16,128,128]{2,1,0:T(8,128)S(1)}, f32[16,128,128]{2,1,0:T(8,128)S(1)}, u32[]{:S(2)}, u32[]{:S(2)}) collective-permute-start(f32[16,128,128]{2,1,0:T(8,128)S(1)} %copy-done.20), channel_id=1, source_target_pairs={{0,1},{1,0},{2,3},{3,2},{4,5},{5,4},{6,7},{7,6},{8,9},{9,8},{10,11... | collective-permute-start | bytes 3145736 | tf_op jit(solution)/shard_map/ppermute | solution.py:358
  28.2 27.9 %collective-permute-start.6 = (f32[17,128,128]{2,1,0:T(8,128)S(1)}, f32[17,128,128]{2,1,0:T(8,128)S(1)}, u32[]{:S(2)}, u32[]{:S(2)}) collective-permute-start(f32[17,128,128]{2,1,0:T(8,128)S(1)} %combine.42.refs_4_), channel_id=1, source_target_pairs={{0,8},{8,0},{16,24},{24,16},{1,9},{9,1},{17,25},{25,17},{2,10},{10... | collective-permute-start | bytes 3342344 | tf_op jit(solution)/shard_map/ppermute | solution.py:360
  30.9 20.6 %copy-start.3 = (f32[16,128,128]{2,1,0:T(8,128)S(1)}, f32[16,128,128]{2,1,0:T(8,128)}, u32[]{:S(2)}) copy-start(f32[16,128,128]{2,1,0:T(8,128)} %get-tuple-element.82.refs_0_) | copy-start | bytes 3145732
  30.9 22.7 %collective-permute-start.1 = (f32[8,128,128]{2,1,0:T(8,128)S(1)}, f32[8,128,128]{2,1,0:T(8,128)S(1)}, u32[]{:S(2)}, u32[]{:S(2)}) collective-permute-start(f32[8,128,128]{2,1,0:T(8,128)S(1)} %copy-done.21), channel_id=1, source_target_pairs={{0,1},{1,0},{2,3},{3,2},{4,5},{5,4},{6,7},{7,6},{8,9},{9,8},{10,11... | collective-permute-start | bytes 1572872 | tf_op jit(solution)/shard_map/ppermute | solution.py:358
  31.2 2.8 %copy-start.14 = (bf16[192,128,128]{2,1,0:T(8,128)(2,1)S(1)}, bf16[192,128,128]{2,1,0:T(8,128)(2,1)}, u32[]{:S(2)}) copy-start(bf16[192,128,128]{2,1,0:T(8,128)(2,1)} %tiles.3) | copy-start | bytes 18874372
  38.4 15.0 %copy-start.2 = (f32[16,128,128]{2,1,0:T(8,128)S(1)}, f32[16,128,128]{2,1,0:T(8,128)}, u32[]{:S(2)}) copy-start(f32[16,128,128]{2,1,0:T(8,128)} %get-tuple-element.74.refs_0_) | copy-start | bytes 3145732
  48.0 14.8 %collective-permute-start.14 = (f32[8,128,128]{2,1,0:T(8,128)S(1)}, f32[8,128,128]{2,1,0:T(8,128)S(1)}, u32[]{:S(2)}, u32[]{:S(2)}) collective-permute-start(f32[8,128,128]{2,1,0:T(8,128)S(1)} %get-tuple-element.86), channel_id=1, source_target_pairs={{0,1},{1,0},{2,3},{3,2},{4,5},{5,4},{6,7},{7,6},{8,9},{9,8},{10,11... | collective-permute-start | bytes 1572872 | tf_op jit(solution)/shard_map/ppermute | solution.py:358
  51.5 11.4 %collective-permute-start.15 = (f32[8,128,128]{2,1,0:T(8,128)S(1)}, f32[8,128,128]{2,1,0:T(8,128)S(1)}, u32[]{:S(2)}, u32[]{:S(2)}) collective-permute-start(f32[8,128,128]{2,1,0:T(8,128)S(1)} %get-tuple-element.87), channel_id=1, source_target_pairs={{0,1},{1,0},{2,3},{3,2},{4,5},{5,4},{6,7},{7,6},{8,9},{9,8},{10,11... | collective-permute-start | bytes 1572872 | tf_op jit(solution)/shard_map/ppermute | solution.py:358
  51.6 2.2 %copy-start.9 = (f32[8,128,128]{2,1,0:T(8,128)S(1)}, f32[8,128,128]{2,1,0:T(8,128)}, u32[]{:S(2)}) copy-start(f32[8,128,128]{2,1,0:T(8,128)} %get-tuple-element.60.refs_0_) | copy-start | bytes 1572868
  51.6 2.2 %copy-start.10 = (f32[8,128,128]{2,1,0:T(8,128)S(1)}, f32[8,128,128]{2,1,0:T(8,128)}, u32[]{:S(2)}) copy-start(f32[8,128,128]{2,1,0:T(8,128)} %get-tuple-element.62.refs_2_) | copy-start | bytes 1572868
  51.7 14.8 %collective-permute-start.11 = (f32[8,128,128]{2,1,0:T(8,128)S(1)}, f32[8,128,128]{2,1,0:T(8,128)S(1)}, u32[]{:S(2)}, u32[]{:S(2)}) collective-permute-start(f32[8,128,128]{2,1,0:T(8,128)S(1)} %combine.48), channel_id=1, source_target_pairs={{0,4},{1,5},{2,6},{3,7},{4,0},{5,1},{6,2},{7,3},{8,12},{9,13},{10,... | collective-permute-start | bytes 1572872 | tf_op jit(solution)/shard_map/ppermute | solution.py:358
  53.7 14.8 %collective-permute-start.12 = (f32[8,128,128]{2,1,0:T(8,128)S(1)}, f32[8,128,128]{2,1,0:T(8,128)S(1)}, u32[]{:S(2)}, u32[]{:S(2)}) collective-permute-start(f32[8,128,128]{2,1,0:T(8,128)S(1)} %combine.45), channel_id=1, source_target_pairs={{0,2},{1,3},{2,0},{3,1},{4,6},{5,7},{6,4},{7,5},{8,10},{9,11},{10,... | collective-permute-start | bytes 1572872 | tf_op jit(solution)/shard_map/ppermute | solution.py:358
  56.2 32.7 %collective-permute-start.13 = (f32[9,128,128]{2,1,0:T(8,128)S(1)}, f32[9,128,128]{2,1,0:T(8,128)S(1)}, u32[]{:S(2)}, u32[]{:S(2)}) collective-permute-start(f32[9,128,128]{2,1,0:T(8,128)S(1)} %combine.49.refs_2_), channel_id=1, source_target_pairs={{0,16},{8,24},{16,0},{24,8},{1,17},{9,25},{17,1},{25,9},{2,18},{10... | collective-permute-start | bytes 1769480 | tf_op jit(solution)/shard_map/ppermute | solution.py:360
  62.9 14.4 %collective-permute-start.17 = (f32[8,128,128]{2,1,0:T(8,128)S(1)}, f32[8,128,128]{2,1,0:T(8,128)S(1)}, u32[]{:S(2)}, u32[]{:S(2)}) collective-permute-start(f32[8,128,128]{2,1,0:T(8,128)S(1)} %combine.51), channel_id=1, source_target_pairs={{0,4},{1,5},{2,6},{3,7},{4,0},{5,1},{6,2},{7,3},{8,12},{9,13},{10,... | collective-permute-start | bytes 1572872 | tf_op jit(solution)/shard_map/ppermute | solution.py:358
  63.3 15.7 %collective-permute-start.16 = (f32[8,128,128]{2,1,0:T(8,128)S(1)}, f32[8,128,128]{2,1,0:T(8,128)S(1)}, u32[]{:S(2)}, u32[]{:S(2)}) collective-permute-start(f32[8,128,128]{2,1,0:T(8,128)S(1)} %combine.50), channel_id=1, source_target_pairs={{0,2},{1,3},{2,0},{3,1},{4,6},{5,7},{6,4},{7,5},{8,10},{9,11},{10,... | collective-permute-start | bytes 1572872 | tf_op jit(solution)/shard_map/ppermute | solution.py:358
  66.5 23.3 %collective-permute-start.21 = (f32[8,128,128]{2,1,0:T(8,128)S(1)}, f32[8,128,128]{2,1,0:T(8,128)S(1)}, u32[]{:S(2)}, u32[]{:S(2)}) collective-permute-start(f32[8,128,128]{2,1,0:T(8,128)S(1)} %get-tuple-element.94), channel_id=1, source_target_pairs={{0,1},{1,0},{2,3},{3,2},{4,5},{5,4},{6,7},{7,6},{8,9},{9,8},{10,11... | collective-permute-start | bytes 1572872 | tf_op jit(solution)/shard_map/ppermute | solution.py:358
  68.5 21.7 %collective-permute-start.23 = (f32[8,128,128]{2,1,0:T(8,128)S(1)}, f32[8,128,128]{2,1,0:T(8,128)S(1)}, u32[]{:S(2)}, u32[]{:S(2)}) collective-permute-start(f32[8,128,128]{2,1,0:T(8,128)S(1)} %get-tuple-element.97), channel_id=1, source_target_pairs={{0,1},{1,0},{2,3},{3,2},{4,5},{5,4},{6,7},{7,6},{8,9},{9,8},{10,11... | collective-permute-start | bytes 1572872 | tf_op jit(solution)/shard_map/ppermute | solution.py:358
  88.9 13.3 %collective-permute-start.18 = (f32[8,128,128]{2,1,0:T(8,128)S(1)}, f32[8,128,128]{2,1,0:T(8,128)S(1)}, u32[]{:S(2)}, u32[]{:S(2)}) collective-permute-start(f32[8,128,128]{2,1,0:T(8,128)S(1)} %combine.55), channel_id=1, source_target_pairs={{0,8},{8,0},{16,24},{24,16},{1,9},{9,1},{17,25},{25,17},{2,10},{10... | collective-permute-start | bytes 1572872 | tf_op jit(solution)/shard_map/ppermute | solution.py:360
  89.8 12.2 %collective-permute-start.22 = (f32[5,128,128]{2,1,0:T(8,128)S(1)}, f32[5,128,128]{2,1,0:T(8,128)S(1)}, u32[]{:S(2)}, u32[]{:S(2)}) collective-permute-start(f32[5,128,128]{2,1,0:T(8,128)S(1)} %combine.59.refs_2_), channel_id=1, source_target_pairs={{0,4},{1,5},{2,6},{3,7},{4,0},{5,1},{6,2},{7,3},{8,12},{9,13},{10,... | collective-permute-start | bytes 983048 | tf_op jit(solution)/shard_map/ppermute | solution.py:358
  90.3 11.7 %collective-permute-start.24 = (f32[4,128,128]{2,1,0:T(8,128)S(1)}, f32[4,128,128]{2,1,0:T(8,128)S(1)}, u32[]{:S(2)}, u32[]{:S(2)}) collective-permute-start(f32[4,128,128]{2,1,0:T(8,128)S(1)} %combine.61), channel_id=1, source_target_pairs={{0,2},{1,3},{2,0},{3,1},{4,6},{5,7},{6,4},{7,5},{8,10},{9,11},{10,... | collective-permute-start | bytes 786440 | tf_op jit(solution)/shard_map/ppermute | solution.py:358
  90.5 10.4 %collective-permute-start.19 = (f32[2,128,128]{2,1,0:T(8,128)S(1)}, f32[2,128,128]{2,1,0:T(8,128)S(1)}, u32[]{:S(2)}, u32[]{:S(2)}) collective-permute-start(f32[2,128,128]{2,1,0:T(8,128)S(1)} %combine.56), channel_id=1, source_target_pairs={{0,2},{1,3},{2,0},{3,1},{4,6},{5,7},{6,4},{7,5},{8,10},{9,11},{10,... | collective-permute-start | bytes 393224 | tf_op jit(solution)/shard_map/ppermute | solution.py:358
  92.6 9.5 %collective-permute-start.20 = (f32[2,128,128]{2,1,0:T(8,128)S(1)}, f32[2,128,128]{2,1,0:T(8,128)S(1)}, u32[]{:S(2)}, u32[]{:S(2)}) collective-permute-start(f32[2,128,128]{2,1,0:T(8,128)S(1)} %combine.57), channel_id=1, source_target_pairs={{0,4},{1,5},{2,6},{3,7},{4,0},{5,1},{6,2},{7,3},{8,12},{9,13},{10,... | collective-permute-start | bytes 393224 | tf_op jit(solution)/shard_map/ppermute | solution.py:358
  102.2 14.8 %collective-permute-start.25 = (f32[4,128,128]{2,1,0:T(8,128)S(1)}, f32[4,128,128]{2,1,0:T(8,128)S(1)}, u32[]{:S(2)}, u32[]{:S(2)}) collective-permute-start(f32[4,128,128]{2,1,0:T(8,128)S(1)} %combine.67), channel_id=1, source_target_pairs={{0,16},{8,24},{16,0},{24,8},{1,17},{9,25},{17,1},{25,9},{2,18},{10... | collective-permute-start | bytes 786440 | tf_op jit(solution)/shard_map/ppermute | solution.py:360
  105.6 11.9 %collective-permute-start.28 = (f32[4,128,128]{2,1,0:T(8,128)S(1)}, f32[4,128,128]{2,1,0:T(8,128)S(1)}, u32[]{:S(2)}, u32[]{:S(2)}) collective-permute-start(f32[4,128,128]{2,1,0:T(8,128)S(1)} %combine.70), channel_id=1, source_target_pairs={{0,8},{8,0},{16,24},{24,16},{1,9},{9,1},{17,25},{25,17},{2,10},{10... | collective-permute-start | bytes 786440 | tf_op jit(solution)/shard_map/ppermute | solution.py:360
  107.2 11.3 %copy-start.11 = (f32[2,128,128]{2,1,0:T(8,128)}, f32[2,128,128]{2,1,0:T(8,128)S(1)}, u32[]{:S(2)}) copy-start(f32[2,128,128]{2,1,0:T(8,128)S(1)} %combine.62.refs_0_) | copy-start | bytes 393220
  107.2 5.0 %collective-permute-start.27 = (f32[2,128,128]{2,1,0:T(8,128)S(1)}, f32[2,128,128]{2,1,0:T(8,128)S(1)}, u32[]{:S(2)}, u32[]{:S(2)}) collective-permute-start(f32[2,128,128]{2,1,0:T(8,128)S(1)} %combine.62.refs_0_), channel_id=1, source_target_pairs={{0,2},{1,3},{2,0},{3,1},{4,6},{5,7},{6,4},{7,5},{8,10},{9,11},{10,... | collective-permute-start | bytes 393224 | tf_op jit(solution)/shard_map/ppermute | solution.py:358
  107.5 4.3 %collective-permute-start.26 = (f32[1,128,128]{2,1,0:T(8,128)S(1)}, f32[1,128,128]{2,1,0:T(8,128)S(1)}, u32[]{:S(2)}, u32[]{:S(2)}) collective-permute-start(f32[1,128,128]{2,1,0:T(8,128)S(1)} %combine.69), channel_id=1, source_target_pairs={{0,4},{1,5},{2,6},{3,7},{4,0},{5,1},{6,2},{7,3},{8,12},{9,13},{10,... | collective-permute-start | bytes 196616 | tf_op jit(solution)/shard_map/ppermute | solution.py:358
  112.2 6.2 %copy-start.15 = (f32[2,128,128]{2,1,0:T(8,128)}, f32[2,128,128]{2,1,0:T(8,128)S(1)}, u32[]{:S(2)}) copy-start(f32[2,128,128]{2,1,0:T(8,128)S(1)} %collective-permute-done.27.refs_1_.refs_7_) | copy-start | bytes 393220
  117.5 9.9 %collective-permute-start.29 = (f32[2,128,128]{2,1,0:T(8,128)S(1)}, f32[2,128,128]{2,1,0:T(8,128)S(1)}, u32[]{:S(2)}, u32[]{:S(2)}) collective-permute-start(f32[2,128,128]{2,1,0:T(8,128)S(1)} %combine.71), channel_id=1, source_target_pairs={{0,16},{8,24},{16,0},{24,8},{1,17},{9,25},{17,1},{25,9},{2,18},{10... | collective-permute-start | bytes 393224 | tf_op jit(solution)/shard_map/ppermute | solution.py:360
  124.2 0.8 copy-start.12
  125.1 0.9 copy-start.16
  126.0 22.4 %copy-start.1 = (bf16[64,128,256]{2,1,0:T(8,128)(2,1)S(1)}, bf16[64,128,256]{2,1,0:T(8,128)(2,1)}, u32[]{:S(2)}) copy-start(bf16[64,128,256]{2,1,0:T(8,128)(2,1)} %get-tuple-element.78.split) | copy-start | bytes 12582916
  126.0 22.4 %copy-start.13 = (f32[128,128]{1,0:T(8,128)S(1)}, f32[128,128]{1,0:T(8,128)}, u32[]{:S(2)}) copy-start(f32[128,128]{1,0:T(8,128)} %cell_cholesky.1.inverse) | copy-start | bytes 196612
  128.2 1.3 collective-permute-start.30
  129.5 4.3 %collective-permute-start.31 = (f32[1,128,128]{2,1,0:T(8,128)S(1)}, f32[1,128,128]{2,1,0:T(8,128)S(1)}, u32[]{:S(2)}, u32[]{:S(2)}) collective-permute-start(f32[1,128,128]{2,1,0:T(8,128)S(1)} %combine.76.refs_0_), channel_id=1, source_target_pairs={{0,2},{1,3},{2,0},{3,1},{4,6},{5,7},{6,4},{7,5},{8,10},{9,11},{10,... | collective-permute-start | bytes 196616 | tf_op jit(solution)/shard_map/ppermute | solution.py:358
  133.9 4.3 %collective-permute-start.32 = (f32[1,128,128]{2,1,0:T(8,128)S(1)}, f32[1,128,128]{2,1,0:T(8,128)S(1)}, u32[]{:S(2)}, u32[]{:S(2)}) collective-permute-start(f32[1,128,128]{2,1,0:T(8,128)S(1)} %combine.77.refs_0_), channel_id=1, source_target_pairs={{0,4},{1,5},{2,6},{3,7},{4,0},{5,1},{6,2},{7,3},{8,12},{9,13},{10,... | collective-permute-start | bytes 196616 | tf_op jit(solution)/shard_map/ppermute | solution.py:358
  138.2 4.9 %collective-permute-start.33 = (f32[1,128,128]{2,1,0:T(8,128)S(1)}, f32[1,128,128]{2,1,0:T(8,128)S(1)}, u32[]{:S(2)}, u32[]{:S(2)}) collective-permute-start(f32[1,128,128]{2,1,0:T(8,128)S(1)} %combine.78.refs_0_), channel_id=1, source_target_pairs={{0,8},{8,0},{16,24},{24,16},{1,9},{9,1},{17,25},{25,17},{2,10},{10... | collective-permute-start | bytes 196616 | tf_op jit(solution)/shard_map/ppermute | solution.py:360
  143.1 5.2 %collective-permute-start.34 = (f32[1,128,128]{2,1,0:T(8,128)S(1)}, f32[1,128,128]{2,1,0:T(8,128)S(1)}, u32[]{:S(2)}, u32[]{:S(2)}) collective-permute-start(f32[1,128,128]{2,1,0:T(8,128)S(1)} %combine.79.refs_0_), channel_id=1, source_target_pairs={{0,16},{8,24},{16,0},{24,8},{1,17},{9,25},{17,1},{25,9},{2,18},{10... | collective-permute-start | bytes 196616 | tf_op jit(solution)/shard_map/ppermute | solution.py:360

commit v6 on v5

--- a/solution.py
+++ b/solution.py
@@ -107,9 +107,12 @@
 
 
 def zero(ref):
-    @pl.loop(0, ref.shape[0])
+    many = max(d for d in range(1, 9) if ref.shape[0] % d == 0)
+
+    @pl.loop(0, ref.shape[0] // many)
     def _(b):
-        ref[b] = jnp.zeros(ref.shape[1:], ref.dtype)
+        for j in range(many):
+            ref[b * many + j] = jnp.zeros(ref.shape[1:], ref.dtype)
 
 
 def add_and_save(pairs, found, list_row, list_tile, list_slot, tiles_v, split_v, sums_v, pieces, sem):

time: 156 us -> 156 us (level)
  starting transfers between devices: 35.3 us -> 40.3 us
  waiting for transfers between devices: 76.2 us -> 71.9 us
    ppermute x27, starting transfers between devices: 15.1 us -> 20.3 us  [swap(): return lax.ppermute(value, 'gy', [(i, i ^ partner) for i in range(ny)])]
    ppermute x27, waiting for transfers between devices: 52.9 us -> 48.4 us  [swap(): return lax.ppermute(value, 'gy', [(i, i ^ partner) for i in range(ny)])]
  transfers between devices with their start and end apart: 35 -> 35, of which waited for: 22 -> 21; matrix products, arithmetic and copies ran while one was open for 0% -> 0% of each run, Pallas kernels for 9% -> 8%
where the time goes in v6:
time: 156 us; the launch traced here: 155 us
  waiting for transfers between devices  71.9 us (46%)
  starting transfers between devices  40.3 us (26%)
  Pallas kernels  34.2 us (22%)
  local copies, waits for them, and re-layouts  7.09 us (5%)
  between operations  1.89 us (1%)
    ppermute x27, waiting for transfers between devices, swap(): return lax.ppermute(value, 'gy', [(i, i ^ partner) for i in range(ny)])  48.4 us
    ppermute x8, waiting for transfers between devices, swap(): return lax.ppermute(value, 'gx', [(i, i ^ partner) for i in range(nx)])  23.5 us
    ppermute x27, starting transfers between devices, swap(): return lax.ppermute(value, 'gy', [(i, i ^ partner) for i in range(ny)])  20.3 us
    ppermute x8, starting transfers between devices, swap(): return lax.ppermute(value, 'gx', [(i, i ^ partner) for i in range(nx)])  20 us
    pallas_call x1, Pallas kernels, on_device(): pl.pallas_call(functools.partial(first_kernel, nx, ny, early_pairs, owned...  13.4 us
    pallas_call x1, Pallas kernels, on_device(): pl.pallas_call(functools.partial(last_kernel, math.sqrt(genes), len(grams...  7.35 us
    unnamed x44, local copies, waits for them, and re-layouts  7.09 us
    pallas_call x1, Pallas kernels, cell_inverse(): pl.pallas_call(functools.partial(factor_kernel, math.sqrt(cells_all)), gr...  5.78 us
  transfers between devices with their start and end apart: 35, of which 21 were waited for; matrix products, arithmetic and copies ran while one was open for 0% of the time, Pallas kernels for 8%

profile of v6, /device:TPU:0, one launch (start us, length us, event | category | flops | bytes accessed | tf_op | source)
XLA Modules:
  0.0 155.3 jit_solution(14125322146860872233)
XLA Ops:
  1.3 13.4 %tile_products.1 = (f32[16,128,128]{2,1,0:T(8,128)}, f32[16,128,128]{2,1,0:T(8,128)}, f32[16,128,128]{2,1,0:T(8,128)}, f32[16,128,128]{2,1,0:T(8,128)}, f32[16,1...) custom-call(s32[192]{0:T(256)} %rows.3, s32[192]{0:T(256)} %cols.3, ...), custom_call_target="tpu_custom_call" | custom-call | flops 4000000000 | bytes 12000000 | tf_op jit(solution)/shard_map/tile_products/pallas_call | solution.py:365
  14.6 1.5 collective-permute-start.4
  16.2 0.4 collective-permute-start.3
  16.8 0.4 collective-permute-start.10
  17.2 1.5 collective-permute-done.4.refs_1_
  18.7 0.4 collective-permute-start
  19.0 1.1 collective-permute-done.5.refs_1_
  20.2 1.2 copy-done.5
  21.4 0.1 combine.44
  21.6 2.4 %collective-permute-start.8 = (f32[16,128,128]{2,1,0:T(8,128)S(1)}, f32[16,128,128]{2,1,0:T(8,128)S(1)}, u32[]{:S(2)}, u32[]{:S(2)}) collective-permute-start(f32[16,128,128]{2,1,0:T(8,128)S(1)} %combine.44), channel_id=1, source_target_pairs={{0,2},{1,3},{2,0},{3,1},{4,6},{5,7},{6,4},{7,5},{8,10},{9,11},{10,... | collective-permute-start | bytes 3145736 | tf_op jit(solution)/shard_map/ppermute | solution.py:361
  24.0 1.2 copy-done.4
  25.2 0.1 combine.41
  25.3 2.3 %collective-permute-start.9 = (f32[16,128,128]{2,1,0:T(8,128)S(1)}, f32[16,128,128]{2,1,0:T(8,128)S(1)}, u32[]{:S(2)}, u32[]{:S(2)}) collective-permute-start(f32[16,128,128]{2,1,0:T(8,128)S(1)} %combine.41), channel_id=1, source_target_pairs={{0,4},{1,5},{2,6},{3,7},{4,0},{5,1},{6,2},{7,3},{8,12},{9,13},{10,... | collective-permute-start | bytes 3145736 | tf_op jit(solution)/shard_map/ppermute | solution.py:361
  27.7 0.1 combine.42.refs_4_
  27.8 3.7 %collective-permute-start.6 = (f32[17,128,128]{2,1,0:T(8,128)S(1)}, f32[17,128,128]{2,1,0:T(8,128)S(1)}, u32[]{:S(2)}, u32[]{:S(2)}) collective-permute-start(f32[17,128,128]{2,1,0:T(8,128)S(1)} %combine.42.refs_4_), channel_id=1, source_target_pairs={{0,8},{8,0},{16,24},{24,16},{1,9},{9,1},{17,25},{25,17},{2,10},{10... | collective-permute-start | bytes 3342344 | tf_op jit(solution)/shard_map/ppermute | solution.py:363
  31.6 0.3 collective-permute-start.1
  31.9 2.8 %copy-done.14 = bf16[192,128,128]{2,1,0:T(8,128)(2,1)S(1)} copy-done((bf16[192,128,128]{2,1,0:T(8,128)(2,1)S(1)}, bf16[192,128,128]{2,1,0:T(8,128)(2,1)}, u32[]{:S(2)}) %copy-start.14) | copy-done | bytes 6291480
  34.7 3.7 %late_products.1 = (f32[8,128,128]{2,1,0:T(8,128)S(1)}, f32[8,128,128]{2,1,0:T(8,128)S(1)}, f32[8,128,128]{2,1,0:T(8,128)S(1)}, f32[8,128,128]{2,1,0:T(8,128)S(1...) custom-call(s32[192]{0:T(256)S(1)} %copy-done.17, ...), custom_call_target="tpu_custom_call" | custom-call | flops 4000000000 | bytes 12000000 | tf_op jit(solution)/shard_map/late_products/pallas_call | solution.py:515
  38.4 9.3 %collective-permute-done.8.refs_1_ = f32[16,128,128]{2,1,0:T(8,128)S(1)} collective-permute-done((f32[16,128,128]{2,1,0:T(8,128)S(1)}, f32[16,128,128]{2,1,0:T(8,128)S(1)}, u32[]{:S(2)}, u32[]{:S(2)}) %collective-permute-start.8) | collective-permute-done | bytes 1048608 | tf_op jit(solution)/shard_map/ppermute | solution.py:361
  47.7 3.4 %collective-permute-done.9.refs_1_ = f32[16,128,128]{2,1,0:T(8,128)S(1)} collective-permute-done((f32[16,128,128]{2,1,0:T(8,128)S(1)}, f32[16,128,128]{2,1,0:T(8,128)S(1)}, u32[]{:S(2)}, u32[]{:S(2)}) %collective-permute-start.9) | collective-permute-done | bytes 1048608 | tf_op jit(solution)/shard_map/ppermute | solution.py:361
  51.1 0.1 combine.47.refs_0_
  51.3 1.8 %collective-permute-start.11 = (f32[8,128,128]{2,1,0:T(8,128)S(1)}, f32[8,128,128]{2,1,0:T(8,128)S(1)}, u32[]{:S(2)}, u32[]{:S(2)}) collective-permute-start(f32[8,128,128]{2,1,0:T(8,128)S(1)} %combine.48), channel_id=1, source_target_pairs={{0,4},{1,5},{2,6},{3,7},{4,0},{5,1},{6,2},{7,3},{8,12},{9,13},{10,... | collective-permute-start | bytes 1572872 | tf_op jit(solution)/shard_map/ppermute | solution.py:361
  53.3 0.5 collective-permute-start.12
  53.8 0.1 combine.40.refs_0_.refs_2_
  53.9 2.9 %collective-permute-done.6.refs_1_.refs_3_.refs_5_ = f32[17,128,128]{2,1,0:T(8,128)S(1)} collective-permute-done((f32[17,128,128]{2,1,0:T(8,128)S(1)}, f32[17,128,128]{2,1,0:T(8,128)S(1)}, u32[]{:S(2)}, u32[]{:S(2)}) %collective-permute-start.6) | collective-permute-done | bytes 1114144 | tf_op jit(solution)/shard_map/ppermute | solution.py:363
  56.9 5.5 %collective-permute-start.13 = (f32[9,128,128]{2,1,0:T(8,128)S(1)}, f32[9,128,128]{2,1,0:T(8,128)S(1)}, u32[]{:S(2)}, u32[]{:S(2)}) collective-permute-start(f32[9,128,128]{2,1,0:T(8,128)S(1)} %combine.49.refs_2_), channel_id=1, source_target_pairs={{0,16},{8,24},{16,0},{24,8},{1,17},{9,25},{17,1},{25,9},{2,18},{10... | collective-permute-start | bytes 1769480 | tf_op jit(solution)/shard_map/ppermute | solution.py:363
  62.4 1.1 collective-permute-start.17
  63.6 0.6 collective-permute-start.16
  64.2 1.9 %collective-permute-done.11.refs_1_ = f32[8,128,128]{2,1,0:T(8,128)S(1)} collective-permute-done((f32[8,128,128]{2,1,0:T(8,128)S(1)}, f32[8,128,128]{2,1,0:T(8,128)S(1)}, u32[]{:S(2)}, u32[]{:S(2)}) %collective-permute-start.11) | collective-permute-done | bytes 524320 | tf_op jit(solution)/shard_map/ppermute | solution.py:361
  66.1 2.0 %collective-permute-done.12.refs_3_ = f32[8,128,128]{2,1,0:T(8,128)S(1)} collective-permute-done((f32[8,128,128]{2,1,0:T(8,128)S(1)}, f32[8,128,128]{2,1,0:T(8,128)S(1)}, u32[]{:S(2)}, u32[]{:S(2)}) %collective-permute-start.12) | collective-permute-done | bytes 524320 | tf_op jit(solution)/shard_map/ppermute | solution.py:361
  68.2 8.7 %collective-permute-done.17.refs_1_ = f32[8,128,128]{2,1,0:T(8,128)S(1)} collective-permute-done((f32[8,128,128]{2,1,0:T(8,128)S(1)}, f32[8,128,128]{2,1,0:T(8,128)S(1)}, u32[]{:S(2)}, u32[]{:S(2)}) %collective-permute-start.17) | collective-permute-done | bytes 524320 | tf_op jit(solution)/shard_map/ppermute | solution.py:361
  76.9 1.7 %collective-permute-done.16.refs_1_ = f32[8,128,128]{2,1,0:T(8,128)S(1)} collective-permute-done((f32[8,128,128]{2,1,0:T(8,128)S(1)}, f32[8,128,128]{2,1,0:T(8,128)S(1)}, u32[]{:S(2)}, u32[]{:S(2)}) %collective-permute-start.16) | collective-permute-done | bytes 524320 | tf_op jit(solution)/shard_map/ppermute | solution.py:361
  78.6 9.7 %collective-permute-done.13.refs_1_.refs_3_ = f32[9,128,128]{2,1,0:T(8,128)S(1)} collective-permute-done((f32[9,128,128]{2,1,0:T(8,128)S(1)}, f32[9,128,128]{2,1,0:T(8,128)S(1)}, u32[]{:S(2)}, u32[]{:S(2)}) %collective-permute-start.13) | collective-permute-done | bytes 589856 | tf_op jit(solution)/shard_map/ppermute | solution.py:363
  88.4 0.8 collective-permute-start.18
  89.3 1.1 collective-permute-start.22
  90.6 0.6 collective-permute-start.24
  91.3 1.5 collective-permute-start.19
  92.8 1.0 collective-permute-start.20
  93.9 7.2 %collective-permute-done.19.refs_1_ = f32[2,128,128]{2,1,0:T(8,128)S(1)} collective-permute-done((f32[2,128,128]{2,1,0:T(8,128)S(1)}, f32[2,128,128]{2,1,0:T(8,128)S(1)}, u32[]{:S(2)}, u32[]{:S(2)}) %collective-permute-start.19) | collective-permute-done | bytes 131104 | tf_op jit(solution)/shard_map/ppermute | solution.py:361
  101.1 0.4 collective-permute-done.20.refs_1_
  101.5 0.1 collective-permute-done.18.refs_1_.refs_3_
  101.7 3.3 %collective-permute-start.25 = (f32[4,128,128]{2,1,0:T(8,128)S(1)}, f32[4,128,128]{2,1,0:T(8,128)S(1)}, u32[]{:S(2)}, u32[]{:S(2)}) collective-permute-start(f32[4,128,128]{2,1,0:T(8,128)S(1)} %combine.67), channel_id=1, source_target_pairs={{0,16},{8,24},{16,0},{24,8},{1,17},{9,25},{17,1},{25,9},{2,18},{10... | collective-permute-start | bytes 786440 | tf_op jit(solution)/shard_map/ppermute | solution.py:363
  105.1 1.6 %collective-permute-start.28 = (f32[4,128,128]{2,1,0:T(8,128)S(1)}, f32[4,128,128]{2,1,0:T(8,128)S(1)}, u32[]{:S(2)}, u32[]{:S(2)}) collective-permute-start(f32[4,128,128]{2,1,0:T(8,128)S(1)} %combine.70), channel_id=1, source_target_pairs={{0,8},{8,0},{16,24},{24,16},{1,9},{9,1},{17,25},{25,17},{2,10},{10... | collective-permute-start | bytes 786440 | tf_op jit(solution)/shard_map/ppermute | solution.py:363
  106.7 1.1 collective-permute-start.27
  107.8 0.7 collective-permute-start.26
  108.6 3.5 %collective-permute-done.26.refs_5_ = f32[1,128,128]{2,1,0:T(8,128)S(1)} collective-permute-done((f32[1,128,128]{2,1,0:T(8,128)S(1)}, f32[1,128,128]{2,1,0:T(8,128)S(1)}, u32[]{:S(2)}, u32[]{:S(2)}) %collective-permute-start.26) | collective-permute-done | bytes 65568 | tf_op jit(solution)/shard_map/ppermute | solution.py:361
  112.1 4.3 %collective-permute-done.25.refs_1_.refs_3_ = f32[4,128,128]{2,1,0:T(8,128)S(1)} collective-permute-done((f32[4,128,128]{2,1,0:T(8,128)S(1)}, f32[4,128,128]{2,1,0:T(8,128)S(1)}, u32[]{:S(2)}, u32[]{:S(2)}) %collective-permute-start.25) | collective-permute-done | bytes 262176 | tf_op jit(solution)/shard_map/ppermute | solution.py:363
  116.5 0.5 collective-permute-done.28.refs_1_.refs_3_
  117.0 0.9 collective-permute-start.29
  117.9 5.8 %cell_cholesky.1.inverse = f32[128,128]{1,0:T(8,128)} custom-call(f32[2,128,128]{2,1,0:T(8,128)} %copy-done.11, f32[2,128,128]{2,1,0:T(8,128)} %copy-done.15), custom_call_target="tpu_custom_call" | custom-call | flops 1500000000 | bytes 4500000 | tf_op jit(solution)/shard_map/cell_cholesky/pallas_call | solution.py:537
  123.7 0.8 copy-done.12
  124.6 0.9 copy-done.16
  125.5 1.5 owned_gram.2
  126.9 0.7 owned_gram.3
  127.7 1.2 collective-permute-done.30.refs_1_
  129.0 1.1 collective-permute-start.31
  130.0 3.3 %collective-permute-done.31.refs_1_ = f32[1,128,128]{2,1,0:T(8,128)S(1)} collective-permute-done((f32[1,128,128]{2,1,0:T(8,128)S(1)}, f32[1,128,128]{2,1,0:T(8,128)S(1)}, u32[]{:S(2)}, u32[]{:S(2)}) %collective-permute-start.31) | collective-permute-done | bytes 65568 | tf_op jit(solution)/shard_map/ppermute | solution.py:361
  133.3 1.1 collective-permute-start.32
  134.5 3.2 %collective-permute-done.32.refs_1_ = f32[1,128,128]{2,1,0:T(8,128)S(1)} collective-permute-done((f32[1,128,128]{2,1,0:T(8,128)S(1)}, f32[1,128,128]{2,1,0:T(8,128)S(1)}, u32[]{:S(2)}, u32[]{:S(2)}) %collective-permute-start.32) | collective-permute-done | bytes 65568 | tf_op jit(solution)/shard_map/ppermute | solution.py:361
  137.7 2.7 %collective-permute-start.33 = (f32[1,128,128]{2,1,0:T(8,128)S(1)}, f32[1,128,128]{2,1,0:T(8,128)S(1)}, u32[]{:S(2)}, u32[]{:S(2)}) collective-permute-start(f32[1,128,128]{2,1,0:T(8,128)S(1)} %combine.78.refs_0_), channel_id=1, source_target_pairs={{0,8},{8,0},{16,24},{24,16},{1,9},{9,1},{17,25},{25,17},{2,10},{10... | collective-permute-start | bytes 196616 | tf_op jit(solution)/shard_map/ppermute | solution.py:363
  140.3 2.2 %collective-permute-done.33.refs_1_ = f32[1,128,128]{2,1,0:T(8,128)S(1)} collective-permute-done((f32[1,128,128]{2,1,0:T(8,128)S(1)}, f32[1,128,128]{2,1,0:T(8,128)S(1)}, u32[]{:S(2)}, u32[]{:S(2)}) %collective-permute-start.33) | collective-permute-done | bytes 65568 | tf_op jit(solution)/shard_map/ppermute | solution.py:363
  142.6 1.5 collective-permute-start.34
  144.1 3.7 %collective-permute-done.34.refs_1_ = f32[1,128,128]{2,1,0:T(8,128)S(1)} collective-permute-done((f32[1,128,128]{2,1,0:T(8,128)S(1)}, f32[1,128,128]{2,1,0:T(8,128)S(1)}, u32[]{:S(2)}, u32[]{:S(2)}) %collective-permute-start.34) | collective-permute-done | bytes 65568 | tf_op jit(solution)/shard_map/ppermute | solution.py:363
  147.8 7.4 %factors.1 = (f32[1024,128]{1,0:T(8,128)}, bf16[8192,128]{1,0:T(8,128)(2,1)}) custom-call(bf16[64,128,256]{2,1,0:T(8,128)(2,1)S(1)} %copy-done.1, f32[128,128]{1,0:T(8,128)S(1)} %copy-done.13, f32[1,128,128]{2,1,0:T(8,128)S(1)} %combine.79.refs_0_, f32[1,128,128]{2,1,0:T(8,128)S(1)} %collective-permute-done.34.refs_1_, ...), custom_call_target="tpu_custom_call" | custom-call | tf_op jit(solution)/shard_map/factors/pallas_call | solution.py:596
  (96 shorter events, 1.6 us)
Async XLA Ops:
  14.6 4.0 %collective-permute-start.4 = (f32[16,128,128]{2,1,0:T(8,128)}, f32[16,128,128]{2,1,0:T(8,128)S(1)}, u32[]{:S(2)}, u32[]{:S(2)}) collective-permute-start(f32[16,128,128]{2,1,0:T(8,128)} %get-tuple-element.68), channel_id=1, source_target_pairs={{0,1},{1,0},{2,3},{3,2},{4,5},{5,4},{6,7},{7,6},{8,9},{9,8},{10,11... | collective-permute-start | bytes 3145736 | tf_op jit(solution)/shard_map/ppermute | solution.py:361
  16.2 4.0 %collective-permute-start.5 = (f32[16,128,128]{2,1,0:T(8,128)}, f32[16,128,128]{2,1,0:T(8,128)S(1)}, u32[]{:S(2)}, u32[]{:S(2)}) collective-permute-start(f32[16,128,128]{2,1,0:T(8,128)} %get-tuple-element.69), channel_id=1, source_target_pairs={{0,1},{1,0},{2,3},{3,2},{4,5},{5,4},{6,7},{7,6},{8,9},{9,8},{10,11... | collective-permute-start | bytes 3145736 | tf_op jit(solution)/shard_map/ppermute | solution.py:361
  16.2 9.1 %collective-permute-start.3 = (f32[8,128,128]{2,1,0:T(8,128)}, f32[8,128,128]{2,1,0:T(8,128)S(1)}, u32[]{:S(2)}, u32[]{:S(2)}) collective-permute-start(f32[8,128,128]{2,1,0:T(8,128)} %get-tuple-element.66), channel_id=1, source_target_pairs={{0,1},{1,0},{2,3},{3,2},{4,5},{5,4},{6,7},{7,6},{8,9},{9,8},{10,11... | collective-permute-start | bytes 1572872 | tf_op jit(solution)/shard_map/ppermute | solution.py:361
  16.7 11.0 %collective-permute-start.2 = (f32[9,128,128]{2,1,0:T(8,128)}, f32[9,128,128]{2,1,0:T(8,128)S(1)}, u32[]{:S(2)}, u32[]{:S(2)}) collective-permute-start(f32[9,128,128]{2,1,0:T(8,128)} %get-tuple-element.65.refs_4_), channel_id=1, source_target_pairs={{0,1},{1,0},{2,3},{3,2},{4,5},{5,4},{6,7},{7,6},{8,9},{9,8},{10,11... | collective-permute-start | bytes 1769480 | tf_op jit(solution)/shard_map/ppermute | solution.py:361
  16.8 14.8 %collective-permute-start.10 = (f32[16,128,128]{2,1,0:T(8,128)}, f32[16,128,128]{2,1,0:T(8,128)S(1)}, u32[]{:S(2)}, u32[]{:S(2)}) collective-permute-start(f32[16,128,128]{2,1,0:T(8,128)} %get-tuple-element.83), channel_id=1, source_target_pairs={{0,1},{1,0},{2,3},{3,2},{4,5},{5,4},{6,7},{7,6},{8,9},{9,8},{10,11... | collective-permute-start | bytes 3145736 | tf_op jit(solution)/shard_map/ppermute | solution.py:361
  18.7 9.2 %collective-permute-start = (f32[8,128,128]{2,1,0:T(8,128)}, f32[8,128,128]{2,1,0:T(8,128)S(1)}, u32[]{:S(2)}, u32[]{:S(2)}) collective-permute-start(f32[8,128,128]{2,1,0:T(8,128)} %get-tuple-element.61), channel_id=1, source_target_pairs={{0,1},{1,0},{2,3},{3,2},{4,5},{5,4},{6,7},{7,6},{8,9},{9,8},{10,11... | collective-permute-start | bytes 1572872 | tf_op jit(solution)/shard_map/ppermute | solution.py:361
  20.2 1.2 copy-start.5
  21.4 6.3 %copy-start.20 = (f32[16,128,128]{2,1,0:T(8,128)S(1)}, f32[16,128,128]{2,1,0:T(8,128)}, u32[]{:S(2)}) copy-start(f32[16,128,128]{2,1,0:T(8,128)} %get-tuple-element.75) | copy-start | bytes 3145732
  21.4 6.3 %copy-start.6 = (f32[9,128,128]{2,1,0:T(8,128)S(1)}, f32[9,128,128]{2,1,0:T(8,128)}, u32[]{:S(2)}) copy-start(f32[9,128,128]{2,1,0:T(8,128)} %get-tuple-element.65.refs_4_) | copy-start | bytes 1769476
  21.4 6.3 %copy-start.7 = (f32[8,128,128]{2,1,0:T(8,128)S(1)}, f32[8,128,128]{2,1,0:T(8,128)}, u32[]{:S(2)}) copy-start(f32[8,128,128]{2,1,0:T(8,128)} %get-tuple-element.64.refs_0_) | copy-start | bytes 1572868
  21.4 6.3 %copy-start.8 = (f32[8,128,128]{2,1,0:T(8,128)S(1)}, f32[8,128,128]{2,1,0:T(8,128)}, u32[]{:S(2)}) copy-start(f32[8,128,128]{2,1,0:T(8,128)} %get-tuple-element.72.refs_2_) | copy-start | bytes 1572868
  21.4 10.5 %copy-start.17 = (s32[192]{0:T(256)S(1)}, s32[192]{0:T(256)}, u32[]{:S(2)}) copy-start(s32[192]{0:T(256)} %rows.3) | copy-start | bytes 2308
  21.4 10.4 %copy-start.18 = (s32[192]{0:T(256)S(1)}, s32[192]{0:T(256)}, u32[]{:S(2)}) copy-start(s32[192]{0:T(256)} %cols.3) | copy-start | bytes 2308
  21.4 10.4 %copy-start.19 = (s32[256]{0:T(256)S(1)}, s32[256]{0:T(256)}, u32[]{:S(2)}) copy-start(s32[256]{0:T(256)} %order.3) | copy-start | bytes 3076
  21.6 10.3 %copy-start = (bf16[64,128,256]{2,1,0:T(8,128)(2,1)S(1)}, bf16[64,128,256]{2,1,0:T(8,128)(2,1)}, u32[]{:S(2)}) copy-start(bf16[64,128,256]{2,1,0:T(8,128)(2,1)} %get-tuple-element.78.split) | copy-start | bytes 12582916
  21.6 26.1 %collective-permute-start.8 = (f32[16,128,128]{2,1,0:T(8,128)S(1)}, f32[16,128,128]{2,1,0:T(8,128)S(1)}, u32[]{:S(2)}, u32[]{:S(2)}) collective-permute-start(f32[16,128,128]{2,1,0:T(8,128)S(1)} %combine.44), channel_id=1, source_target_pairs={{0,2},{1,3},{2,0},{3,1},{4,6},{5,7},{6,4},{7,5},{8,10},{9,11},{10,... | collective-permute-start | bytes 3145736 | tf_op jit(solution)/shard_map/ppermute | solution.py:361
  24.0 1.2 copy-start.4
  25.2 6.4 %copy-start.21 = (f32[8,128,128]{2,1,0:T(8,128)S(1)}, f32[8,128,128]{2,1,0:T(8,128)}, u32[]{:S(2)}) copy-start(f32[8,128,128]{2,1,0:T(8,128)} %get-tuple-element.63) | copy-start | bytes 1572868
  25.3 25.7 %collective-permute-start.9 = (f32[16,128,128]{2,1,0:T(8,128)S(1)}, f32[16,128,128]{2,1,0:T(8,128)S(1)}, u32[]{:S(2)}, u32[]{:S(2)}) collective-permute-start(f32[16,128,128]{2,1,0:T(8,128)S(1)} %combine.41), channel_id=1, source_target_pairs={{0,4},{1,5},{2,6},{3,7},{4,0},{5,1},{6,2},{7,3},{8,12},{9,13},{10,... | collective-permute-start | bytes 3145736 | tf_op jit(solution)/shard_map/ppermute | solution.py:361
  27.7 23.6 %collective-permute-start.7 = (f32[16,128,128]{2,1,0:T(8,128)S(1)}, f32[16,128,128]{2,1,0:T(8,128)S(1)}, u32[]{:S(2)}, u32[]{:S(2)}) collective-permute-start(f32[16,128,128]{2,1,0:T(8,128)S(1)} %copy-done.20), channel_id=1, source_target_pairs={{0,1},{1,0},{2,3},{3,2},{4,5},{5,4},{6,7},{7,6},{8,9},{9,8},{10,11... | collective-permute-start | bytes 3145736 | tf_op jit(solution)/shard_map/ppermute | solution.py:361
  27.8 28.9 %collective-permute-start.6 = (f32[17,128,128]{2,1,0:T(8,128)S(1)}, f32[17,128,128]{2,1,0:T(8,128)S(1)}, u32[]{:S(2)}, u32[]{:S(2)}) collective-permute-start(f32[17,128,128]{2,1,0:T(8,128)S(1)} %combine.42.refs_4_), channel_id=1, source_target_pairs={{0,8},{8,0},{16,24},{24,16},{1,9},{9,1},{17,25},{25,17},{2,10},{10... | collective-permute-start | bytes 3342344 | tf_op jit(solution)/shard_map/ppermute | solution.py:363
  31.6 19.5 %copy-start.3 = (f32[16,128,128]{2,1,0:T(8,128)S(1)}, f32[16,128,128]{2,1,0:T(8,128)}, u32[]{:S(2)}) copy-start(f32[16,128,128]{2,1,0:T(8,128)} %get-tuple-element.82.refs_0_) | copy-start | bytes 3145732
  31.6 21.7 %collective-permute-start.1 = (f32[8,128,128]{2,1,0:T(8,128)S(1)}, f32[8,128,128]{2,1,0:T(8,128)S(1)}, u32[]{:S(2)}, u32[]{:S(2)}) collective-permute-start(f32[8,128,128]{2,1,0:T(8,128)S(1)} %copy-done.21), channel_id=1, source_target_pairs={{0,1},{1,0},{2,3},{3,2},{4,5},{5,4},{6,7},{7,6},{8,9},{9,8},{10,11... | collective-permute-start | bytes 1572872 | tf_op jit(solution)/shard_map/ppermute | solution.py:361
  31.9 2.8 %copy-start.14 = (bf16[192,128,128]{2,1,0:T(8,128)(2,1)S(1)}, bf16[192,128,128]{2,1,0:T(8,128)(2,1)}, u32[]{:S(2)}) copy-start(bf16[192,128,128]{2,1,0:T(8,128)(2,1)} %tiles.3) | copy-start | bytes 18874372
  38.4 14.7 %copy-start.2 = (f32[16,128,128]{2,1,0:T(8,128)S(1)}, f32[16,128,128]{2,1,0:T(8,128)}, u32[]{:S(2)}) copy-start(f32[16,128,128]{2,1,0:T(8,128)} %get-tuple-element.74.refs_0_) | copy-start | bytes 3145732
  47.7 14.6 %collective-permute-start.14 = (f32[8,128,128]{2,1,0:T(8,128)S(1)}, f32[8,128,128]{2,1,0:T(8,128)S(1)}, u32[]{:S(2)}, u32[]{:S(2)}) collective-permute-start(f32[8,128,128]{2,1,0:T(8,128)S(1)} %get-tuple-element.86), channel_id=1, source_target_pairs={{0,1},{1,0},{2,3},{3,2},{4,5},{5,4},{6,7},{7,6},{8,9},{9,8},{10,11... | collective-permute-start | bytes 1572872 | tf_op jit(solution)/shard_map/ppermute | solution.py:361
  51.1 11.2 %collective-permute-start.15 = (f32[8,128,128]{2,1,0:T(8,128)S(1)}, f32[8,128,128]{2,1,0:T(8,128)S(1)}, u32[]{:S(2)}, u32[]{:S(2)}) collective-permute-start(f32[8,128,128]{2,1,0:T(8,128)S(1)} %get-tuple-element.87), channel_id=1, source_target_pairs={{0,1},{1,0},{2,3},{3,2},{4,5},{5,4},{6,7},{7,6},{8,9},{9,8},{10,11... | collective-permute-start | bytes 1572872 | tf_op jit(solution)/shard_map/ppermute | solution.py:361
  51.2 2.6 %copy-start.9 = (f32[8,128,128]{2,1,0:T(8,128)S(1)}, f32[8,128,128]{2,1,0:T(8,128)}, u32[]{:S(2)}) copy-start(f32[8,128,128]{2,1,0:T(8,128)} %get-tuple-element.60.refs_0_) | copy-start | bytes 1572868
  51.2 2.6 %copy-start.10 = (f32[8,128,128]{2,1,0:T(8,128)S(1)}, f32[8,128,128]{2,1,0:T(8,128)}, u32[]{:S(2)}) copy-start(f32[8,128,128]{2,1,0:T(8,128)} %get-tuple-element.62.refs_2_) | copy-start | bytes 1572868
  51.3 14.8 %collective-permute-start.11 = (f32[8,128,128]{2,1,0:T(8,128)S(1)}, f32[8,128,128]{2,1,0:T(8,128)S(1)}, u32[]{:S(2)}, u32[]{:S(2)}) collective-permute-start(f32[8,128,128]{2,1,0:T(8,128)S(1)} %combine.48), channel_id=1, source_target_pairs={{0,4},{1,5},{2,6},{3,7},{4,0},{5,1},{6,2},{7,3},{8,12},{9,13},{10,... | collective-permute-start | bytes 1572872 | tf_op jit(solution)/shard_map/ppermute | solution.py:361
  53.3 14.8 %collective-permute-start.12 = (f32[8,128,128]{2,1,0:T(8,128)S(1)}, f32[8,128,128]{2,1,0:T(8,128)S(1)}, u32[]{:S(2)}, u32[]{:S(2)}) collective-permute-start(f32[8,128,128]{2,1,0:T(8,128)S(1)} %combine.45), channel_id=1, source_target_pairs={{0,2},{1,3},{2,0},{3,1},{4,6},{5,7},{6,4},{7,5},{8,10},{9,11},{10,... | collective-permute-start | bytes 1572872 | tf_op jit(solution)/shard_map/ppermute | solution.py:361
  56.9 31.5 %collective-permute-start.13 = (f32[9,128,128]{2,1,0:T(8,128)S(1)}, f32[9,128,128]{2,1,0:T(8,128)S(1)}, u32[]{:S(2)}, u32[]{:S(2)}) collective-permute-start(f32[9,128,128]{2,1,0:T(8,128)S(1)} %combine.49.refs_2_), channel_id=1, source_target_pairs={{0,16},{8,24},{16,0},{24,8},{1,17},{9,25},{17,1},{25,9},{2,18},{10... | collective-permute-start | bytes 1769480 | tf_op jit(solution)/shard_map/ppermute | solution.py:363
  62.4 14.5 %collective-permute-start.17 = (f32[8,128,128]{2,1,0:T(8,128)S(1)}, f32[8,128,128]{2,1,0:T(8,128)S(1)}, u32[]{:S(2)}, u32[]{:S(2)}) collective-permute-start(f32[8,128,128]{2,1,0:T(8,128)S(1)} %combine.51), channel_id=1, source_target_pairs={{0,4},{1,5},{2,6},{3,7},{4,0},{5,1},{6,2},{7,3},{8,12},{9,13},{10,... | collective-permute-start | bytes 1572872 | tf_op jit(solution)/shard_map/ppermute | solution.py:361
  63.6 15.0 %collective-permute-start.16 = (f32[8,128,128]{2,1,0:T(8,128)S(1)}, f32[8,128,128]{2,1,0:T(8,128)S(1)}, u32[]{:S(2)}, u32[]{:S(2)}) collective-permute-start(f32[8,128,128]{2,1,0:T(8,128)S(1)} %combine.50), channel_id=1, source_target_pairs={{0,2},{1,3},{2,0},{3,1},{4,6},{5,7},{6,4},{7,5},{8,10},{9,11},{10,... | collective-permute-start | bytes 1572872 | tf_op jit(solution)/shard_map/ppermute | solution.py:361
  66.1 23.1 %collective-permute-start.21 = (f32[8,128,128]{2,1,0:T(8,128)S(1)}, f32[8,128,128]{2,1,0:T(8,128)S(1)}, u32[]{:S(2)}, u32[]{:S(2)}) collective-permute-start(f32[8,128,128]{2,1,0:T(8,128)S(1)} %get-tuple-element.94), channel_id=1, source_target_pairs={{0,1},{1,0},{2,3},{3,2},{4,5},{5,4},{6,7},{7,6},{8,9},{9,8},{10,11... | collective-permute-start | bytes 1572872 | tf_op jit(solution)/shard_map/ppermute | solution.py:361
  68.1 22.3 %collective-permute-start.23 = (f32[8,128,128]{2,1,0:T(8,128)S(1)}, f32[8,128,128]{2,1,0:T(8,128)S(1)}, u32[]{:S(2)}, u32[]{:S(2)}) collective-permute-start(f32[8,128,128]{2,1,0:T(8,128)S(1)} %get-tuple-element.97), channel_id=1, source_target_pairs={{0,1},{1,0},{2,3},{3,2},{4,5},{5,4},{6,7},{7,6},{8,9},{9,8},{10,11... | collective-permute-start | bytes 1572872 | tf_op jit(solution)/shard_map/ppermute | solution.py:361
  88.4 13.3 %collective-permute-start.18 = (f32[8,128,128]{2,1,0:T(8,128)S(1)}, f32[8,128,128]{2,1,0:T(8,128)S(1)}, u32[]{:S(2)}, u32[]{:S(2)}) collective-permute-start(f32[8,128,128]{2,1,0:T(8,128)S(1)} %combine.55), channel_id=1, source_target_pairs={{0,8},{8,0},{16,24},{24,16},{1,9},{9,1},{17,25},{25,17},{2,10},{10... | collective-permute-start | bytes 1572872 | tf_op jit(solution)/shard_map/ppermute | solution.py:363
  89.3 12.2 %collective-permute-start.22 = (f32[5,128,128]{2,1,0:T(8,128)S(1)}, f32[5,128,128]{2,1,0:T(8,128)S(1)}, u32[]{:S(2)}, u32[]{:S(2)}) collective-permute-start(f32[5,128,128]{2,1,0:T(8,128)S(1)} %combine.59.refs_2_), channel_id=1, source_target_pairs={{0,4},{1,5},{2,6},{3,7},{4,0},{5,1},{6,2},{7,3},{8,12},{9,13},{10,... | collective-permute-start | bytes 983048 | tf_op jit(solution)/shard_map/ppermute | solution.py:361
  90.6 11.0 %collective-permute-start.24 = (f32[4,128,128]{2,1,0:T(8,128)S(1)}, f32[4,128,128]{2,1,0:T(8,128)S(1)}, u32[]{:S(2)}, u32[]{:S(2)}) collective-permute-start(f32[4,128,128]{2,1,0:T(8,128)S(1)} %combine.61), channel_id=1, source_target_pairs={{0,2},{1,3},{2,0},{3,1},{4,6},{5,7},{6,4},{7,5},{8,10},{9,11},{10,... | collective-permute-start | bytes 786440 | tf_op jit(solution)/shard_map/ppermute | solution.py:361
  91.3 9.8 %collective-permute-start.19 = (f32[2,128,128]{2,1,0:T(8,128)S(1)}, f32[2,128,128]{2,1,0:T(8,128)S(1)}, u32[]{:S(2)}, u32[]{:S(2)}) collective-permute-start(f32[2,128,128]{2,1,0:T(8,128)S(1)} %combine.56), channel_id=1, source_target_pairs={{0,2},{1,3},{2,0},{3,1},{4,6},{5,7},{6,4},{7,5},{8,10},{9,11},{10,... | collective-permute-start | bytes 393224 | tf_op jit(solution)/shard_map/ppermute | solution.py:361
  92.8 8.7 %collective-permute-start.20 = (f32[2,128,128]{2,1,0:T(8,128)S(1)}, f32[2,128,128]{2,1,0:T(8,128)S(1)}, u32[]{:S(2)}, u32[]{:S(2)}) collective-permute-start(f32[2,128,128]{2,1,0:T(8,128)S(1)} %combine.57), channel_id=1, source_target_pairs={{0,4},{1,5},{2,6},{3,7},{4,0},{5,1},{6,2},{7,3},{8,12},{9,13},{10,... | collective-permute-start | bytes 393224 | tf_op jit(solution)/shard_map/ppermute | solution.py:361
  101.7 14.8 %collective-permute-start.25 = (f32[4,128,128]{2,1,0:T(8,128)S(1)}, f32[4,128,128]{2,1,0:T(8,128)S(1)}, u32[]{:S(2)}, u32[]{:S(2)}) collective-permute-start(f32[4,128,128]{2,1,0:T(8,128)S(1)} %combine.67), channel_id=1, source_target_pairs={{0,16},{8,24},{16,0},{24,8},{1,17},{9,25},{17,1},{25,9},{2,18},{10... | collective-permute-start | bytes 786440 | tf_op jit(solution)/shard_map/ppermute | solution.py:363
  105.1 11.9 %collective-permute-start.28 = (f32[4,128,128]{2,1,0:T(8,128)S(1)}, f32[4,128,128]{2,1,0:T(8,128)S(1)}, u32[]{:S(2)}, u32[]{:S(2)}) collective-permute-start(f32[4,128,128]{2,1,0:T(8,128)S(1)} %combine.70), channel_id=1, source_target_pairs={{0,8},{8,0},{16,24},{24,16},{1,9},{9,1},{17,25},{25,17},{2,10},{10... | collective-permute-start | bytes 786440 | tf_op jit(solution)/shard_map/ppermute | solution.py:363
  106.7 11.3 %copy-start.11 = (f32[2,128,128]{2,1,0:T(8,128)}, f32[2,128,128]{2,1,0:T(8,128)S(1)}, u32[]{:S(2)}) copy-start(f32[2,128,128]{2,1,0:T(8,128)S(1)} %combine.62.refs_0_) | copy-start | bytes 393220
  106.7 5.4 %collective-permute-start.27 = (f32[2,128,128]{2,1,0:T(8,128)S(1)}, f32[2,128,128]{2,1,0:T(8,128)S(1)}, u32[]{:S(2)}, u32[]{:S(2)}) collective-permute-start(f32[2,128,128]{2,1,0:T(8,128)S(1)} %combine.62.refs_0_), channel_id=1, source_target_pairs={{0,2},{1,3},{2,0},{3,1},{4,6},{5,7},{6,4},{7,5},{8,10},{9,11},{10,... | collective-permute-start | bytes 393224 | tf_op jit(solution)/shard_map/ppermute | solution.py:361
  107.8 4.3 %collective-permute-start.26 = (f32[1,128,128]{2,1,0:T(8,128)S(1)}, f32[1,128,128]{2,1,0:T(8,128)S(1)}, u32[]{:S(2)}, u32[]{:S(2)}) collective-permute-start(f32[1,128,128]{2,1,0:T(8,128)S(1)} %combine.69), channel_id=1, source_target_pairs={{0,4},{1,5},{2,6},{3,7},{4,0},{5,1},{6,2},{7,3},{8,12},{9,13},{10,... | collective-permute-start | bytes 196616 | tf_op jit(solution)/shard_map/ppermute | solution.py:361
  112.1 5.8 %copy-start.15 = (f32[2,128,128]{2,1,0:T(8,128)}, f32[2,128,128]{2,1,0:T(8,128)S(1)}, u32[]{:S(2)}) copy-start(f32[2,128,128]{2,1,0:T(8,128)S(1)} %collective-permute-done.27.refs_1_.refs_7_) | copy-start | bytes 393220
  117.0 9.9 %collective-permute-start.29 = (f32[2,128,128]{2,1,0:T(8,128)S(1)}, f32[2,128,128]{2,1,0:T(8,128)S(1)}, u32[]{:S(2)}, u32[]{:S(2)}) collective-permute-start(f32[2,128,128]{2,1,0:T(8,128)S(1)} %combine.71), channel_id=1, source_target_pairs={{0,16},{8,24},{16,0},{24,8},{1,17},{9,25},{17,1},{25,9},{2,18},{10... | collective-permute-start | bytes 393224 | tf_op jit(solution)/shard_map/ppermute | solution.py:363
  123.7 0.8 copy-start.12
  124.6 0.9 copy-start.16
  125.5 22.4 %copy-start.1 = (bf16[64,128,256]{2,1,0:T(8,128)(2,1)S(1)}, bf16[64,128,256]{2,1,0:T(8,128)(2,1)}, u32[]{:S(2)}) copy-start(bf16[64,128,256]{2,1,0:T(8,128)(2,1)} %get-tuple-element.78.split) | copy-start | bytes 12582916
  125.5 22.4 %copy-start.13 = (f32[128,128]{1,0:T(8,128)S(1)}, f32[128,128]{1,0:T(8,128)}, u32[]{:S(2)}) copy-start(f32[128,128]{1,0:T(8,128)} %cell_cholesky.1.inverse) | copy-start | bytes 196612
  127.6 1.3 collective-permute-start.30
  129.0 4.3 %collective-permute-start.31 = (f32[1,128,128]{2,1,0:T(8,128)S(1)}, f32[1,128,128]{2,1,0:T(8,128)S(1)}, u32[]{:S(2)}, u32[]{:S(2)}) collective-permute-start(f32[1,128,128]{2,1,0:T(8,128)S(1)} %combine.76.refs_0_), channel_id=1, source_target_pairs={{0,2},{1,3},{2,0},{3,1},{4,6},{5,7},{6,4},{7,5},{8,10},{9,11},{10,... | collective-permute-start | bytes 196616 | tf_op jit(solution)/shard_map/ppermute | solution.py:361
  133.3 4.3 %collective-permute-start.32 = (f32[1,128,128]{2,1,0:T(8,128)S(1)}, f32[1,128,128]{2,1,0:T(8,128)S(1)}, u32[]{:S(2)}, u32[]{:S(2)}) collective-permute-start(f32[1,128,128]{2,1,0:T(8,128)S(1)} %combine.77.refs_0_), channel_id=1, source_target_pairs={{0,4},{1,5},{2,6},{3,7},{4,0},{5,1},{6,2},{7,3},{8,12},{9,13},{10,... | collective-permute-start | bytes 196616 | tf_op jit(solution)/shard_map/ppermute | solution.py:361
  137.7 4.9 %collective-permute-start.33 = (f32[1,128,128]{2,1,0:T(8,128)S(1)}, f32[1,128,128]{2,1,0:T(8,128)S(1)}, u32[]{:S(2)}, u32[]{:S(2)}) collective-permute-start(f32[1,128,128]{2,1,0:T(8,128)S(1)} %combine.78.refs_0_), channel_id=1, source_target_pairs={{0,8},{8,0},{16,24},{24,16},{1,9},{9,1},{17,25},{25,17},{2,10},{10... | collective-permute-start | bytes 196616 | tf_op jit(solution)/shard_map/ppermute | solution.py:363
  142.6 5.2 %collective-permute-start.34 = (f32[1,128,128]{2,1,0:T(8,128)S(1)}, f32[1,128,128]{2,1,0:T(8,128)S(1)}, u32[]{:S(2)}, u32[]{:S(2)}) collective-permute-start(f32[1,128,128]{2,1,0:T(8,128)S(1)} %combine.79.refs_0_), channel_id=1, source_target_pairs={{0,16},{8,24},{16,0},{24,8},{1,17},{9,25},{17,1},{25,9},{2,18},{10... | collective-permute-start | bytes 196616 | tf_op jit(solution)/shard_map/ppermute | solution.py:363
